TPU v7x, 32 devices: a whole 2x2x4 slice. The times are simulated.
32 devices in a mesh: grp: 4 (over x, core), peak: 8 (over z, y).
Axes of the slice: x: 2, y: 2, z: 4, core: 2. Of those that a mesh axis runs over, the one named last changes fastest.
Arguments:
- counts: bfloat16 [128, 65536], P(None, ('grp', 'peak')), may hold values from 0.099609375 to 4
- tile_mask: int32 [128, 512], P(None, ('grp', 'peak')), may hold values 0 or 1
- neighbours: int32 [128, 15], P(('grp', 'peak')), may hold values from 0 to 127, as said below
- peak_weight: bfloat16 [65536, 512], P(('grp', 'peak')), may hold values from -0.0390625 to 0.0390625
- gain: float32 [512], replicated, may hold values from 0.25 to 1.75
- w_in: bfloat16 [512, 512], replicated, may hold values from -0.25 to 0.25
- w_out: bfloat16 [512, 256], replicated, may hold values from -0.25 to 0.25
Outputs:
- peak_grad: float32 [65536, 512], P(('grp', 'peak'))
- gain_grad: float32 [512], replicated
- in_grad: float32 [512, 512], replicated
- out_grad: float32 [512, 256], replicated
Inputs may be any that keep to these rules, and one draw needn't show every extreme that they name: `neighbours`: every entry is a cell index other than its own row's cell.
All inputs are finite; a program needn't handle non-finite values. No bound on the sum of `tile_mask` on one device may be relied on, other than what follows from the above.
Results may differ from a plain program's by a relative error of at most 0.012.
Values may be sent and summed in bfloat16 or wider, within the bound.
No kernel may reach another device: no remote copies, remote signals or barrier semaphores. Data moves between devices by JAX's collectives and lax.ppermute only.
A program may use at most 64 MiB of HBM per device.

v0:
```python
import jax
import jax.numpy as jnp
from jax import lax
from jax.sharding import PartitionSpec as P

TILE = 128
K = 15


sharpness_divisor = 0.2
eps_norm = 1e-06
gelu_coef = 0.7978845608
cubic_coef = 0.044715


def gelu_tanh(values):
    return (
        0.5
        * values
        * (1.0 + jnp.tanh(gelu_coef * (values + cubic_coef * values * values * values)))
    )


def gelu_slope(values):
    tangent = jnp.tanh(gelu_coef * (values + cubic_coef * values * values * values))
    return 0.5 * (1.0 + tangent) + 0.5 * values * (1.0 - tangent * tangent) * gelu_coef * (
        1.0 + 3.0 * cubic_coef * values * values
    )


def collapsed_lines(left, right):
    return lax.dot_general(
        left, right, (((0,), (0,)), ((), ())), preferred_element_type=jnp.float32
    )


def tower_forward(hidden, gain, w_in, w_out):
    scale = lax.rsqrt(jnp.mean(hidden * hidden, axis=1, keepdims=True) + eps_norm)
    normed = hidden * scale
    rounded = (normed * gain[None, :]).astype(jnp.bfloat16)
    preact = jnp.dot(rounded, w_in, preferred_element_type=jnp.float32)
    activ = gelu_tanh(preact).astype(jnp.bfloat16)
    project = jnp.dot(activ, w_out, preferred_element_type=jnp.float32)
    length = lax.rsqrt(jnp.sum(project * project, axis=1, keepdims=True) + eps_norm)
    unit = project * length
    return ((scale, normed, rounded, preact, activ, length, unit), unit.astype(jnp.bfloat16))


def tower_backward(vector_derivative, gain, w_in, w_out, saved):
    scale, normed, rounded, preact, activ, length, unit = saved
    dproj = (
        length
        * (vector_derivative - unit * jnp.sum(unit * vector_derivative, axis=1, keepdims=True))
    ).astype(jnp.bfloat16)
    out_grad = collapsed_lines(activ, dproj)
    dact = jnp.dot(dproj, w_out.T, preferred_element_type=jnp.float32)
    dpre = (dact * gelu_slope(preact)).astype(jnp.bfloat16)
    in_grad = collapsed_lines(rounded, dpre)
    dround = jnp.dot(dpre, w_in.T, preferred_element_type=jnp.float32)
    gain_grad = jnp.sum(dround * normed, axis=0)
    dnorm = dround * gain[None, :]
    dhidden = scale * (dnorm - normed * jnp.mean(dnorm * normed, axis=1, keepdims=True))
    return (dhidden.astype(jnp.bfloat16), gain_grad, in_grad, out_grad)


def count_lists(lists, column_ids):
    tallies = jnp.zeros((lists.shape[0], column_ids.shape[1]), jnp.float32)
    for slot in range(lists.shape[1]):
        tallies = tallies + (lists[:, slot][:, None] == column_ids).astype(jnp.float32)
    return tallies


def body(counts, tile_mask, neighbours, peak_weight, gain, w_in, w_out):
    total_cells = counts.shape[0]
    own_rows = neighbours.shape[0]
    position = lax.axis_index(("grp", "peak"))
    first_row = position * own_rows
    masked = counts * jnp.repeat(tile_mask.astype(jnp.bfloat16), TILE, axis=1)
    whole_term = jnp.dot(masked, peak_weight, preferred_element_type=jnp.float32)
    hidden = lax.psum_scatter(whole_term, ("grp", "peak"), scatter_dimension=0, tiled=True)
    saved, sample_vectors = tower_forward(hidden, gain, w_in, w_out)
    codes_whole = lax.all_gather(sample_vectors, ("grp", "peak"), axis=0, tiled=True)
    affinity_scores = (
        jnp.einsum("ce,ke->ck", sample_vectors, codes_whole, preferred_element_type=jnp.float32)
        / sharpness_divisor
    )
    row_ids = lax.broadcasted_iota(jnp.int32, (own_rows, total_cells), 0) + first_row
    col_ids = lax.broadcasted_iota(jnp.int32, (own_rows, total_cells), 1)
    expo = jnp.where(row_ids == col_ids, jnp.float32(0.0), jnp.exp(affinity_scores))
    row_total = jnp.sum(expo, axis=1, keepdims=True)
    prob = expo / row_total
    neighbour_coefficients = (prob - count_lists(neighbours, col_ids) / K).astype(jnp.bfloat16)
    source_portion = jnp.dot(
        neighbour_coefficients, codes_whole, preferred_element_type=jnp.float32
    )
    target_portion = lax.psum_scatter(
        collapsed_lines(neighbour_coefficients, sample_vectors),
        ("grp", "peak"),
        scatter_dimension=0,
        tiled=True,
    )
    vector_derivative = (source_portion + target_portion) / sharpness_divisor
    dhidden, gain_part, in_part, out_part = tower_backward(
        vector_derivative, gain, w_in, w_out, saved
    )
    gain_grad, in_grad, out_grad = lax.psum((gain_part, in_part, out_part), ("grp", "peak"))
    dhidden_whole = lax.all_gather(dhidden, ("grp", "peak"), axis=0, tiled=True)
    peak_grad = collapsed_lines(masked, dhidden_whole)
    return (peak_grad, gain_grad, in_grad, out_grad)


def solution(mesh):
    placed = (
        P(None, ("grp", "peak")),
        P(None, ("grp", "peak")),
        P(("grp", "peak"), None),
        P(("grp", "peak"), None),
        P(),
        P(),
        P(),
    )
    return jax.shard_map(
        body,
        mesh=mesh,
        in_specs=placed,
        out_specs=(P(("grp", "peak"), None), P(), P(), P()),
        check_vma=False,
    )
```

profile of v0, /device:TPU:0, one launch (start us, length us, event | category | flops | bytes accessed | tf_op | source)
XLA Modules:
  0.0 479.7 jit_solution(14219044609887219653)
XLA Ops:
  7.2 0.8 convert_element_type.69
  8.1 0.1 copy.12
  8.2 0.3 broadcast_in_dim.6
  8.6 0.2 copy-done
  8.8 2.2 fusion.5
  11.0 0.0 all-reduce.9.cloned.1.call-start
  11.1 0.5 iota_add_fusion
  11.6 1.0 slice_reduce_fusion.14
  12.6 129.2 %all-reduce.7.cloned.1.call-done = f32[128,512]{1,0:T(8,128)} async-done(((f32[128,512]{1,0:T(8,128)}), f32[128,512]{1,0:T(8,128)}) %all-reduce.7.cloned.1.call-update) | async-done | bytes 262160
  141.7 0.8 multiply_reduce_fusion.2
  142.6 0.5 copy-done.6
  143.1 0.9 fusion.14
  144.0 0.3 multiply_reduce_fusion.4
  144.3 0.1 fusion.33
  144.4 0.4 copy-done.8
  144.8 65.5 %all-gather = bf16[32,4,256]{2,1,0:T(4,128)(2,1)S(1)} all-gather(bf16[1,4,256]{2,1,0:T(4,128)(2,1)S(1)} %fusion.33), channel_id=1, replica_groups=mesh['grp'=4,'peak'=8] {'grp','peak'}, dimensions={0}, use_global_device_ids=true | all-gather | bytes 67584 | tf_op jit(solution)/shard_map/all_gather | solution.py:82
  210.4 1.0 fusion.20
  211.4 1.7 fusion.17
  213.1 0.0 all-reduce.11.cloned.1.call-start
  213.2 119.6 %all-reduce.9.cloned.1.call-done = f32[128,256]{1,0:T(8,128)} async-done(((f32[128,256]{1,0:T(8,128)}), f32[128,256]{1,0:T(8,128)}) %all-reduce.9.cloned.1.call-update) | async-done | bytes 131088
  332.8 1.1 multiply_reduce_fusion.3
  333.9 0.2 fusion
  334.0 1.1 fusion.15
  335.1 2.1 fusion.13
  337.3 1.1 multiply_reduce_fusion
  338.4 0.8 fusion.11
  339.2 66.2 %all-gather.1 = bf16[32,4,512]{2,1,0:T(4,128)(2,1)S(1)} all-gather(bf16[1,4,512]{2,1,0:T(4,128)(2,1)S(1)} %fusion.11), channel_id=1, replica_groups=mesh['grp'=4,'peak'=8] {'grp','peak'}, dimensions={0}, use_global_device_ids=true | all-gather | bytes 135168 | tf_op jit(solution)/shard_map/all_gather | solution.py:107
  405.4 37.0 %psum.21 = f32[512]{0:T(512)} all-reduce(f32[512]{0:T(512)S(1)} %get-tuple-element.4), channel_id=1, replica_groups=mesh['grp'=4,'peak'=8] {'grp','peak'}, use_global_device_ids=true, to_apply=%region_8.9 | all-reduce | flops 512 | bytes 4096 | tf_op jit(solution)/shard_map/psum | solution.py:106
  442.4 3.8 fusion.4
  446.2 23.9 %all-reduce.11.cloned.1.call-done = (f32[512,512]{1,0:T(8,128)}, f32[512,256]{1,0:T(8,128)}) async-done(((f32[512,512]{1,0:T(8,128)}, f32[512,256]{1,0:T(8,128)}), (f32[512,512]{1,0:T(8,128)}, f32[512,256]{1,0:T(8,128)})) %all-reduce.11.cloned.1.call-update) | async-done | bytes 1572880 | tf_op jit(solution)/shard_map/psum | solution.py:106
  470.1 2.3 copy.21
  472.4 0.8 copy.22
  (26 shorter events, 0.2 us)
Async XLA Ops:
  7.2 1.6 copy-start
  7.2 134.5 %all-reduce.7.cloned.1.call-start = ((), (), s32[]{:S(2)}) async-start(), calls=%async_computation | async-start | bytes 524288
  8.2 3.4 copy-start.3
  8.2 134.9 %copy-start.1 = (bf16[512,512]{1,0:T(8,128)(2,1)S(1)}, bf16[512,512]{1,0:T(8,128)(2,1)}, u32[]{:S(2)}) copy-start(bf16[512,512]{1,0:T(8,128)(2,1)} %param.12) | copy-start | bytes 1572868
  8.2 134.9 %copy-start.5 = (f32[512]{0:T(512)S(1)}, f32[512]{0:T(512)}, u32[]{:S(2)}) copy-start(f32[512]{0:T(512)} %param.11) | copy-start | bytes 6148
  8.8 135.2 %copy-start.4 = (bf16[512,256]{1,0:T(8,128)(2,1)S(1)}, bf16[512,256]{1,0:T(8,128)(2,1)}, u32[]{:S(2)}) copy-start(bf16[512,256]{1,0:T(8,128)(2,1)} %param.13) | copy-start | bytes 786436
  11.0 321.7 %all-reduce.9.cloned.1.call-start = ((), (), s32[]{:S(2)}) async-start(), calls=%async_computation.1 | async-start | bytes 262144
  142.6 0.5 copy-start.6
  144.3 0.5 copy-start.8
  210.4 123.5 %copy-start.9 = (f32[4]{0:T(128)S(1)}, f32[4]{0:T(128)}, u32[]{:S(2)}) copy-start(f32[4]{0:T(128)} %copy-done.8) | copy-start | bytes 52
  210.4 124.8 %copy-start.7 = (f32[4]{0:T(128)S(1)}, f32[4]{0:T(128)}, u32[]{:S(2)}) copy-start(f32[4]{0:T(128)} %copy-done.6) | copy-start | bytes 52
  213.1 257.0 %all-reduce.11.cloned.1.call-start = ((), (), s32[]{:S(2)}) async-start(), calls=%async_computation.2 | async-start | bytes 3145728 | tf_op jit(solution)/shard_map/psum | solution.py:106
  470.1 2.3 copy-start.2
Sparse Core Ops, SparseCore 0:
  14.1 127.5 all-reduce.6
  213.2 119.4 all-reduce.8
  338.7 131.3 all-reduce.10
where the time goes:
time: 481 us; the launch traced here: 480 us
  waiting for transfers between devices  273 us (57%)
  blocking collectives  169 us (35%)
  matrix products  15.5 us (3%)
  between operations  13.8 us (3%)
  local copies, waits for them, and re-layouts  5.79 us (1%)
    unnamed x5, waiting for transfers between devices  249 us
    all_gather x1, blocking collectives, body(): dhidden_whole = lax.all_gather(dhidden, ('grp', 'peak'), axis=0, tiled=True)  66.2 us
    all_gather x1, blocking collectives, body(): lax.all_gather(sample_vectors, ('grp', 'peak'), axis=0, tiled=True)  65.5 us
    psum x1, blocking collectives, body(): lax.psum((gain_part, in_part, out_part), ('grp', 'peak'))  37 us
    psum x1, waiting for transfers between devices, body(): lax.psum((gain_part, in_part, out_part), ('grp', 'peak'))  23.9 us
  transfers between devices with their start and end apart: 3, of which 3 were waited for; matrix products, arithmetic and copies ran while one was open for 2% of the time, Pallas kernels for 0%

commit v1 on v0

v1 whole, which is shorter than its diff:
```python
import functools

import jax
import jax.numpy as jnp
from jax import lax
from jax.experimental import pallas as pl
from jax.experimental.pallas import tpu as pltpu
from jax.sharding import PartitionSpec as P

TILE = 128
EXTRA = 16
ALL = ("grp", "peak")
VMEM_BYTES = 56 * 1024 * 1024

sharpness_divisor = 0.2
eps_norm = 1e-06
gelu_coef = 0.7978845608
cubic_coef = 0.044715

F32 = jnp.float32
BF16 = jnp.bfloat16


def dot(left, right, left_dim, right_dim):
    return lax.dot_general(
        left, right, (((left_dim,), (right_dim,)), ((), ())), preferred_element_type=F32
    )


def core_index():
    return lax.rem(lax.axis_index("grp"), 2)


def partial_kernel(
    carried, pieces, counts_hbm, mask_ref, lists_ref, weight_hbm, send_ref, keep_ref,
    counts_ref, weight_ref, total_ref, counts_sem, weight_sem,
):
    cells, peaks = counts_ref.shape
    half = cells // 2
    span = peaks // pieces

    def copies(piece):
        at = pl.ds(piece * span, span)
        return (
            pltpu.make_async_copy(counts_hbm.at[:, at], counts_ref.at[:, at], counts_sem.at[piece]),
            pltpu.make_async_copy(weight_hbm.at[at, :], weight_ref.at[at, :], weight_sem.at[piece]),
        )

    for piece in range(pieces):
        for copy in copies(piece):
            copy.start()
    mask = mask_ref[...].astype(F32).astype(BF16)
    for piece in range(pieces):
        for copy in copies(piece):
            copy.wait()
        first = piece * span
        masked = jnp.concatenate(
            [
                counts_ref[:, start : start + TILE] * mask[:, start // TILE : start // TILE + 1]
                for start in range(first, first + span, TILE)
            ],
            axis=1,
        )
        term = jnp.dot(masked, weight_ref[first : first + span, :], preferred_element_type=F32)
        total_ref[...] = term if piece == 0 else total_ref[...] + term
    core = core_index()
    send_ref[:half, :] = total_ref[pl.ds((1 - core) * half, half), :].astype(BF16)
    keep_ref[:half, :] = total_ref[pl.ds(core * half, half), :].astype(BF16)
    if carried:
        own, length = lists_ref.shape
        position = lax.axis_index("grp") * lax.axis_size("peak") + lax.axis_index("peak")
        columns = lax.broadcasted_iota(jnp.int32, (own, keep_ref.shape[1]), 1)
        rows = lax.broadcasted_iota(jnp.int32, (own, keep_ref.shape[1]), 0)
        place = (columns == rows + position * own).astype(F32)
        lists = dot(lists_ref[...].astype(F32), place, 0, 0)
        lists = jnp.concatenate([lists, jnp.zeros((2 * EXTRA - length, lists.shape[1]), F32)], axis=0)
        low, high = lists[:EXTRA], lists[EXTRA:]
        send_ref[half:, :] = jnp.where(core == 0, high, low).astype(BF16)
        keep_ref[half:, :] = jnp.where(core == 0, low, high).astype(BF16)


def partial_hidden(carried, counts, tile_mask, neighbours, peak_weight):
    cells, peaks = counts.shape
    width = peak_weight.shape[1]
    pieces = 4
    whole = pl.BlockSpec(memory_space=pltpu.VMEM)
    remote = pl.BlockSpec(memory_space=pl.ANY)
    rows = cells // 2 + (EXTRA if carried else 0)
    return pl.pallas_call(
        functools.partial(partial_kernel, carried, pieces),
        out_shape=[jax.ShapeDtypeStruct((rows, width), BF16)] * 2,
        in_specs=[remote, whole, whole, remote],
        out_specs=[whole, whole],
        scratch_shapes=[
            pltpu.VMEM((cells, peaks), BF16),
            pltpu.VMEM((peaks, width), BF16),
            pltpu.VMEM((cells, width), F32),
            pltpu.SemaphoreType.DMA((pieces,)),
            pltpu.SemaphoreType.DMA((pieces,)),
        ],
        compiler_params=pltpu.CompilerParams(vmem_limit_bytes=VMEM_BYTES),
        cost_estimate=pl.CostEstimate(
            flops=2 * cells * peaks * width,
            bytes_accessed=2 * (cells * peaks + peaks * width + 2 * rows * width),
            transcendentals=0,
        ),
    )(counts, tile_mask, neighbours, peak_weight)


def turn_kernel(counts_ref, mask_ref, turned_ref):
    mask = mask_ref[...].astype(F32).astype(BF16)
    for start in range(0, counts_ref.shape[1], TILE):
        tile = start // TILE
        piece = counts_ref[:, start : start + TILE] * mask[:, tile : tile + 1]
        turned_ref[start : start + TILE, :] = piece.T


def turn(counts, tile_mask):
    cells, peaks = counts.shape
    whole = pl.BlockSpec(memory_space=pltpu.VMEM)
    return pl.pallas_call(
        turn_kernel,
        out_shape=jax.ShapeDtypeStruct((peaks, cells), BF16),
        in_specs=[whole, whole],
        out_specs=whole,
        compiler_params=pltpu.CompilerParams(vmem_limit_bytes=VMEM_BYTES),
        cost_estimate=pl.CostEstimate(
            flops=cells * peaks, bytes_accessed=4 * cells * peaks, transcendentals=0
        ),
    )(counts, tile_mask)


def tower_kernel(
    carried, length_of, pieces, own_ref, other_ref, lists_ref, turned_ref, gain_ref, w_in_ref, w_out_ref,
    peak_grad_hbm, gain_grad_ref, in_grad_hbm, out_grad_hbm,
    hidden_ref, peak_grad_ref, in_grad_ref, out_grad_ref, peak_sem, side_sem,
):
    cells = hidden_ref.shape[0]
    half = cells // 2
    core = core_index()
    hidden_ref[pl.ds(core * half, half), :] = own_ref[:half, :].astype(F32)
    hidden_ref[pl.ds((1 - core) * half, half), :] = other_ref[:half, :].astype(F32)
    if carried:
        own_lists, other_lists = own_ref[half:, :cells].astype(F32), other_ref[half:, :cells].astype(F32)
        lists = jnp.concatenate(
            [jnp.where(core == 0, own_lists, other_lists), jnp.where(core == 0, other_lists, own_lists)], axis=0
        )
    else:
        lists = lists_ref[...].astype(F32)
    gain = gain_ref[...]
    w_in, w_out = w_in_ref[...], w_out_ref[...]

    hidden = hidden_ref[...]
    scale = lax.rsqrt(jnp.mean(hidden * hidden, axis=1, keepdims=True) + eps_norm)
    normed = hidden * scale
    rounded = (normed * gain).astype(BF16)
    preact = jnp.dot(rounded, w_in, preferred_element_type=F32)
    square = preact * preact
    tangent = jnp.tanh(gelu_coef * preact * (1.0 + cubic_coef * square))
    activ = (0.5 * preact * (1.0 + tangent)).astype(BF16)
    slope = 0.5 * (1.0 + tangent) + 0.5 * preact * (1.0 - tangent * tangent) * gelu_coef * (
        1.0 + 3.0 * cubic_coef * square
    )
    project = jnp.dot(activ, w_out, preferred_element_type=F32)
    length = lax.rsqrt(jnp.sum(project * project, axis=1, keepdims=True) + eps_norm)
    unit = project * length
    codes = unit.astype(BF16)

    scores = dot(codes, codes, 1, 1) / sharpness_divisor
    targets = lax.broadcasted_iota(jnp.int32, (cells, cells), 0)
    sources = lax.broadcasted_iota(jnp.int32, (cells, cells), 1)
    expo = jnp.where(targets == sources, 0.0, jnp.exp(scores))
    prob = expo * (1.0 / jnp.sum(expo, axis=0, keepdims=True))
    places = targets.astype(F32)
    tallies = jnp.zeros((cells, cells), F32)
    for slot in range(length_of):
        tallies = tallies + (lists[slot : slot + 1, :] == places).astype(F32)
    coupling = (prob - tallies / length_of).astype(BF16)
    dcodes = (dot(coupling, codes, 0, 0) + dot(coupling, codes, 1, 0)) / sharpness_divisor

    dproj = (length * (dcodes - unit * jnp.sum(unit * dcodes, axis=1, keepdims=True))).astype(BF16)
    dpre = (dot(dproj, w_out, 1, 1) * slope).astype(BF16)
    dround = dot(dpre, w_in, 1, 1)
    gain_grad_ref[...] = jnp.sum(dround * normed, axis=0, keepdims=True)
    dnorm = dround * gain
    dhidden = (scale * (dnorm - normed * jnp.mean(dnorm * normed, axis=1, keepdims=True))).astype(BF16)

    span = turned_ref.shape[0] // pieces

    def peak_copy(piece):
        at = pl.ds(piece * span, span)
        return pltpu.make_async_copy(peak_grad_ref.at[at, :], peak_grad_hbm.at[at, :], peak_sem.at[piece])

    for piece in range(pieces):
        at = pl.ds(piece * span, span)
        peak_grad_ref[at, :] = jnp.dot(turned_ref[at, :], dhidden, preferred_element_type=F32)
        peak_copy(piece).start()
    in_copy = pltpu.make_async_copy(in_grad_ref, in_grad_hbm, side_sem.at[0])
    out_copy = pltpu.make_async_copy(out_grad_ref, out_grad_hbm, side_sem.at[1])
    in_grad_ref[...] = dot(rounded, dpre, 0, 0)
    in_copy.start()
    out_grad_ref[...] = dot(activ, dproj, 0, 0)
    out_copy.start()
    for piece in range(pieces):
        peak_copy(piece).wait()
    in_copy.wait()
    out_copy.wait()


def tower(carried, length_of, own, other, lists, turned, gain, w_in, w_out):
    peaks, cells = turned.shape
    width, hid = w_in.shape
    codes = w_out.shape[1]
    pieces = 8
    whole = pl.BlockSpec(memory_space=pltpu.VMEM)
    remote = pl.BlockSpec(memory_space=pl.ANY)
    return pl.pallas_call(
        functools.partial(tower_kernel, carried, length_of, pieces),
        out_shape=[
            jax.ShapeDtypeStruct((peaks, width), F32),
            jax.ShapeDtypeStruct((1, width), F32),
            jax.ShapeDtypeStruct((width, hid), F32),
            jax.ShapeDtypeStruct((hid, codes), F32),
        ],
        in_specs=[whole] * 7,
        out_specs=[remote, whole, remote, remote],
        scratch_shapes=[
            pltpu.VMEM((cells, width), F32),
            pltpu.VMEM((peaks, width), F32),
            pltpu.VMEM((width, hid), F32),
            pltpu.VMEM((hid, codes), F32),
            pltpu.SemaphoreType.DMA((pieces,)),
            pltpu.SemaphoreType.DMA((2,)),
        ],
        compiler_params=pltpu.CompilerParams(vmem_limit_bytes=VMEM_BYTES),
        cost_estimate=pl.CostEstimate(
            flops=2 * cells * width * (peaks + 3 * hid + 3 * codes),
            bytes_accessed=2 * peaks * cells + 4 * peaks * width + 6 * width * hid + 6 * hid * codes,
            transcendentals=cells * (hid + cells),
        ),
    )(own, other, lists, turned, gain, w_in, w_out)


def flips(n_grp, n_peak):
    grp_bits = [bit * n_peak for bit in (2, 4, 8, 16, 32, 64) if bit < n_grp]
    peak_bits = [bit for bit in (1, 2, 4, 8, 16, 32, 64) if bit < n_peak]
    order = grp_bits + peak_bits
    if len(order) == 4:
        order = [order[0], order[2], order[1], order[3]]
    swapped = list(order)
    for at in range(0, len(order) - 1, 2):
        swapped[at], swapped[at + 1] = order[at + 1], order[at]
    return list(zip(order, swapped, strict=True))


def body(n_grp, n_peak, counts, tile_mask, neighbours, peak_weight, gain, w_in, w_out):
    cells = counts.shape[0]
    length_of = neighbours.shape[1]
    carried = cells <= 256 and cells <= peak_weight.shape[1]
    devices = n_grp * n_peak

    def exchange(values, bits):
        pairs = [(i, i ^ bits[(i // n_peak) % 2]) for i in range(devices)]
        return lax.ppermute(values, ALL, pairs)

    def add(left, right):
        return (left.astype(F32) + right.astype(F32)).astype(BF16)

    send, held = partial_hidden(carried, counts, tile_mask, neighbours, peak_weight)
    held = add(held, exchange(send, (n_peak, n_peak)))
    turned = turn(counts, tile_mask)
    for bits in flips(n_grp, n_peak):
        held = add(held, exchange(held, bits))
    other = exchange(held, (n_peak, n_peak))
    if carried:
        lists = neighbours
    else:
        lists = lax.all_gather(neighbours, ALL, axis=0, tiled=True).T
    peak_grad, gain_grad, in_grad, out_grad = tower(
        carried, length_of, held, other, lists, turned, gain.reshape(1, -1), w_in, w_out
    )
    return (peak_grad, gain_grad.reshape(-1), in_grad, out_grad)


def solution(mesh):
    placed = (
        P(None, ALL),
        P(None, ALL),
        P(ALL, None),
        P(ALL, None),
        P(),
        P(),
        P(),
    )
    return jax.shard_map(
        functools.partial(body, mesh.shape["grp"], mesh.shape["peak"]),
        mesh=mesh,
        in_specs=placed,
        out_specs=(P(ALL, None), P(), P(), P()),
        check_vma=False,
    )
```

time: 481 us -> 38.5 us (0.08)
  waiting for transfers between devices: 273 us -> 10.9 us
  blocking collectives: 169 us -> 0 us
  matrix products: 15.5 us -> 0 us
  between operations: 13.8 us -> 0.68 us
  Pallas kernels: 0 us -> 12.5 us
  starting transfers between devices: 0.12 us -> 10.8 us
    unnamed x5 -> x0, waiting for transfers between devices: 249 us -> none
    all_gather x2 -> x0, blocking collectives: 132 us -> none  [the longest x1 66.2 us: body(): dhidden_whole = lax.all_gather(dhidden, ('grp', 'peak'), axis=0, tiled=True)]
    psum x1 -> x0, blocking collectives: 37 us -> none  [body(): lax.psum((gain_part, in_part, out_part), ('grp', 'peak'))]
    psum x1 -> x0, waiting for transfers between devices: 23.9 us -> none  [body(): lax.psum((gain_part, in_part, out_part), ('grp', 'peak'))]
    dot_general x11 -> x0, matrix products: 15.5 us -> none  [the longest x4 8.7 us: collapsed_lines(): lax.dot_general(left, right, (((0,), (0,)), ((), ())), preferred_element_...]
    pallas_call x0 -> x3, Pallas kernels: none -> 12.5 us  [the longest x1 6.33 us: tower(): pl.pallas_call(functools.partial(tower_kernel, carried, length_of, pieces...]
    ppermute x0 -> x6, waiting for transfers between devices: none -> 10.9 us  [exchange(): return lax.ppermute(values, ALL, pairs)]
    ppermute x0 -> x6, starting transfers between devices: none -> 10.8 us  [exchange(): return lax.ppermute(values, ALL, pairs)]
  transfers between devices with their start and end apart: 3 -> 6, of which waited for: 3 -> 5; matrix products, arithmetic and copies ran while one was open for 2% -> 0% of each run, Pallas kernels for 0% -> 7%
where the time goes in v1:
time: 38.5 us; the launch traced here: 37.9 us
  Pallas kernels  12.5 us (32%)
  waiting for transfers between devices  10.9 us (28%)
  starting transfers between devices  10.8 us (28%)
  local copies, waits for them, and re-layouts  2.04 us (5%)
  other arithmetic  1 us (3%)
  between operations  0.68 us (2%)
    ppermute x6, waiting for transfers between devices, exchange(): return lax.ppermute(values, ALL, pairs)  10.9 us
    ppermute x6, starting transfers between devices, exchange(): return lax.ppermute(values, ALL, pairs)  10.8 us
    pallas_call x1, Pallas kernels, tower(): pl.pallas_call(functools.partial(tower_kernel, carried, length_of, pieces...  6.33 us
    pallas_call x1, Pallas kernels, partial_hidden(): pl.pallas_call(functools.partial(partial_kernel, carried, pieces), out_sh...  3.59 us
    pallas_call x1, Pallas kernels, turn(): pl.pallas_call(turn_kernel, out_shape=jax.ShapeDtypeStruct((peaks, cells)...  2.54 us
    unnamed x5, local copies, waits for them, and re-layouts  2.04 us
    convert_element_type x5, other arithmetic, add(): return (left.astype(F32) + right.astype(F32)).astype(BF16)  1 us
  transfers between devices with their start and end apart: 6, of which 5 were waited for; matrix products, arithmetic and copies ran while one was open for 0% of the time, Pallas kernels for 7%

profile of v1, /device:TPU:0, one launch (start us, length us, event | category | flops | bytes accessed | tf_op | source)
XLA Modules:
  0.0 37.9 jit_solution(13062182555156448930)
XLA Ops:
  0.6 1.4 %copy.11.mask_ref = s32[128,16]{1,0:T(8,128)} copy(s32[128,16]{0,1:T(8,128)} %param.8) | data formatting | bytes 16384 | tf_op args[1]
  2.1 3.6 %shard_map.102 = (bf16[80,512]{1,0:T(8,128)(2,1)}, bf16[80,512]{1,0:T(8,128)(2,1)}) custom-call(bf16[128,2048]{1,0:T(8,128)(2,1)} %counts_ref.1, s32[128,16]{1,0:T(8,128)} %copy.11.mask_ref, s32[4,15]{1,0:T(4,128)} %lists_ref.3, bf16[2048,512]{1,0:T(8,128)(2,1)} %weight_hbm.1), custom_call_target="tpu_custom_call" | custom-call | flops 268435456 | bytes 2785280 | tf_op jit(solution)/shard_map/pallas_call | solution.py:89
  5.7 0.5 %collective-permute-start = (bf16[80,512]{1,0:T(8,128)(2,1)}, bf16[80,512]{1,0:T(8,128)(2,1)S(1)}, u32[]{:S(2)}, u32[]{:S(2)}) collective-permute-start(bf16[80,512]{1,0:T(8,128)(2,1)} %get-tuple-element.11), channel_id=1, source_target_pairs={{0,8},{1,9},{2,10},{3,11},{4,12},{5,13},{6,14},{7,15},{8,0},{9,1},... | collective-permute-start | bytes 245768 | tf_op jit(solution)/shard_map/ppermute | solution.py:264
  6.2 1.1 %collective-permute-done = bf16[80,512]{1,0:T(8,128)(2,1)S(1)} collective-permute-done((bf16[80,512]{1,0:T(8,128)(2,1)}, bf16[80,512]{1,0:T(8,128)(2,1)S(1)}, u32[]{:S(2)}, u32[]{:S(2)}) %collective-permute-start) | collective-permute-done | bytes 81952 | tf_op jit(solution)/shard_map/ppermute | solution.py:264
  7.3 0.9 %add_convert_fusion.4 = bf16[80,512]{1,0:T(8,128)(2,1)S(1)} fusion(bf16[80,512]{1,0:T(8,128)(2,1)S(1)} %collective-permute-done, bf16[80,512]{1,0:T(8,128)(2,1)} %get-tuple-element.10), kind=kLoop, calls=%fused_computation.4 | loop fusion | flops 163840 | bytes 245760 | tf_op jit(solution)/shard_map/convert_element_type | solution.py:267
  8.2 2.9 %collective-permute-start.1 = (bf16[80,512]{1,0:T(8,128)(2,1)S(1)}, bf16[80,512]{1,0:T(8,128)(2,1)S(1)}, u32[]{:S(2)}, u32[]{:S(2)}) collective-permute-start(bf16[80,512]{1,0:T(8,128)(2,1)S(1)} %add_convert_fusion.4), channel_id=1, source_target_pairs={{0,16},{1,17},{2,18},{3,19},{4,20},{5,21},{6,22},{7,23},{8,10},{9,... | collective-permute-start | bytes 245768 | tf_op jit(solution)/shard_map/ppermute | solution.py:264
  11.1 2.4 %collective-permute-done.1 = bf16[80,512]{1,0:T(8,128)(2,1)S(1)} collective-permute-done((bf16[80,512]{1,0:T(8,128)(2,1)S(1)}, bf16[80,512]{1,0:T(8,128)(2,1)S(1)}, u32[]{:S(2)}, u32[]{:S(2)}) %collective-permute-start.1) | collective-permute-done | bytes 81952 | tf_op jit(solution)/shard_map/ppermute | solution.py:264
  13.6 2.2 %collective-permute-start.2 = (bf16[80,512]{1,0:T(8,128)(2,1)S(1)}, bf16[80,512]{1,0:T(8,128)(2,1)S(1)}, u32[]{:S(2)}, u32[]{:S(2)}) collective-permute-start(bf16[80,512]{1,0:T(8,128)(2,1)S(1)} %add_convert_fusion.3), channel_id=1, source_target_pairs={{0,2},{1,3},{2,0},{3,1},{4,6},{5,7},{6,4},{7,5},{8,24},{9,25},{10,... | collective-permute-start | bytes 245768 | tf_op jit(solution)/shard_map/ppermute | solution.py:264
  15.7 2.4 %collective-permute-done.2 = bf16[80,512]{1,0:T(8,128)(2,1)S(1)} collective-permute-done((bf16[80,512]{1,0:T(8,128)(2,1)S(1)}, bf16[80,512]{1,0:T(8,128)(2,1)S(1)}, u32[]{:S(2)}, u32[]{:S(2)}) %collective-permute-start.2) | collective-permute-done | bytes 81952 | tf_op jit(solution)/shard_map/ppermute | solution.py:264
  18.2 2.0 %collective-permute-start.3 = (bf16[80,512]{1,0:T(8,128)(2,1)S(1)}, bf16[80,512]{1,0:T(8,128)(2,1)S(1)}, u32[]{:S(2)}, u32[]{:S(2)}) collective-permute-start(bf16[80,512]{1,0:T(8,128)(2,1)S(1)} %add_convert_fusion.2), channel_id=1, source_target_pairs={{0,1},{1,0},{2,3},{3,2},{4,5},{5,4},{6,7},{7,6},{8,12},{9,13},{10,... | collective-permute-start | bytes 245768 | tf_op jit(solution)/shard_map/ppermute | solution.py:264
  20.2 2.5 %collective-permute-done.3 = bf16[80,512]{1,0:T(8,128)(2,1)S(1)} collective-permute-done((bf16[80,512]{1,0:T(8,128)(2,1)S(1)}, bf16[80,512]{1,0:T(8,128)(2,1)S(1)}, u32[]{:S(2)}, u32[]{:S(2)}) %collective-permute-start.3) | collective-permute-done | bytes 81952 | tf_op jit(solution)/shard_map/ppermute | solution.py:264
  22.7 3.1 %collective-permute-start.4 = (bf16[80,512]{1,0:T(8,128)(2,1)S(1)}, bf16[80,512]{1,0:T(8,128)(2,1)S(1)}, u32[]{:S(2)}, u32[]{:S(2)}) collective-permute-start(bf16[80,512]{1,0:T(8,128)(2,1)S(1)} %add_convert_fusion.1), channel_id=1, source_target_pairs={{0,4},{1,5},{2,6},{3,7},{4,0},{5,1},{6,2},{7,3},{8,9},{9,8},{10,11... | collective-permute-start | bytes 245768 | tf_op jit(solution)/shard_map/ppermute | solution.py:264
  25.8 2.4 %collective-permute-done.4 = bf16[80,512]{1,0:T(8,128)(2,1)S(1)} collective-permute-done((bf16[80,512]{1,0:T(8,128)(2,1)S(1)}, bf16[80,512]{1,0:T(8,128)(2,1)S(1)}, u32[]{:S(2)}, u32[]{:S(2)}) %collective-permute-start.4) | collective-permute-done | bytes 81952 | tf_op jit(solution)/shard_map/ppermute | solution.py:264
  28.3 0.0 copy-start
  28.3 0.1 collective-permute-start.5
  28.4 2.5 %shard_map.103.turned_ref = bf16[2048,128]{1,0:T(8,128)(2,1)} custom-call(bf16[128,2048]{1,0:T(8,128)(2,1)} %counts_ref.1, s32[128,16]{1,0:T(8,128)} %copy.11.mask_ref), custom_call_target="tpu_custom_call" | custom-call | flops 262144 | bytes 1048576 | tf_op jit(solution)/shard_map/pallas_call | solution.py:121
  30.9 0.0 collective-permute-done.5.other_ref
  30.9 0.0 copy-start.1
  30.9 0.0 copy-done
  30.9 0.6 %copy-done.1 = bf16[80,512]{1,0:T(8,128)(2,1)} copy-done((bf16[80,512]{1,0:T(8,128)(2,1)}, bf16[80,512]{1,0:T(8,128)(2,1)S(1)}, u32[]{:S(2)}) %copy-start.1) | copy-done | bytes 81944
  31.5 6.3 %shard_map.104 = (f32[2048,512]{1,0:T(8,128)}, f32[1,512]{1,0:T(1,128)}, f32[512,512]{1,0:T(8,128)}, f32[512,256]{1,0:T(8,128)}) custom-call(bf16[80,512]{1,0:T(8,128)(2,1)} %copy-done, bf16[80,512]{1,0:T(8,128)(2,1)} %copy-done.1, s32[4,15]{1,0:T(4,128)} %lists_ref.3, bf16[2048,128]{1,0:T(8,128)(2,1)} %shard_map.103.turned_ref, f32[1,512]{1,0:T(1,128)} %bitcast.2, ...), custom_call_target="tpu_custom_call" | custom-call | flops 570425344 | bytes 7077888 | tf_op jit(solution)/shard_map/pallas_call | solution.py:217
  (4 shorter events, 0.1 us)
Async XLA Ops:
  5.7 1.7 %collective-permute-start = (bf16[80,512]{1,0:T(8,128)(2,1)}, bf16[80,512]{1,0:T(8,128)(2,1)S(1)}, u32[]{:S(2)}, u32[]{:S(2)}) collective-permute-start(bf16[80,512]{1,0:T(8,128)(2,1)} %get-tuple-element.11), channel_id=1, source_target_pairs={{0,8},{1,9},{2,10},{3,11},{4,12},{5,13},{6,14},{7,15},{8,0},{9,1},... | collective-permute-start | bytes 245768 | tf_op jit(solution)/shard_map/ppermute | solution.py:264
  8.2 5.3 %collective-permute-start.1 = (bf16[80,512]{1,0:T(8,128)(2,1)S(1)}, bf16[80,512]{1,0:T(8,128)(2,1)S(1)}, u32[]{:S(2)}, u32[]{:S(2)}) collective-permute-start(bf16[80,512]{1,0:T(8,128)(2,1)S(1)} %add_convert_fusion.4), channel_id=1, source_target_pairs={{0,16},{1,17},{2,18},{3,19},{4,20},{5,21},{6,22},{7,23},{8,10},{9,... | collective-permute-start | bytes 245768 | tf_op jit(solution)/shard_map/ppermute | solution.py:264
  13.6 4.6 %collective-permute-start.2 = (bf16[80,512]{1,0:T(8,128)(2,1)S(1)}, bf16[80,512]{1,0:T(8,128)(2,1)S(1)}, u32[]{:S(2)}, u32[]{:S(2)}) collective-permute-start(bf16[80,512]{1,0:T(8,128)(2,1)S(1)} %add_convert_fusion.3), channel_id=1, source_target_pairs={{0,2},{1,3},{2,0},{3,1},{4,6},{5,7},{6,4},{7,5},{8,24},{9,25},{10,... | collective-permute-start | bytes 245768 | tf_op jit(solution)/shard_map/ppermute | solution.py:264
  18.2 4.5 %collective-permute-start.3 = (bf16[80,512]{1,0:T(8,128)(2,1)S(1)}, bf16[80,512]{1,0:T(8,128)(2,1)S(1)}, u32[]{:S(2)}, u32[]{:S(2)}) collective-permute-start(bf16[80,512]{1,0:T(8,128)(2,1)S(1)} %add_convert_fusion.2), channel_id=1, source_target_pairs={{0,1},{1,0},{2,3},{3,2},{4,5},{5,4},{6,7},{7,6},{8,12},{9,13},{10,... | collective-permute-start | bytes 245768 | tf_op jit(solution)/shard_map/ppermute | solution.py:264
  22.7 5.5 %collective-permute-start.4 = (bf16[80,512]{1,0:T(8,128)(2,1)S(1)}, bf16[80,512]{1,0:T(8,128)(2,1)S(1)}, u32[]{:S(2)}, u32[]{:S(2)}) collective-permute-start(bf16[80,512]{1,0:T(8,128)(2,1)S(1)} %add_convert_fusion.1), channel_id=1, source_target_pairs={{0,4},{1,5},{2,6},{3,7},{4,0},{5,1},{6,2},{7,3},{8,9},{9,8},{10,11... | collective-permute-start | bytes 245768 | tf_op jit(solution)/shard_map/ppermute | solution.py:264
  28.3 2.6 %copy-start = (bf16[80,512]{1,0:T(8,128)(2,1)}, bf16[80,512]{1,0:T(8,128)(2,1)S(1)}, u32[]{:S(2)}) copy-start(bf16[80,512]{1,0:T(8,128)(2,1)S(1)} %add_convert_fusion.own_ref) | copy-start | bytes 245764
  28.3 2.6 %collective-permute-start.5 = (bf16[80,512]{1,0:T(8,128)(2,1)S(1)}, bf16[80,512]{1,0:T(8,128)(2,1)S(1)}, u32[]{:S(2)}, u32[]{:S(2)}) collective-permute-start(bf16[80,512]{1,0:T(8,128)(2,1)S(1)} %add_convert_fusion.own_ref), channel_id=1, source_target_pairs={{0,8},{1,9},{2,10},{3,11},{4,12},{5,13},{6,14},{7,15},{8,0},{9,1},... | collective-permute-start | bytes 245768 | tf_op jit(solution)/shard_map/ppermute | solution.py:264
  30.9 0.6 %copy-start.1 = (bf16[80,512]{1,0:T(8,128)(2,1)}, bf16[80,512]{1,0:T(8,128)(2,1)S(1)}, u32[]{:S(2)}) copy-start(bf16[80,512]{1,0:T(8,128)(2,1)S(1)} %collective-permute-done.5.other_ref) | copy-start | bytes 245764

commit v2 on v1

--- a/solution.py
+++ b/solution.py
@@ -10,16 +10,17 @@
 TILE = 128
 EXTRA = 16
 ALL = ("grp", "peak")
-VMEM_BYTES = 56 * 1024 * 1024
+MIB = 1024 * 1024
+F32 = jnp.float32
+BF16 = jnp.bfloat16
+LINK = jnp.float16
+LIFT = 2.0
 
 sharpness_divisor = 0.2
 eps_norm = 1e-06
 gelu_coef = 0.7978845608
 cubic_coef = 0.044715
 
-F32 = jnp.float32
-BF16 = jnp.bfloat16
-
 
 def dot(left, right, left_dim, right_dim):
     return lax.dot_general(
@@ -32,8 +33,8 @@
 
 
 def partial_kernel(
-    carried, pieces, counts_hbm, mask_ref, lists_ref, weight_hbm, send_ref, keep_ref,
-    counts_ref, weight_ref, total_ref, counts_sem, weight_sem,
+    carried, pieces, counts_hbm, mask_hbm, lists_hbm, weight_hbm, send_ref, keep_ref,
+    counts_ref, mask_ref, lists_ref, weight_ref, total_ref, counts_sem, weight_sem, side_sem,
 ):
     cells, peaks = counts_ref.shape
     half = cells // 2
@@ -46,26 +47,18 @@
             pltpu.make_async_copy(weight_hbm.at[at, :], weight_ref.at[at, :], weight_sem.at[piece]),
         )
 
+    sides = (
+        pltpu.make_async_copy(mask_hbm, mask_ref, side_sem.at[0]),
+        pltpu.make_async_copy(lists_hbm, lists_ref, side_sem.at[1]),
+    )
+    for copy in sides:
+        copy.start()
     for piece in range(pieces):
         for copy in copies(piece):
             copy.start()
-    mask = mask_ref[...].astype(F32).astype(BF16)
-    for piece in range(pieces):
-        for copy in copies(piece):
-            copy.wait()
-        first = piece * span
-        masked = jnp.concatenate(
-            [
-                counts_ref[:, start : start + TILE] * mask[:, start // TILE : start // TILE + 1]
-                for start in range(first, first + span, TILE)
-            ],
-            axis=1,
-        )
-        term = jnp.dot(masked, weight_ref[first : first + span, :], preferred_element_type=F32)
-        total_ref[...] = term if piece == 0 else total_ref[...] + term
+    for copy in sides:
+        copy.wait()
     core = core_index()
-    send_ref[:half, :] = total_ref[pl.ds((1 - core) * half, half), :].astype(BF16)
-    keep_ref[:half, :] = total_ref[pl.ds(core * half, half), :].astype(BF16)
     if carried:
         own, length = lists_ref.shape
         position = lax.axis_index("grp") * lax.axis_size("peak") + lax.axis_index("peak")
@@ -75,47 +68,70 @@
         lists = dot(lists_ref[...].astype(F32), place, 0, 0)
         lists = jnp.concatenate([lists, jnp.zeros((2 * EXTRA - length, lists.shape[1]), F32)], axis=0)
         low, high = lists[:EXTRA], lists[EXTRA:]
-        send_ref[half:, :] = jnp.where(core == 0, high, low).astype(BF16)
-        keep_ref[half:, :] = jnp.where(core == 0, low, high).astype(BF16)
-
-
-def partial_hidden(carried, counts, tile_mask, neighbours, peak_weight):
+        send_ref[half:, :] = jnp.where(core == 0, high, low)
+        keep_ref[half:, :] = jnp.where(core == 0, low, high)
+    mask = (LIFT * mask_ref[...].astype(F32)).T
+    for piece in range(pieces):
+        for copy in copies(piece):
+            copy.wait()
+        first = piece * span
+        masked = jnp.concatenate(
+            [
+                counts_ref[:, start : start + TILE]
+                * jnp.broadcast_to(mask[:, start // TILE : start // TILE + 1], (cells, TILE)).astype(BF16)
+                for start in range(first, first + span, TILE)
+            ],
+            axis=1,
+        )
+        term = jnp.dot(masked, weight_ref[first : first + span, :], preferred_element_type=F32)
+        total_ref[...] = term if piece == 0 else total_ref[...] + term
+    send_ref[:half, :] = total_ref[pl.ds((1 - core) * half, half), :]
+    keep_ref[:half, :] = total_ref[pl.ds(core * half, half), :]
+
+
+def partial_hidden(carried, counts, mask, neighbours, peak_weight):
     cells, peaks = counts.shape
     width = peak_weight.shape[1]
     pieces = 4
     whole = pl.BlockSpec(memory_space=pltpu.VMEM)
-    remote = pl.BlockSpec(memory_space=pl.ANY)
+    main = pl.BlockSpec(memory_space=pltpu.HBM)
     rows = cells // 2 + (EXTRA if carried else 0)
     return pl.pallas_call(
         functools.partial(partial_kernel, carried, pieces),
-        out_shape=[jax.ShapeDtypeStruct((rows, width), BF16)] * 2,
-        in_specs=[remote, whole, whole, remote],
+        out_shape=[pltpu.VMEM((rows, width), F32)] * 2,
+        in_specs=[main] * 4,
         out_specs=[whole, whole],
         scratch_shapes=[
             pltpu.VMEM((cells, peaks), BF16),
+            pltpu.VMEM(mask.shape, jnp.int32),
+            pltpu.VMEM(neighbours.shape, jnp.int32),
             pltpu.VMEM((peaks, width), BF16),
             pltpu.VMEM((cells, width), F32),
             pltpu.SemaphoreType.DMA((pieces,)),
             pltpu.SemaphoreType.DMA((pieces,)),
+            pltpu.SemaphoreType.DMA((2,)),
         ],
-        compiler_params=pltpu.CompilerParams(vmem_limit_bytes=VMEM_BYTES),
+        compiler_params=pltpu.CompilerParams(
+            vmem_limit_bytes=4 * MIB + 2 * (cells * peaks + peaks * width) + 20 * cells * width
+        ),
         cost_estimate=pl.CostEstimate(
             flops=2 * cells * peaks * width,
-            bytes_accessed=2 * (cells * peaks + peaks * width + 2 * rows * width),
+            bytes_accessed=2 * (cells * peaks + peaks * width) + 8 * rows * width,
             transcendentals=0,
         ),
-    )(counts, tile_mask, neighbours, peak_weight)
+    )(*(pltpu.with_memory_space_constraint(x, pltpu.HBM) for x in (counts, mask, neighbours, peak_weight)))
 
 
 def turn_kernel(counts_ref, mask_ref, turned_ref):
-    mask = mask_ref[...].astype(F32).astype(BF16)
+    cells = counts_ref.shape[0]
+    mask = mask_ref[...].astype(F32).T
     for start in range(0, counts_ref.shape[1], TILE):
         tile = start // TILE
-        piece = counts_ref[:, start : start + TILE] * mask[:, tile : tile + 1]
-        turned_ref[start : start + TILE, :] = piece.T
-
-
-def turn(counts, tile_mask):
+        column = jnp.broadcast_to(mask[:, tile : tile + 1], (cells, TILE)).astype(BF16)
+        turned_ref[start : start + TILE, :] = (counts_ref[:, start : start + TILE] * column).T
+
+
+def turn(counts, mask):
     cells, peaks = counts.shape
     whole = pl.BlockSpec(memory_space=pltpu.VMEM)
     return pl.pallas_call(
@@ -123,11 +139,11 @@
         out_shape=jax.ShapeDtypeStruct((peaks, cells), BF16),
         in_specs=[whole, whole],
         out_specs=whole,
-        compiler_params=pltpu.CompilerParams(vmem_limit_bytes=VMEM_BYTES),
+        compiler_params=pltpu.CompilerParams(vmem_limit_bytes=4 * MIB + 8 * cells * peaks),
         cost_estimate=pl.CostEstimate(
             flops=cells * peaks, bytes_accessed=4 * cells * peaks, transcendentals=0
         ),
-    )(counts, tile_mask)
+    )(counts, mask)
 
 
 def tower_kernel(
@@ -138,10 +154,10 @@
     cells = hidden_ref.shape[0]
     half = cells // 2
     core = core_index()
-    hidden_ref[pl.ds(core * half, half), :] = own_ref[:half, :].astype(F32)
-    hidden_ref[pl.ds((1 - core) * half, half), :] = other_ref[:half, :].astype(F32)
+    hidden_ref[pl.ds(core * half, half), :] = own_ref[:half, :] * (1.0 / LIFT)
+    hidden_ref[pl.ds((1 - core) * half, half), :] = other_ref[:half, :] * (1.0 / LIFT)
     if carried:
-        own_lists, other_lists = own_ref[half:, :cells].astype(F32), other_ref[half:, :cells].astype(F32)
+        own_lists, other_lists = own_ref[half:, :cells], other_ref[half:, :cells]
         lists = jnp.concatenate(
             [jnp.where(core == 0, own_lists, other_lists), jnp.where(core == 0, other_lists, own_lists)], axis=0
         )
@@ -213,7 +229,7 @@
     codes = w_out.shape[1]
     pieces = 8
     whole = pl.BlockSpec(memory_space=pltpu.VMEM)
-    remote = pl.BlockSpec(memory_space=pl.ANY)
+    main = pl.BlockSpec(memory_space=pltpu.HBM)
     return pl.pallas_call(
         functools.partial(tower_kernel, carried, length_of, pieces),
         out_shape=[
@@ -223,7 +239,7 @@
             jax.ShapeDtypeStruct((hid, codes), F32),
         ],
         in_specs=[whole] * 7,
-        out_specs=[remote, whole, remote, remote],
+        out_specs=[main, whole, main, main],
         scratch_shapes=[
             pltpu.VMEM((cells, width), F32),
             pltpu.VMEM((peaks, width), F32),
@@ -232,7 +248,12 @@
             pltpu.SemaphoreType.DMA((pieces,)),
             pltpu.SemaphoreType.DMA((2,)),
         ],
-        compiler_params=pltpu.CompilerParams(vmem_limit_bytes=VMEM_BYTES),
+        compiler_params=pltpu.CompilerParams(
+            vmem_limit_bytes=min(
+                56 * MIB,
+                4 * (MIB + peaks * width + width * hid + hid * codes) + cells * (64 * width + 20 * cells),
+            )
+        ),
         cost_estimate=pl.CostEstimate(
             flops=2 * cells * width * (peaks + 3 * hid + 3 * codes),
             bytes_accessed=2 * peaks * cells + 4 * peaks * width + 6 * width * hid + 6 * hid * codes,
@@ -264,14 +285,19 @@
         return lax.ppermute(values, ALL, pairs)
 
     def add(left, right):
-        return (left.astype(F32) + right.astype(F32)).astype(BF16)
-
-    send, held = partial_hidden(carried, counts, tile_mask, neighbours, peak_weight)
+        return lax.optimization_barrier((left.astype(F32) + right.astype(F32)).astype(LINK))
+
+    mask = tile_mask.T
+    send, held = partial_hidden(carried, counts, mask, neighbours, peak_weight)
     held = add(held, exchange(send, (n_peak, n_peak)))
-    turned = turn(counts, tile_mask)
-    for bits in flips(n_grp, n_peak):
+    turned = turn(counts, mask)
+    steps = flips(n_grp, n_peak)
+    for at, bits in enumerate(steps):
         held = add(held, exchange(held, bits))
-    other = exchange(held, (n_peak, n_peak))
+        if at == len(steps) // 2:
+            held, turned = lax.optimization_barrier((held, turned))
+    other = exchange(held, (n_peak, n_peak)).astype(F32)
+    held = held.astype(F32)
     if carried:
         lists = neighbours
     else:

time: 38.5 us -> 31.5 us (0.82); the launches traced: 37.9 us -> 31.2 us
  Pallas kernels: 12.5 us -> 8.29 us
  waiting for transfers between devices: 10.9 us -> 9.54 us
  other arithmetic: 1 us -> 0.16 us
    pallas_call x1, Pallas kernels: 2.54 us -> 0.79 us  [turn(): pl.pallas_call(turn_kernel, out_shape=jax.ShapeDtypeStruct((peaks, cells)...]
    pallas_call x1, Pallas kernels: 6.33 us -> 4.97 us  [tower(): pl.pallas_call(functools.partial(tower_kernel, carried, length_of, pieces...]
    ppermute x6, waiting for transfers between devices: 10.9 us -> 9.54 us  [exchange(): return lax.ppermute(values, ALL, pairs)]
    pallas_call x1, Pallas kernels: 3.59 us -> 2.53 us  [partial_hidden(): pl.pallas_call(functools.partial(partial_kernel, carried, pieces), out_sh...]
    convert_element_type x5 -> x7, other arithmetic: 1 us -> 0.16 us  [the longest x5 0.14 us: add(): (left.astype(F32) + right.astype(F32)).astype(LINK)]
    unnamed x5 -> x12, local copies, waits for them, and re-layouts: 2.04 us -> 1.75 us
  transfers between devices with their start and end apart: 6 -> 6, of which waited for: 5 -> 5; matrix products, arithmetic and copies ran while one was open for 0% -> 0% of each run, Pallas kernels for 7% -> 3%
where the time goes in v2:
time: 31.5 us; the launch traced here: 31.2 us
  starting transfers between devices  10.7 us (34%)
  waiting for transfers between devices  9.54 us (30%)
  Pallas kernels  8.29 us (26%)
  local copies, waits for them, and re-layouts  1.75 us (6%)
  between operations  0.76 us (2%)
    ppermute x6, starting transfers between devices, exchange(): return lax.ppermute(values, ALL, pairs)  10.7 us
    ppermute x6, waiting for transfers between devices, exchange(): return lax.ppermute(values, ALL, pairs)  9.54 us
    pallas_call x1, Pallas kernels, tower(): pl.pallas_call(functools.partial(tower_kernel, carried, length_of, pieces...  4.97 us
    pallas_call x1, Pallas kernels, partial_hidden(): pl.pallas_call(functools.partial(partial_kernel, carried, pieces), out_sh...  2.53 us
    unnamed x12, local copies, waits for them, and re-layouts  1.75 us
    pallas_call x1, Pallas kernels, turn(): pl.pallas_call(turn_kernel, out_shape=jax.ShapeDtypeStruct((peaks, cells)...  0.79 us
  transfers between devices with their start and end apart: 6, of which 5 were waited for; matrix products, arithmetic and copies ran while one was open for 0% of the time, Pallas kernels for 3%

profile of v2, /device:TPU:0, one launch (start us, length us, event | category | flops | bytes accessed | tf_op | source)
XLA Modules:
  0.0 31.2 jit_solution(1386400849436071536)
XLA Ops:
  0.6 0.0 copy-start.2
  0.6 0.0 copy-start.4
  0.7 0.0 copy-start.3
  0.7 0.0 copy-start.5
  0.7 2.5 %shard_map.102 = (f32[80,512]{1,0:T(8,128)S(1)}, f32[80,512]{1,0:T(8,128)S(1)}) custom-call(bf16[128,2048]{1,0:T(8,128)(2,1)} %counts_ref.1, s32[16,128]{1,0:T(8,128)} %bitcast.3, s32[4,15]{1,0:T(4,128)} %lists_ref.1, bf16[2048,512]{1,0:T(8,128)(2,1)} %weight_hbm.1), custom_call_target="tpu_custom_call" | custom-call | flops 268435456 | bytes 2949120 | tf_op jit(solution)/shard_map/pallas_call | solution.py:99
  3.2 0.5 %collective-permute-start = (f32[80,512]{1,0:T(8,128)S(1)}, f32[80,512]{1,0:T(8,128)S(1)}, u32[]{:S(2)}, u32[]{:S(2)}) collective-permute-start(f32[80,512]{1,0:T(8,128)S(1)} %get-tuple-element.13), channel_id=1, source_target_pairs={{0,8},{1,9},{2,10},{3,11},{4,12},{5,13},{6,14},{7,15},{8,0},{9,1},... | collective-permute-start | bytes 491528 | tf_op jit(solution)/shard_map/ppermute | solution.py:285
  3.7 1.0 %collective-permute-done = f32[80,512]{1,0:T(8,128)S(1)} collective-permute-done((f32[80,512]{1,0:T(8,128)S(1)}, f32[80,512]{1,0:T(8,128)S(1)}, u32[]{:S(2)}, u32[]{:S(2)}) %collective-permute-start) | collective-permute-done | bytes 163872 | tf_op jit(solution)/shard_map/ppermute | solution.py:285
  4.8 2.9 %collective-permute-start.1 = (f16[80,512]{1,0:T(8,128)(2,1)S(1)}, f16[80,512]{1,0:T(8,128)(2,1)S(1)}, u32[]{:S(2)}, u32[]{:S(2)}) collective-permute-start(f16[80,512]{1,0:T(8,128)(2,1)S(1)} %add_convert_fusion.4), channel_id=1, source_target_pairs={{0,16},{1,17},{2,18},{3,19},{4,20},{5,21},{6,22},{7,23},{8,10},{9,... | collective-permute-start | bytes 245768 | tf_op jit(solution)/shard_map/ppermute | solution.py:285
  7.7 2.4 %collective-permute-done.1 = f16[80,512]{1,0:T(8,128)(2,1)S(1)} collective-permute-done((f16[80,512]{1,0:T(8,128)(2,1)S(1)}, f16[80,512]{1,0:T(8,128)(2,1)S(1)}, u32[]{:S(2)}, u32[]{:S(2)}) %collective-permute-start.1) | collective-permute-done | bytes 81952 | tf_op jit(solution)/shard_map/ppermute | solution.py:285
  10.2 2.2 %collective-permute-start.2 = (f16[80,512]{1,0:T(8,128)(2,1)S(1)}, f16[80,512]{1,0:T(8,128)(2,1)S(1)}, u32[]{:S(2)}, u32[]{:S(2)}) collective-permute-start(f16[80,512]{1,0:T(8,128)(2,1)S(1)} %add_convert_fusion.3), channel_id=1, source_target_pairs={{0,2},{1,3},{2,0},{3,1},{4,6},{5,7},{6,4},{7,5},{8,24},{9,25},{10,... | collective-permute-start | bytes 245768 | tf_op jit(solution)/shard_map/ppermute | solution.py:285
  12.3 2.4 %collective-permute-done.2 = f16[80,512]{1,0:T(8,128)(2,1)S(1)} collective-permute-done((f16[80,512]{1,0:T(8,128)(2,1)S(1)}, f16[80,512]{1,0:T(8,128)(2,1)S(1)}, u32[]{:S(2)}, u32[]{:S(2)}) %collective-permute-start.2) | collective-permute-done | bytes 81952 | tf_op jit(solution)/shard_map/ppermute | solution.py:285
  14.8 2.0 %collective-permute-start.3 = (f16[80,512]{1,0:T(8,128)(2,1)S(1)}, f16[80,512]{1,0:T(8,128)(2,1)S(1)}, u32[]{:S(2)}, u32[]{:S(2)}) collective-permute-start(f16[80,512]{1,0:T(8,128)(2,1)S(1)} %add_convert_fusion.2), channel_id=1, source_target_pairs={{0,1},{1,0},{2,3},{3,2},{4,5},{5,4},{6,7},{7,6},{8,12},{9,13},{10,... | collective-permute-start | bytes 245768 | tf_op jit(solution)/shard_map/ppermute | solution.py:285
  16.8 0.0 copy-start
  16.8 1.0 %copy-done = bf16[128,2048]{1,0:T(8,128)(2,1)S(1)} copy-done((bf16[128,2048]{1,0:T(8,128)(2,1)S(1)}, bf16[128,2048]{1,0:T(8,128)(2,1)}, u32[]{:S(2)}) %copy-start) | copy-done | bytes 524312
  17.8 0.0 copy-start.1
  17.8 0.7 %copy-done.1 = s32[128,16]{0,1:T(8,128)S(1)} copy-done((s32[128,16]{0,1:T(8,128)S(1)}, s32[128,16]{0,1:T(8,128)}, u32[]{:S(2)}) %copy-start.1) | copy-done | bytes 8216
  18.5 0.8 %shard_map.103.turned_ref = bf16[2048,128]{1,0:T(8,128)(2,1)S(1)} custom-call(bf16[128,2048]{1,0:T(8,128)(2,1)S(1)} %copy-done, s32[16,128]{1,0:T(8,128)S(1)} %bitcast.4), custom_call_target="tpu_custom_call" | custom-call | flops 262144 | bytes 1048576 | tf_op jit(solution)/shard_map/pallas_call | solution.py:137
  19.3 0.0 collective-permute-done.3
  19.4 3.0 %collective-permute-start.4 = (f16[80,512]{1,0:T(8,128)(2,1)S(1)}, f16[80,512]{1,0:T(8,128)(2,1)S(1)}, u32[]{:S(2)}, u32[]{:S(2)}) collective-permute-start(f16[80,512]{1,0:T(8,128)(2,1)S(1)} %add_convert_fusion.1), channel_id=1, source_target_pairs={{0,4},{1,5},{2,6},{3,7},{4,0},{5,1},{6,2},{7,3},{8,9},{9,8},{10,11... | collective-permute-start | bytes 245768 | tf_op jit(solution)/shard_map/ppermute | solution.py:285
  22.4 2.4 %collective-permute-done.4 = f16[80,512]{1,0:T(8,128)(2,1)S(1)} collective-permute-done((f16[80,512]{1,0:T(8,128)(2,1)S(1)}, f16[80,512]{1,0:T(8,128)(2,1)S(1)}, u32[]{:S(2)}, u32[]{:S(2)}) %collective-permute-start.4) | collective-permute-done | bytes 81952 | tf_op jit(solution)/shard_map/ppermute | solution.py:285
  24.9 0.1 collective-permute-start.5
  25.0 1.2 %collective-permute-done.5 = f16[80,512]{1,0:T(8,128)(2,1)S(1)} collective-permute-done((f16[80,512]{1,0:T(8,128)(2,1)S(1)}, f16[80,512]{1,0:T(8,128)(2,1)S(1)}, u32[]{:S(2)}, u32[]{:S(2)}) %collective-permute-start.5) | collective-permute-done | bytes 81952 | tf_op jit(solution)/shard_map/ppermute | solution.py:285
  26.2 0.0 copy-done.2
  26.2 0.0 copy-done.4
  26.2 0.0 copy-done.3
  26.3 0.0 copy-done.5
  26.3 5.0 %shard_map.104 = (f32[2048,512]{1,0:T(8,128)}, f32[1,512]{1,0:T(1,128)}, f32[512,512]{1,0:T(8,128)}, f32[512,256]{1,0:T(8,128)}) custom-call(f32[80,512]{1,0:T(8,128)S(1)} %convert_element_type.58.own_ref, f32[80,512]{1,0:T(8,128)S(1)} %convert_element_type.59.other_ref, s32[4,15]{1,0:T(4,128)S(1)} %copy-done.2, ...), custom_call_target="tpu_custom_call" | custom-call | flops 570425344 | bytes 7077888 | tf_op jit(solution)/shard_map/pallas_call | solution.py:233
  (7 shorter events, 0.2 us)
Async XLA Ops:
  0.6 25.6 %copy-start.2 = (s32[4,15]{1,0:T(4,128)S(1)}, s32[4,15]{1,0:T(4,128)}, u32[]{:S(2)}) copy-start(s32[4,15]{1,0:T(4,128)} %lists_ref.1) | copy-start | bytes 724
  0.6 25.6 %copy-start.4 = (bf16[512,256]{1,0:T(8,128)(2,1)S(1)}, bf16[512,256]{1,0:T(8,128)(2,1)}, u32[]{:S(2)}) copy-start(bf16[512,256]{1,0:T(8,128)(2,1)} %w_out_ref.1) | copy-start | bytes 786436
  0.7 25.6 %copy-start.3 = (bf16[512,512]{1,0:T(8,128)(2,1)S(1)}, bf16[512,512]{1,0:T(8,128)(2,1)}, u32[]{:S(2)}) copy-start(bf16[512,512]{1,0:T(8,128)(2,1)} %w_in_ref.1) | copy-start | bytes 1572868
  0.7 25.6 %copy-start.5 = (f32[512]{0:T(512)S(1)}, f32[512]{0:T(512)}, u32[]{:S(2)}) copy-start(f32[512]{0:T(512)} %param.11) | copy-start | bytes 6148
  3.2 1.5 %collective-permute-start = (f32[80,512]{1,0:T(8,128)S(1)}, f32[80,512]{1,0:T(8,128)S(1)}, u32[]{:S(2)}, u32[]{:S(2)}) collective-permute-start(f32[80,512]{1,0:T(8,128)S(1)} %get-tuple-element.13), channel_id=1, source_target_pairs={{0,8},{1,9},{2,10},{3,11},{4,12},{5,13},{6,14},{7,15},{8,0},{9,1},... | collective-permute-start | bytes 491528 | tf_op jit(solution)/shard_map/ppermute | solution.py:285
  4.8 5.3 %collective-permute-start.1 = (f16[80,512]{1,0:T(8,128)(2,1)S(1)}, f16[80,512]{1,0:T(8,128)(2,1)S(1)}, u32[]{:S(2)}, u32[]{:S(2)}) collective-permute-start(f16[80,512]{1,0:T(8,128)(2,1)S(1)} %add_convert_fusion.4), channel_id=1, source_target_pairs={{0,16},{1,17},{2,18},{3,19},{4,20},{5,21},{6,22},{7,23},{8,10},{9,... | collective-permute-start | bytes 245768 | tf_op jit(solution)/shard_map/ppermute | solution.py:285
  10.2 4.6 %collective-permute-start.2 = (f16[80,512]{1,0:T(8,128)(2,1)S(1)}, f16[80,512]{1,0:T(8,128)(2,1)S(1)}, u32[]{:S(2)}, u32[]{:S(2)}) collective-permute-start(f16[80,512]{1,0:T(8,128)(2,1)S(1)} %add_convert_fusion.3), channel_id=1, source_target_pairs={{0,2},{1,3},{2,0},{3,1},{4,6},{5,7},{6,4},{7,5},{8,24},{9,25},{10,... | collective-permute-start | bytes 245768 | tf_op jit(solution)/shard_map/ppermute | solution.py:285
  14.8 4.6 %collective-permute-start.3 = (f16[80,512]{1,0:T(8,128)(2,1)S(1)}, f16[80,512]{1,0:T(8,128)(2,1)S(1)}, u32[]{:S(2)}, u32[]{:S(2)}) collective-permute-start(f16[80,512]{1,0:T(8,128)(2,1)S(1)} %add_convert_fusion.2), channel_id=1, source_target_pairs={{0,1},{1,0},{2,3},{3,2},{4,5},{5,4},{6,7},{7,6},{8,12},{9,13},{10,... | collective-permute-start | bytes 245768 | tf_op jit(solution)/shard_map/ppermute | solution.py:285
  16.8 1.0 %copy-start = (bf16[128,2048]{1,0:T(8,128)(2,1)S(1)}, bf16[128,2048]{1,0:T(8,128)(2,1)}, u32[]{:S(2)}) copy-start(bf16[128,2048]{1,0:T(8,128)(2,1)} %counts_ref.1) | copy-start | bytes 1572868
  17.8 0.7 %copy-start.1 = (s32[128,16]{0,1:T(8,128)S(1)}, s32[128,16]{0,1:T(8,128)}, u32[]{:S(2)}) copy-start(s32[128,16]{0,1:T(8,128)} %param.8) | copy-start | bytes 24580
  19.4 5.4 %collective-permute-start.4 = (f16[80,512]{1,0:T(8,128)(2,1)S(1)}, f16[80,512]{1,0:T(8,128)(2,1)S(1)}, u32[]{:S(2)}, u32[]{:S(2)}) collective-permute-start(f16[80,512]{1,0:T(8,128)(2,1)S(1)} %add_convert_fusion.1), channel_id=1, source_target_pairs={{0,4},{1,5},{2,6},{3,7},{4,0},{5,1},{6,2},{7,3},{8,9},{9,8},{10,11... | collective-permute-start | bytes 245768 | tf_op jit(solution)/shard_map/ppermute | solution.py:285
  24.9 1.3 %collective-permute-start.5 = (f16[80,512]{1,0:T(8,128)(2,1)S(1)}, f16[80,512]{1,0:T(8,128)(2,1)S(1)}, u32[]{:S(2)}, u32[]{:S(2)}) collective-permute-start(f16[80,512]{1,0:T(8,128)(2,1)S(1)} %add_convert_fusion), channel_id=1, source_target_pairs={{0,8},{1,9},{2,10},{3,11},{4,12},{5,13},{6,14},{7,15},{8,0},{9,1},... | collective-permute-start | bytes 245768 | tf_op jit(solution)/shard_map/ppermute | solution.py:285

commit v3 on v2

--- a/solution.py
+++ b/solution.py
@@ -8,7 +8,7 @@
 from jax.sharding import PartitionSpec as P
 
 TILE = 128
-EXTRA = 16
+EXTRA = 8
 ALL = ("grp", "peak")
 MIB = 1024 * 1024
 F32 = jnp.float32
@@ -28,12 +28,26 @@
     )
 
 
-def core_index():
-    return lax.rem(lax.axis_index("grp"), 2)
+def place():
+    return lax.axis_index("grp") * lax.axis_size("peak") + lax.axis_index("peak")
+
+
+def own_half():
+    position = place()
+    ones = position
+    for bit in range(1, (lax.axis_size("grp") * lax.axis_size("peak")).bit_length()):
+        ones = ones + lax.shift_right_logical(position, bit)
+    return lax.rem(ones, 2)
+
+
+def list_places(length, cells, width):
+    half = -(-length // 2)
+    across = width // cells
+    return [(slot // half, slot % half // across, slot % half % across * cells) for slot in range(length)]
 
 
 def partial_kernel(
-    carried, pieces, counts_hbm, mask_hbm, lists_hbm, weight_hbm, send_ref, keep_ref,
+    carried, pieces, counts_hbm, mask_hbm, lists_hbm, weight_hbm, send_ref, keep_ref, masked_ref,
     counts_ref, mask_ref, lists_ref, weight_ref, total_ref, counts_sem, weight_sem, side_sem,
 ):
     cells, peaks = counts_ref.shape
@@ -58,35 +72,32 @@
             copy.start()
     for copy in sides:
         copy.wait()
-    core = core_index()
+    mine = own_half()
     if carried:
         own, length = lists_ref.shape
-        position = lax.axis_index("grp") * lax.axis_size("peak") + lax.axis_index("peak")
-        columns = lax.broadcasted_iota(jnp.int32, (own, keep_ref.shape[1]), 1)
-        rows = lax.broadcasted_iota(jnp.int32, (own, keep_ref.shape[1]), 0)
-        place = (columns == rows + position * own).astype(F32)
-        lists = dot(lists_ref[...].astype(F32), place, 0, 0)
-        lists = jnp.concatenate([lists, jnp.zeros((2 * EXTRA - length, lists.shape[1]), F32)], axis=0)
-        low, high = lists[:EXTRA], lists[EXTRA:]
-        send_ref[half:, :] = jnp.where(core == 0, high, low)
-        keep_ref[half:, :] = jnp.where(core == 0, low, high)
-    mask = (LIFT * mask_ref[...].astype(F32)).T
+        columns = lax.broadcasted_iota(jnp.int32, (own, cells), 1)
+        rows = lax.broadcasted_iota(jnp.int32, (own, cells), 0)
+        lists = dot(lists_ref[...].astype(F32), (columns == rows + place() * own).astype(F32), 0, 0)
+        send_ref[half:, :] = jnp.zeros((EXTRA, send_ref.shape[1]), F32)
+        keep_ref[half:, :] = jnp.zeros((EXTRA, keep_ref.shape[1]), F32)
+        for slot, (side, row, column) in enumerate(list_places(length, cells, keep_ref.shape[1])):
+            at = (pl.ds(half + row, 1), pl.ds(column, cells))
+            keep_ref[at] = jnp.where(mine == side, lists[slot : slot + 1], keep_ref[at])
+            send_ref[at] = jnp.where(mine == side, send_ref[at], lists[slot : slot + 1])
+    mask = mask_ref[...].astype(F32).T
     for piece in range(pieces):
         for copy in copies(piece):
             copy.wait()
         first = piece * span
-        masked = jnp.concatenate(
-            [
-                counts_ref[:, start : start + TILE]
-                * jnp.broadcast_to(mask[:, start // TILE : start // TILE + 1], (cells, TILE)).astype(BF16)
-                for start in range(first, first + span, TILE)
-            ],
-            axis=1,
-        )
-        term = jnp.dot(masked, weight_ref[first : first + span, :], preferred_element_type=F32)
+        for start in range(first, first + span, TILE):
+            tile = start // TILE
+            column = jnp.broadcast_to(mask[:, tile : tile + 1], (cells, TILE)).astype(BF16)
+            masked_ref[:, start : start + TILE] = counts_ref[:, start : start + TILE] * column
+        at = slice(first, first + span)
+        term = jnp.dot(masked_ref[:, at], weight_ref[at, :], preferred_element_type=F32)
         total_ref[...] = term if piece == 0 else total_ref[...] + term
-    send_ref[:half, :] = total_ref[pl.ds((1 - core) * half, half), :]
-    keep_ref[:half, :] = total_ref[pl.ds(core * half, half), :]
+    send_ref[:half, :] = LIFT * total_ref[pl.ds((1 - mine) * half, half), :]
+    keep_ref[:half, :] = LIFT * total_ref[pl.ds(mine * half, half), :]
 
 
 def partial_hidden(carried, counts, mask, neighbours, peak_weight):
@@ -98,9 +109,9 @@
     rows = cells // 2 + (EXTRA if carried else 0)
     return pl.pallas_call(
         functools.partial(partial_kernel, carried, pieces),
-        out_shape=[pltpu.VMEM((rows, width), F32)] * 2,
+        out_shape=[pltpu.VMEM((rows, width), F32)] * 2 + [pltpu.VMEM((cells, peaks), BF16)],
         in_specs=[main] * 4,
-        out_specs=[whole, whole],
+        out_specs=[whole] * 3,
         scratch_shapes=[
             pltpu.VMEM((cells, peaks), BF16),
             pltpu.VMEM(mask.shape, jnp.int32),
@@ -112,38 +123,34 @@
             pltpu.SemaphoreType.DMA((2,)),
         ],
         compiler_params=pltpu.CompilerParams(
-            vmem_limit_bytes=4 * MIB + 2 * (cells * peaks + peaks * width) + 20 * cells * width
+            vmem_limit_bytes=4 * MIB + 2 * (2 * cells * peaks + peaks * width) + 20 * cells * width
         ),
         cost_estimate=pl.CostEstimate(
             flops=2 * cells * peaks * width,
-            bytes_accessed=2 * (cells * peaks + peaks * width) + 8 * rows * width,
+            bytes_accessed=4 * cells * peaks + 2 * peaks * width + 8 * rows * width,
             transcendentals=0,
         ),
     )(*(pltpu.with_memory_space_constraint(x, pltpu.HBM) for x in (counts, mask, neighbours, peak_weight)))
 
 
-def turn_kernel(counts_ref, mask_ref, turned_ref):
-    cells = counts_ref.shape[0]
-    mask = mask_ref[...].astype(F32).T
-    for start in range(0, counts_ref.shape[1], TILE):
-        tile = start // TILE
-        column = jnp.broadcast_to(mask[:, tile : tile + 1], (cells, TILE)).astype(BF16)
-        turned_ref[start : start + TILE, :] = (counts_ref[:, start : start + TILE] * column).T
-
-
-def turn(counts, mask):
-    cells, peaks = counts.shape
+def turn_kernel(masked_ref, turned_ref):
+    for start in range(0, masked_ref.shape[1], TILE):
+        turned_ref[start : start + TILE, :] = masked_ref[:, start : start + TILE].T
+
+
+def turn(masked):
+    cells, peaks = masked.shape
     whole = pl.BlockSpec(memory_space=pltpu.VMEM)
     return pl.pallas_call(
         turn_kernel,
-        out_shape=jax.ShapeDtypeStruct((peaks, cells), BF16),
-        in_specs=[whole, whole],
+        out_shape=pltpu.VMEM((peaks, cells), BF16),
+        in_specs=[whole],
         out_specs=whole,
-        compiler_params=pltpu.CompilerParams(vmem_limit_bytes=4 * MIB + 8 * cells * peaks),
+        compiler_params=pltpu.CompilerParams(vmem_limit_bytes=4 * MIB + 6 * cells * peaks),
         cost_estimate=pl.CostEstimate(
             flops=cells * peaks, bytes_accessed=4 * cells * peaks, transcendentals=0
         ),
-    )(counts, mask)
+    )(pltpu.with_memory_space_constraint(masked, pltpu.VMEM))
 
 
 def tower_kernel(
@@ -153,16 +160,17 @@
 ):
     cells = hidden_ref.shape[0]
     half = cells // 2
-    core = core_index()
-    hidden_ref[pl.ds(core * half, half), :] = own_ref[:half, :] * (1.0 / LIFT)
-    hidden_ref[pl.ds((1 - core) * half, half), :] = other_ref[:half, :] * (1.0 / LIFT)
-    if carried:
-        own_lists, other_lists = own_ref[half:, :cells], other_ref[half:, :cells]
-        lists = jnp.concatenate(
-            [jnp.where(core == 0, own_lists, other_lists), jnp.where(core == 0, other_lists, own_lists)], axis=0
-        )
-    else:
-        lists = lists_ref[...].astype(F32)
+    mine = own_half()
+    hidden_ref[pl.ds(mine * half, half), :] = own_ref[:half, :] * (1.0 / LIFT)
+    hidden_ref[pl.ds((1 - mine) * half, half), :] = other_ref[:half, :] * (1.0 / LIFT)
+
+    def list_row(slot):
+        if not carried:
+            return lists_ref[slot : slot + 1, :].astype(F32)
+        side, row, column = list_places(length_of, cells, own_ref.shape[1])[slot]
+        at = (pl.ds(half + row, 1), pl.ds(column, cells))
+        return jnp.where(mine == side, own_ref[at], other_ref[at])
+
     gain = gain_ref[...]
     w_in, w_out = w_in_ref[...], w_out_ref[...]
 
@@ -190,7 +198,7 @@
     places = targets.astype(F32)
     tallies = jnp.zeros((cells, cells), F32)
     for slot in range(length_of):
-        tallies = tallies + (lists[slot : slot + 1, :] == places).astype(F32)
+        tallies = tallies + (list_row(slot) == places).astype(F32)
     coupling = (prob - tallies / length_of).astype(BF16)
     dcodes = (dot(coupling, codes, 0, 0) + dot(coupling, codes, 1, 0)) / sharpness_divisor
 
@@ -277,23 +285,25 @@
 def body(n_grp, n_peak, counts, tile_mask, neighbours, peak_weight, gain, w_in, w_out):
     cells = counts.shape[0]
     length_of = neighbours.shape[1]
-    carried = cells <= 256 and cells <= peak_weight.shape[1]
+    carried = cells <= peak_weight.shape[1] and 1 + max(
+        row for _, row, _ in list_places(length_of, cells, peak_weight.shape[1])
+    ) <= EXTRA
     devices = n_grp * n_peak
 
     def exchange(values, bits):
-        pairs = [(i, i ^ bits[(i // n_peak) % 2]) for i in range(devices)]
+        pairs = [(i, i ^ bits[i.bit_count() % 2]) for i in range(devices)]
         return lax.ppermute(values, ALL, pairs)
 
     def add(left, right):
         return lax.optimization_barrier((left.astype(F32) + right.astype(F32)).astype(LINK))
 
     mask = tile_mask.T
-    send, held = partial_hidden(carried, counts, mask, neighbours, peak_weight)
+    send, held, masked = partial_hidden(carried, counts, mask, neighbours, peak_weight)
     held = add(held, exchange(send, (n_peak, n_peak)))
-    turned = turn(counts, mask)
+    turned = turn(masked)
     steps = flips(n_grp, n_peak)
     for at, bits in enumerate(steps):
-        held = add(held, exchange(held, bits))
+        held = add(held, exchange(held, tuple(bit ^ n_peak for bit in bits)))
         if at == len(steps) // 2:
             held, turned = lax.optimization_barrier((held, turned))
     other = exchange(held, (n_peak, n_peak)).astype(F32)

time: 31.5 us -> 29.1 us (0.924)
  local copies, waits for them, and re-layouts: 1.75 us -> 0.02 us
  waiting for transfers between devices: 9.54 us -> 10.2 us
  starting transfers between devices: 10.7 us -> 10.1 us
  Pallas kernels: 8.29 us -> 7.76 us
    unnamed x12 -> x8, local copies, waits for them, and re-layouts: 1.75 us -> 0.02 us
    ppermute x6, starting transfers between devices: 10.7 us -> 10.1 us  [exchange(): return lax.ppermute(values, ALL, pairs)]
    ppermute x6, waiting for transfers between devices: 9.54 us -> 10.2 us  [exchange(): return lax.ppermute(values, ALL, pairs)]
    pallas_call x1, Pallas kernels: 0.79 us -> 0.19 us  [turn(): pl.pallas_call(turn_kernel, out_shape=pltpu.VMEM((peaks, cells), BF16), i...]
  transfers between devices with their start and end apart: 6 -> 6, of which waited for: 5 -> 6; matrix products, arithmetic and copies ran while one was open for 0% -> 0% of each run, Pallas kernels for 3% -> 1%
where the time goes in v3:
time: 29.1 us; the launch traced here: 28.9 us
  waiting for transfers between devices  10.2 us (35%)
  starting transfers between devices  10.1 us (35%)
  Pallas kernels  7.76 us (27%)
  between operations  0.74 us (3%)
    ppermute x6, waiting for transfers between devices, exchange(): return lax.ppermute(values, ALL, pairs)  10.2 us
    ppermute x6, starting transfers between devices, exchange(): return lax.ppermute(values, ALL, pairs)  10.1 us
    pallas_call x1, Pallas kernels, tower(): pl.pallas_call(functools.partial(tower_kernel, carried, length_of, pieces...  4.98 us
    pallas_call x1, Pallas kernels, partial_hidden(): pl.pallas_call(functools.partial(partial_kernel, carried, pieces), out_sh...  2.6 us
  transfers between devices with their start and end apart: 6, of which 6 were waited for; matrix products, arithmetic and copies ran while one was open for 0% of the time, Pallas kernels for 1%

profile of v3, /device:TPU:0, one launch (start us, length us, event | category | flops | bytes accessed | tf_op | source)
XLA Modules:
  0.0 28.9 jit_solution(2163342658164804285)
XLA Ops:
  0.6 0.0 copy-start
  0.6 0.0 copy-start.2
  0.7 0.0 copy-start.1
  0.7 0.0 copy-start.3
  0.7 2.6 %shard_map.102 = (f32[72,512]{1,0:T(8,128)S(1)}, f32[72,512]{1,0:T(8,128)S(1)}, bf16[128,2048]{1,0:T(8,128)(2,1)S(1)}) custom-call(bf16[128,2048]{1,0:T(8,128)(2,1)} %counts_hbm.1, s32[16,128]{1,0:T(8,128)} %bitcast.4, s32[4,15]{1,0:T(4,128)} %lists_ref.1, bf16[2048,512]{1,0:T(8,128)(2,1)} %weight_hbm.1), custom_call_target="tpu_custom_call" | custom-call | flops 268435456 | bytes 3440640 | tf_op jit(solution)/shard_map/pallas_call | solution.py:110
  3.3 0.5 %collective-permute-start = (f32[72,512]{1,0:T(8,128)S(1)}, f32[72,512]{1,0:T(8,128)S(1)}, u32[]{:S(2)}, u32[]{:S(2)}) collective-permute-start(f32[72,512]{1,0:T(8,128)S(1)} %get-tuple-element.14), channel_id=1, source_target_pairs={{0,8},{1,9},{2,10},{3,11},{4,12},{5,13},{6,14},{7,15},{8,0},{9,1},... | collective-permute-start | bytes 442376 | tf_op jit(solution)/shard_map/ppermute | solution.py:295
  3.8 1.0 %collective-permute-done = f32[72,512]{1,0:T(8,128)S(1)} collective-permute-done((f32[72,512]{1,0:T(8,128)S(1)}, f32[72,512]{1,0:T(8,128)S(1)}, u32[]{:S(2)}, u32[]{:S(2)}) %collective-permute-start) | collective-permute-done | bytes 147488 | tf_op jit(solution)/shard_map/ppermute | solution.py:295
  4.8 2.7 %collective-permute-start.1 = (f16[72,512]{1,0:T(8,128)(2,1)S(1)}, f16[72,512]{1,0:T(8,128)(2,1)S(1)}, u32[]{:S(2)}, u32[]{:S(2)}) collective-permute-start(f16[72,512]{1,0:T(8,128)(2,1)S(1)} %add_convert_fusion.4), channel_id=1, source_target_pairs={{0,24},{1,11},{2,8},{3,27},{4,14},{5,29},{6,30},{7,13},{8,2},{9,17... | collective-permute-start | bytes 221192 | tf_op jit(solution)/shard_map/ppermute | solution.py:295
  7.5 2.0 %collective-permute-done.1 = f16[72,512]{1,0:T(8,128)(2,1)S(1)} collective-permute-done((f16[72,512]{1,0:T(8,128)(2,1)S(1)}, f16[72,512]{1,0:T(8,128)(2,1)S(1)}, u32[]{:S(2)}, u32[]{:S(2)}) %collective-permute-start.1) | collective-permute-done | bytes 73760 | tf_op jit(solution)/shard_map/ppermute | solution.py:295
  9.6 1.9 %collective-permute-start.2 = (f16[72,512]{1,0:T(8,128)(2,1)S(1)}, f16[72,512]{1,0:T(8,128)(2,1)S(1)}, u32[]{:S(2)}, u32[]{:S(2)}) collective-permute-start(f16[72,512]{1,0:T(8,128)(2,1)S(1)} %add_convert_fusion.3), channel_id=1, source_target_pairs={{0,10},{1,25},{2,26},{3,9},{4,28},{5,15},{6,12},{7,31},{8,16},{9,3... | collective-permute-start | bytes 221192 | tf_op jit(solution)/shard_map/ppermute | solution.py:295
  11.5 2.0 %collective-permute-done.2 = f16[72,512]{1,0:T(8,128)(2,1)S(1)} collective-permute-done((f16[72,512]{1,0:T(8,128)(2,1)S(1)}, f16[72,512]{1,0:T(8,128)(2,1)S(1)}, u32[]{:S(2)}, u32[]{:S(2)}) %collective-permute-start.2) | collective-permute-done | bytes 73760 | tf_op jit(solution)/shard_map/ppermute | solution.py:295
  13.5 1.8 %collective-permute-start.3 = (f16[72,512]{1,0:T(8,128)(2,1)S(1)}, f16[72,512]{1,0:T(8,128)(2,1)S(1)}, u32[]{:S(2)}, u32[]{:S(2)}) collective-permute-start(f16[72,512]{1,0:T(8,128)(2,1)S(1)} %add_convert_fusion.2), channel_id=1, source_target_pairs={{0,9},{1,13},{2,14},{3,10},{4,8},{5,12},{6,15},{7,11},{8,4},{9,0},... | collective-permute-start | bytes 221192 | tf_op jit(solution)/shard_map/ppermute | solution.py:295
  15.3 0.2 shard_map.103.turned_ref
  15.5 1.9 %collective-permute-done.3 = f16[72,512]{1,0:T(8,128)(2,1)S(1)} collective-permute-done((f16[72,512]{1,0:T(8,128)(2,1)S(1)}, f16[72,512]{1,0:T(8,128)(2,1)S(1)}, u32[]{:S(2)}, u32[]{:S(2)}) %collective-permute-start.3) | collective-permute-done | bytes 73760 | tf_op jit(solution)/shard_map/ppermute | solution.py:295
  17.4 3.1 %collective-permute-start.4 = (f16[72,512]{1,0:T(8,128)(2,1)S(1)}, f16[72,512]{1,0:T(8,128)(2,1)S(1)}, u32[]{:S(2)}, u32[]{:S(2)}) collective-permute-start(f16[72,512]{1,0:T(8,128)(2,1)S(1)} %add_convert_fusion.1), channel_id=1, source_target_pairs={{0,12},{1,8},{2,11},{3,15},{4,13},{5,9},{6,10},{7,14},{8,1},{9,5},... | collective-permute-start | bytes 221192 | tf_op jit(solution)/shard_map/ppermute | solution.py:295
  20.5 2.0 %collective-permute-done.4 = f16[72,512]{1,0:T(8,128)(2,1)S(1)} collective-permute-done((f16[72,512]{1,0:T(8,128)(2,1)S(1)}, f16[72,512]{1,0:T(8,128)(2,1)S(1)}, u32[]{:S(2)}, u32[]{:S(2)}) %collective-permute-start.4) | collective-permute-done | bytes 73760 | tf_op jit(solution)/shard_map/ppermute | solution.py:295
  22.6 0.2 collective-permute-start.5
  22.8 1.1 %collective-permute-done.5 = f16[72,512]{1,0:T(8,128)(2,1)S(1)} collective-permute-done((f16[72,512]{1,0:T(8,128)(2,1)S(1)}, f16[72,512]{1,0:T(8,128)(2,1)S(1)}, u32[]{:S(2)}, u32[]{:S(2)}) %collective-permute-start.5) | collective-permute-done | bytes 73760 | tf_op jit(solution)/shard_map/ppermute | solution.py:295
  23.9 0.0 copy-done
  23.9 0.0 copy-done.2
  23.9 0.0 copy-done.1
  24.0 0.0 copy-done.3
  24.0 5.0 %shard_map.104 = (f32[2048,512]{1,0:T(8,128)}, f32[1,512]{1,0:T(1,128)}, f32[512,512]{1,0:T(8,128)}, f32[512,256]{1,0:T(8,128)}) custom-call(f32[72,512]{1,0:T(8,128)S(1)} %convert_element_type.58.own_ref, f32[72,512]{1,0:T(8,128)S(1)} %convert_element_type.59.other_ref, s32[4,15]{1,0:T(4,128)S(1)} %copy-done, bf16[2048,128]{1,0:T(8,128)(2,1)S(1)} %shard_map.103.turned_ref, ...), custom_call_target="tpu_custom_call" | custom-call | flops 570425344 | bytes 7077888 | tf_op jit(solution)/shard_map/pallas_call | solution.py:241
  (7 shorter events, 0.2 us)
Async XLA Ops:
  0.6 23.3 %copy-start = (s32[4,15]{1,0:T(4,128)S(1)}, s32[4,15]{1,0:T(4,128)}, u32[]{:S(2)}) copy-start(s32[4,15]{1,0:T(4,128)} %lists_ref.1) | copy-start | bytes 724
  0.6 23.3 %copy-start.2 = (bf16[512,256]{1,0:T(8,128)(2,1)S(1)}, bf16[512,256]{1,0:T(8,128)(2,1)}, u32[]{:S(2)}) copy-start(bf16[512,256]{1,0:T(8,128)(2,1)} %w_out_ref.1) | copy-start | bytes 786436
  0.7 23.3 %copy-start.1 = (bf16[512,512]{1,0:T(8,128)(2,1)S(1)}, bf16[512,512]{1,0:T(8,128)(2,1)}, u32[]{:S(2)}) copy-start(bf16[512,512]{1,0:T(8,128)(2,1)} %w_in_ref.1) | copy-start | bytes 1572868
  0.7 23.3 %copy-start.3 = (f32[512]{0:T(512)S(1)}, f32[512]{0:T(512)}, u32[]{:S(2)}) copy-start(f32[512]{0:T(512)} %param.11) | copy-start | bytes 6148
  3.3 1.5 %collective-permute-start = (f32[72,512]{1,0:T(8,128)S(1)}, f32[72,512]{1,0:T(8,128)S(1)}, u32[]{:S(2)}, u32[]{:S(2)}) collective-permute-start(f32[72,512]{1,0:T(8,128)S(1)} %get-tuple-element.14), channel_id=1, source_target_pairs={{0,8},{1,9},{2,10},{3,11},{4,12},{5,13},{6,14},{7,15},{8,0},{9,1},... | collective-permute-start | bytes 442376 | tf_op jit(solution)/shard_map/ppermute | solution.py:295
  4.8 4.7 %collective-permute-start.1 = (f16[72,512]{1,0:T(8,128)(2,1)S(1)}, f16[72,512]{1,0:T(8,128)(2,1)S(1)}, u32[]{:S(2)}, u32[]{:S(2)}) collective-permute-start(f16[72,512]{1,0:T(8,128)(2,1)S(1)} %add_convert_fusion.4), channel_id=1, source_target_pairs={{0,24},{1,11},{2,8},{3,27},{4,14},{5,29},{6,30},{7,13},{8,2},{9,17... | collective-permute-start | bytes 221192 | tf_op jit(solution)/shard_map/ppermute | solution.py:295
  9.6 3.9 %collective-permute-start.2 = (f16[72,512]{1,0:T(8,128)(2,1)S(1)}, f16[72,512]{1,0:T(8,128)(2,1)S(1)}, u32[]{:S(2)}, u32[]{:S(2)}) collective-permute-start(f16[72,512]{1,0:T(8,128)(2,1)S(1)} %add_convert_fusion.3), channel_id=1, source_target_pairs={{0,10},{1,25},{2,26},{3,9},{4,28},{5,15},{6,12},{7,31},{8,16},{9,3... | collective-permute-start | bytes 221192 | tf_op jit(solution)/shard_map/ppermute | solution.py:295
  13.5 3.8 %collective-permute-start.3 = (f16[72,512]{1,0:T(8,128)(2,1)S(1)}, f16[72,512]{1,0:T(8,128)(2,1)S(1)}, u32[]{:S(2)}, u32[]{:S(2)}) collective-permute-start(f16[72,512]{1,0:T(8,128)(2,1)S(1)} %add_convert_fusion.2), channel_id=1, source_target_pairs={{0,9},{1,13},{2,14},{3,10},{4,8},{5,12},{6,15},{7,11},{8,4},{9,0},... | collective-permute-start | bytes 221192 | tf_op jit(solution)/shard_map/ppermute | solution.py:295
  17.4 5.1 %collective-permute-start.4 = (f16[72,512]{1,0:T(8,128)(2,1)S(1)}, f16[72,512]{1,0:T(8,128)(2,1)S(1)}, u32[]{:S(2)}, u32[]{:S(2)}) collective-permute-start(f16[72,512]{1,0:T(8,128)(2,1)S(1)} %add_convert_fusion.1), channel_id=1, source_target_pairs={{0,12},{1,8},{2,11},{3,15},{4,13},{5,9},{6,10},{7,14},{8,1},{9,5},... | collective-permute-start | bytes 221192 | tf_op jit(solution)/shard_map/ppermute | solution.py:295
  22.6 1.3 %collective-permute-start.5 = (f16[72,512]{1,0:T(8,128)(2,1)S(1)}, f16[72,512]{1,0:T(8,128)(2,1)S(1)}, u32[]{:S(2)}, u32[]{:S(2)}) collective-permute-start(f16[72,512]{1,0:T(8,128)(2,1)S(1)} %add_convert_fusion), channel_id=1, source_target_pairs={{0,8},{1,9},{2,10},{3,11},{4,12},{5,13},{6,14},{7,15},{8,0},{9,1},... | collective-permute-start | bytes 221192 | tf_op jit(solution)/shard_map/ppermute | solution.py:295

commit v4 on v3

--- a/solution.py
+++ b/solution.py
@@ -155,11 +155,14 @@
 
 def tower_kernel(
     carried, length_of, pieces, own_ref, other_ref, lists_ref, turned_ref, gain_ref, w_in_ref, w_out_ref,
-    peak_grad_hbm, gain_grad_ref, in_grad_hbm, out_grad_hbm,
-    hidden_ref, peak_grad_ref, in_grad_ref, out_grad_ref, peak_sem, side_sem,
+    peak_grad_hbm, gain_grad_hbm, in_grad_hbm, out_grad_hbm,
+    hidden_ref, peak_grad_ref, gain_grad_ref, in_grad_ref, out_grad_ref, peak_sem, side_sem,
 ):
     cells = hidden_ref.shape[0]
     half = cells // 2
+    gain_copy = pltpu.make_async_copy(gain_grad_ref, gain_grad_hbm, side_sem.at[0])
+    in_copy = pltpu.make_async_copy(in_grad_ref, in_grad_hbm, side_sem.at[1])
+    out_copy = pltpu.make_async_copy(out_grad_ref, out_grad_hbm, side_sem.at[2])
     mine = own_half()
     hidden_ref[pl.ds(mine * half, half), :] = own_ref[:half, :] * (1.0 / LIFT)
     hidden_ref[pl.ds((1 - mine) * half, half), :] = other_ref[:half, :] * (1.0 / LIFT)
@@ -204,8 +207,13 @@
 
     dproj = (length * (dcodes - unit * jnp.sum(unit * dcodes, axis=1, keepdims=True))).astype(BF16)
     dpre = (dot(dproj, w_out, 1, 1) * slope).astype(BF16)
+    out_grad_ref[...] = dot(activ, dproj, 0, 0)
+    out_copy.start()
     dround = dot(dpre, w_in, 1, 1)
+    in_grad_ref[...] = dot(rounded, dpre, 0, 0)
+    in_copy.start()
     gain_grad_ref[...] = jnp.sum(dround * normed, axis=0, keepdims=True)
+    gain_copy.start()
     dnorm = dround * gain
     dhidden = (scale * (dnorm - normed * jnp.mean(dnorm * normed, axis=1, keepdims=True))).astype(BF16)
 
@@ -215,18 +223,17 @@
         at = pl.ds(piece * span, span)
         return pltpu.make_async_copy(peak_grad_ref.at[at, :], peak_grad_hbm.at[at, :], peak_sem.at[piece])
 
-    for piece in range(pieces):
-        at = pl.ds(piece * span, span)
-        peak_grad_ref[at, :] = jnp.dot(turned_ref[at, :], dhidden, preferred_element_type=F32)
-        peak_copy(piece).start()
-    in_copy = pltpu.make_async_copy(in_grad_ref, in_grad_hbm, side_sem.at[0])
-    out_copy = pltpu.make_async_copy(out_grad_ref, out_grad_hbm, side_sem.at[1])
-    in_grad_ref[...] = dot(rounded, dpre, 0, 0)
-    in_copy.start()
-    out_grad_ref[...] = dot(activ, dproj, 0, 0)
-    out_copy.start()
+    @pl.loop(0, 2)
+    def _(part):
+        for inner in range(pieces // 2):
+            piece = part * (pieces // 2) + inner
+            at = pl.ds(pl.multiple_of(piece * span, span), span)
+            peak_grad_ref[at, :] = jnp.dot(turned_ref[at, :], dhidden, preferred_element_type=F32)
+            peak_copy(piece).start()
+
     for piece in range(pieces):
         peak_copy(piece).wait()
+    gain_copy.wait()
     in_copy.wait()
     out_copy.wait()
 
@@ -235,7 +242,7 @@
     peaks, cells = turned.shape
     width, hid = w_in.shape
     codes = w_out.shape[1]
-    pieces = 8
+    pieces = 4
     whole = pl.BlockSpec(memory_space=pltpu.VMEM)
     main = pl.BlockSpec(memory_space=pltpu.HBM)
     return pl.pallas_call(
@@ -247,14 +254,15 @@
             jax.ShapeDtypeStruct((hid, codes), F32),
         ],
         in_specs=[whole] * 7,
-        out_specs=[main, whole, main, main],
+        out_specs=[main] * 4,
         scratch_shapes=[
             pltpu.VMEM((cells, width), F32),
             pltpu.VMEM((peaks, width), F32),
+            pltpu.VMEM((1, width), F32),
             pltpu.VMEM((width, hid), F32),
             pltpu.VMEM((hid, codes), F32),
             pltpu.SemaphoreType.DMA((pieces,)),
-            pltpu.SemaphoreType.DMA((2,)),
+            pltpu.SemaphoreType.DMA((3,)),
         ],
         compiler_params=pltpu.CompilerParams(
             vmem_limit_bytes=min(

time: 29.1 us -> 28.1 us (0.966)
  Pallas kernels: 7.76 us -> 6.81 us
    pallas_call x1, Pallas kernels: 4.98 us -> 4.03 us  [tower(): pl.pallas_call(functools.partial(tower_kernel, carried, length_of, pieces...]
where the time goes in v4:
time: 28.1 us; the launch traced here: 28 us
  waiting for transfers between devices  10.2 us (36%)
  starting transfers between devices  10.1 us (36%)
  Pallas kernels  6.81 us (24%)
  between operations  0.74 us (3%)
    ppermute x6, waiting for transfers between devices, exchange(): return lax.ppermute(values, ALL, pairs)  10.2 us
    ppermute x6, starting transfers between devices, exchange(): return lax.ppermute(values, ALL, pairs)  10.1 us
    pallas_call x1, Pallas kernels, tower(): pl.pallas_call(functools.partial(tower_kernel, carried, length_of, pieces...  4.03 us
    pallas_call x1, Pallas kernels, partial_hidden(): pl.pallas_call(functools.partial(partial_kernel, carried, pieces), out_sh...  2.6 us
  transfers between devices with their start and end apart: 6, of which 6 were waited for; matrix products, arithmetic and copies ran while one was open for 0% of the time, Pallas kernels for 1%

profile of v4, /device:TPU:0, one launch (start us, length us, event | category | flops | bytes accessed | tf_op | source)
XLA Modules:
  0.0 28.0 jit_solution(8741027914327696392)
XLA Ops:
  0.6 0.0 copy-start
  0.6 0.0 copy-start.2
  0.7 0.0 copy-start.1
  0.7 0.0 copy-start.3
  0.7 2.6 %shard_map.102 = (f32[72,512]{1,0:T(8,128)S(1)}, f32[72,512]{1,0:T(8,128)S(1)}, bf16[128,2048]{1,0:T(8,128)(2,1)S(1)}) custom-call(bf16[128,2048]{1,0:T(8,128)(2,1)} %counts_hbm.1, s32[16,128]{1,0:T(8,128)} %bitcast.4, s32[4,15]{1,0:T(4,128)} %lists_ref.1, bf16[2048,512]{1,0:T(8,128)(2,1)} %weight_hbm.1), custom_call_target="tpu_custom_call" | custom-call | flops 268435456 | bytes 3440640 | tf_op jit(solution)/shard_map/pallas_call | solution.py:110
  3.3 0.5 %collective-permute-start = (f32[72,512]{1,0:T(8,128)S(1)}, f32[72,512]{1,0:T(8,128)S(1)}, u32[]{:S(2)}, u32[]{:S(2)}) collective-permute-start(f32[72,512]{1,0:T(8,128)S(1)} %get-tuple-element.14), channel_id=1, source_target_pairs={{0,8},{1,9},{2,10},{3,11},{4,12},{5,13},{6,14},{7,15},{8,0},{9,1},... | collective-permute-start | bytes 442376 | tf_op jit(solution)/shard_map/ppermute | solution.py:303
  3.8 1.0 %collective-permute-done = f32[72,512]{1,0:T(8,128)S(1)} collective-permute-done((f32[72,512]{1,0:T(8,128)S(1)}, f32[72,512]{1,0:T(8,128)S(1)}, u32[]{:S(2)}, u32[]{:S(2)}) %collective-permute-start) | collective-permute-done | bytes 147488 | tf_op jit(solution)/shard_map/ppermute | solution.py:303
  4.8 2.7 %collective-permute-start.1 = (f16[72,512]{1,0:T(8,128)(2,1)S(1)}, f16[72,512]{1,0:T(8,128)(2,1)S(1)}, u32[]{:S(2)}, u32[]{:S(2)}) collective-permute-start(f16[72,512]{1,0:T(8,128)(2,1)S(1)} %add_convert_fusion.4), channel_id=1, source_target_pairs={{0,24},{1,11},{2,8},{3,27},{4,14},{5,29},{6,30},{7,13},{8,2},{9,17... | collective-permute-start | bytes 221192 | tf_op jit(solution)/shard_map/ppermute | solution.py:303
  7.5 2.0 %collective-permute-done.1 = f16[72,512]{1,0:T(8,128)(2,1)S(1)} collective-permute-done((f16[72,512]{1,0:T(8,128)(2,1)S(1)}, f16[72,512]{1,0:T(8,128)(2,1)S(1)}, u32[]{:S(2)}, u32[]{:S(2)}) %collective-permute-start.1) | collective-permute-done | bytes 73760 | tf_op jit(solution)/shard_map/ppermute | solution.py:303
  9.6 1.9 %collective-permute-start.2 = (f16[72,512]{1,0:T(8,128)(2,1)S(1)}, f16[72,512]{1,0:T(8,128)(2,1)S(1)}, u32[]{:S(2)}, u32[]{:S(2)}) collective-permute-start(f16[72,512]{1,0:T(8,128)(2,1)S(1)} %add_convert_fusion.3), channel_id=1, source_target_pairs={{0,10},{1,25},{2,26},{3,9},{4,28},{5,15},{6,12},{7,31},{8,16},{9,3... | collective-permute-start | bytes 221192 | tf_op jit(solution)/shard_map/ppermute | solution.py:303
  11.5 2.0 %collective-permute-done.2 = f16[72,512]{1,0:T(8,128)(2,1)S(1)} collective-permute-done((f16[72,512]{1,0:T(8,128)(2,1)S(1)}, f16[72,512]{1,0:T(8,128)(2,1)S(1)}, u32[]{:S(2)}, u32[]{:S(2)}) %collective-permute-start.2) | collective-permute-done | bytes 73760 | tf_op jit(solution)/shard_map/ppermute | solution.py:303
  13.5 1.8 %collective-permute-start.3 = (f16[72,512]{1,0:T(8,128)(2,1)S(1)}, f16[72,512]{1,0:T(8,128)(2,1)S(1)}, u32[]{:S(2)}, u32[]{:S(2)}) collective-permute-start(f16[72,512]{1,0:T(8,128)(2,1)S(1)} %add_convert_fusion.2), channel_id=1, source_target_pairs={{0,9},{1,13},{2,14},{3,10},{4,8},{5,12},{6,15},{7,11},{8,4},{9,0},... | collective-permute-start | bytes 221192 | tf_op jit(solution)/shard_map/ppermute | solution.py:303
  15.3 0.2 shard_map.103.turned_ref
  15.5 1.9 %collective-permute-done.3 = f16[72,512]{1,0:T(8,128)(2,1)S(1)} collective-permute-done((f16[72,512]{1,0:T(8,128)(2,1)S(1)}, f16[72,512]{1,0:T(8,128)(2,1)S(1)}, u32[]{:S(2)}, u32[]{:S(2)}) %collective-permute-start.3) | collective-permute-done | bytes 73760 | tf_op jit(solution)/shard_map/ppermute | solution.py:303
  17.4 3.1 %collective-permute-start.4 = (f16[72,512]{1,0:T(8,128)(2,1)S(1)}, f16[72,512]{1,0:T(8,128)(2,1)S(1)}, u32[]{:S(2)}, u32[]{:S(2)}) collective-permute-start(f16[72,512]{1,0:T(8,128)(2,1)S(1)} %add_convert_fusion.1), channel_id=1, source_target_pairs={{0,12},{1,8},{2,11},{3,15},{4,13},{5,9},{6,10},{7,14},{8,1},{9,5},... | collective-permute-start | bytes 221192 | tf_op jit(solution)/shard_map/ppermute | solution.py:303
  20.5 2.0 %collective-permute-done.4 = f16[72,512]{1,0:T(8,128)(2,1)S(1)} collective-permute-done((f16[72,512]{1,0:T(8,128)(2,1)S(1)}, f16[72,512]{1,0:T(8,128)(2,1)S(1)}, u32[]{:S(2)}, u32[]{:S(2)}) %collective-permute-start.4) | collective-permute-done | bytes 73760 | tf_op jit(solution)/shard_map/ppermute | solution.py:303
  22.6 0.2 collective-permute-start.5
  22.8 1.1 %collective-permute-done.5 = f16[72,512]{1,0:T(8,128)(2,1)S(1)} collective-permute-done((f16[72,512]{1,0:T(8,128)(2,1)S(1)}, f16[72,512]{1,0:T(8,128)(2,1)S(1)}, u32[]{:S(2)}, u32[]{:S(2)}) %collective-permute-start.5) | collective-permute-done | bytes 73760 | tf_op jit(solution)/shard_map/ppermute | solution.py:303
  23.9 0.0 copy-done
  23.9 0.0 copy-done.2
  23.9 0.0 copy-done.1
  24.0 0.0 copy-done.3
  24.0 4.0 %shard_map.104 = (f32[2048,512]{1,0:T(8,128)}, f32[1,512]{1,0:T(1,128)}, f32[512,512]{1,0:T(8,128)}, f32[512,256]{1,0:T(8,128)}) custom-call(f32[72,512]{1,0:T(8,128)S(1)} %convert_element_type.58.own_ref, f32[72,512]{1,0:T(8,128)S(1)} %convert_element_type.59.other_ref, s32[4,15]{1,0:T(4,128)S(1)} %copy-done, bf16[2048,128]{1,0:T(8,128)(2,1)S(1)} %shard_map.103.turned_ref, ...), custom_call_target="tpu_custom_call" | custom-call | flops 570425344 | bytes 7077888 | tf_op jit(solution)/shard_map/pallas_call | solution.py:248
  (7 shorter events, 0.2 us)
Async XLA Ops:
  0.6 23.3 %copy-start = (s32[4,15]{1,0:T(4,128)S(1)}, s32[4,15]{1,0:T(4,128)}, u32[]{:S(2)}) copy-start(s32[4,15]{1,0:T(4,128)} %lists_ref.1) | copy-start | bytes 724
  0.6 23.3 %copy-start.2 = (bf16[512,256]{1,0:T(8,128)(2,1)S(1)}, bf16[512,256]{1,0:T(8,128)(2,1)}, u32[]{:S(2)}) copy-start(bf16[512,256]{1,0:T(8,128)(2,1)} %w_out_ref.1) | copy-start | bytes 786436
  0.7 23.3 %copy-start.1 = (bf16[512,512]{1,0:T(8,128)(2,1)S(1)}, bf16[512,512]{1,0:T(8,128)(2,1)}, u32[]{:S(2)}) copy-start(bf16[512,512]{1,0:T(8,128)(2,1)} %w_in_ref.1) | copy-start | bytes 1572868
  0.7 23.3 %copy-start.3 = (f32[512]{0:T(512)S(1)}, f32[512]{0:T(512)}, u32[]{:S(2)}) copy-start(f32[512]{0:T(512)} %param.11) | copy-start | bytes 6148
  3.3 1.5 %collective-permute-start = (f32[72,512]{1,0:T(8,128)S(1)}, f32[72,512]{1,0:T(8,128)S(1)}, u32[]{:S(2)}, u32[]{:S(2)}) collective-permute-start(f32[72,512]{1,0:T(8,128)S(1)} %get-tuple-element.14), channel_id=1, source_target_pairs={{0,8},{1,9},{2,10},{3,11},{4,12},{5,13},{6,14},{7,15},{8,0},{9,1},... | collective-permute-start | bytes 442376 | tf_op jit(solution)/shard_map/ppermute | solution.py:303
  4.8 4.7 %collective-permute-start.1 = (f16[72,512]{1,0:T(8,128)(2,1)S(1)}, f16[72,512]{1,0:T(8,128)(2,1)S(1)}, u32[]{:S(2)}, u32[]{:S(2)}) collective-permute-start(f16[72,512]{1,0:T(8,128)(2,1)S(1)} %add_convert_fusion.4), channel_id=1, source_target_pairs={{0,24},{1,11},{2,8},{3,27},{4,14},{5,29},{6,30},{7,13},{8,2},{9,17... | collective-permute-start | bytes 221192 | tf_op jit(solution)/shard_map/ppermute | solution.py:303
  9.6 3.9 %collective-permute-start.2 = (f16[72,512]{1,0:T(8,128)(2,1)S(1)}, f16[72,512]{1,0:T(8,128)(2,1)S(1)}, u32[]{:S(2)}, u32[]{:S(2)}) collective-permute-start(f16[72,512]{1,0:T(8,128)(2,1)S(1)} %add_convert_fusion.3), channel_id=1, source_target_pairs={{0,10},{1,25},{2,26},{3,9},{4,28},{5,15},{6,12},{7,31},{8,16},{9,3... | collective-permute-start | bytes 221192 | tf_op jit(solution)/shard_map/ppermute | solution.py:303
  13.5 3.8 %collective-permute-start.3 = (f16[72,512]{1,0:T(8,128)(2,1)S(1)}, f16[72,512]{1,0:T(8,128)(2,1)S(1)}, u32[]{:S(2)}, u32[]{:S(2)}) collective-permute-start(f16[72,512]{1,0:T(8,128)(2,1)S(1)} %add_convert_fusion.2), channel_id=1, source_target_pairs={{0,9},{1,13},{2,14},{3,10},{4,8},{5,12},{6,15},{7,11},{8,4},{9,0},... | collective-permute-start | bytes 221192 | tf_op jit(solution)/shard_map/ppermute | solution.py:303
  17.4 5.1 %collective-permute-start.4 = (f16[72,512]{1,0:T(8,128)(2,1)S(1)}, f16[72,512]{1,0:T(8,128)(2,1)S(1)}, u32[]{:S(2)}, u32[]{:S(2)}) collective-permute-start(f16[72,512]{1,0:T(8,128)(2,1)S(1)} %add_convert_fusion.1), channel_id=1, source_target_pairs={{0,12},{1,8},{2,11},{3,15},{4,13},{5,9},{6,10},{7,14},{8,1},{9,5},... | collective-permute-start | bytes 221192 | tf_op jit(solution)/shard_map/ppermute | solution.py:303
  22.6 1.3 %collective-permute-start.5 = (f16[72,512]{1,0:T(8,128)(2,1)S(1)}, f16[72,512]{1,0:T(8,128)(2,1)S(1)}, u32[]{:S(2)}, u32[]{:S(2)}) collective-permute-start(f16[72,512]{1,0:T(8,128)(2,1)S(1)} %add_convert_fusion), channel_id=1, source_target_pairs={{0,8},{1,9},{2,10},{3,11},{4,12},{5,13},{6,14},{7,15},{8,0},{9,1},... | collective-permute-start | bytes 221192 | tf_op jit(solution)/shard_map/ppermute | solution.py:303

commit v5 on v4

--- a/solution.py
+++ b/solution.py
@@ -8,7 +8,7 @@
 from jax.sharding import PartitionSpec as P
 
 TILE = 128
-EXTRA = 8
+SLOTS = 8
 ALL = ("grp", "peak")
 MIB = 1024 * 1024
 F32 = jnp.float32
@@ -40,10 +40,13 @@
     return lax.rem(ones, 2)
 
 
-def list_places(length, cells, width):
-    half = -(-length // 2)
-    across = width // cells
-    return [(slot // half, slot % half // across, slot % half % across * cells) for slot in range(length)]
+def tiles_of(rows, columns):
+    return rows // 8 * (columns // TILE)
+
+
+def to_tiles(values):
+    rows, columns = values.shape
+    return [values[:, start : start + TILE].reshape(rows // 8, 8, TILE) for start in range(0, columns, TILE)]
 
 
 def partial_kernel(
@@ -78,12 +81,12 @@
         columns = lax.broadcasted_iota(jnp.int32, (own, cells), 1)
         rows = lax.broadcasted_iota(jnp.int32, (own, cells), 0)
         lists = dot(lists_ref[...].astype(F32), (columns == rows + place() * own).astype(F32), 0, 0)
-        send_ref[half:, :] = jnp.zeros((EXTRA, send_ref.shape[1]), F32)
-        keep_ref[half:, :] = jnp.zeros((EXTRA, keep_ref.shape[1]), F32)
-        for slot, (side, row, column) in enumerate(list_places(length, cells, keep_ref.shape[1])):
-            at = (pl.ds(half + row, 1), pl.ds(column, cells))
-            keep_ref[at] = jnp.where(mine == side, lists[slot : slot + 1], keep_ref[at])
-            send_ref[at] = jnp.where(mine == side, send_ref[at], lists[slot : slot + 1])
+        lists = jnp.concatenate([lists, jnp.zeros((2 * SLOTS - length, cells), F32)], axis=0)
+        low, high = lists[:SLOTS], lists[SLOTS:]
+        first = tiles_of(half, total_ref.shape[1])
+        for at, (low_tile, high_tile) in enumerate(zip(to_tiles(low), to_tiles(high), strict=True), first):
+            keep_ref[at : at + 1] = jnp.where(mine == 0, low_tile, high_tile)
+            send_ref[at : at + 1] = jnp.where(mine == 0, high_tile, low_tile)
     mask = mask_ref[...].astype(F32).T
     for piece in range(pieces):
         for copy in copies(piece):
@@ -96,20 +99,21 @@
         at = slice(first, first + span)
         term = jnp.dot(masked_ref[:, at], weight_ref[at, :], preferred_element_type=F32)
         total_ref[...] = term if piece == 0 else total_ref[...] + term
-    send_ref[:half, :] = LIFT * total_ref[pl.ds((1 - mine) * half, half), :]
-    keep_ref[:half, :] = LIFT * total_ref[pl.ds(mine * half, half), :]
+    for ref, side in ((send_ref, 1 - mine), (keep_ref, mine)):
+        for at, tiles in enumerate(to_tiles(LIFT * total_ref[pl.ds(side * half, half), :])):
+            ref[at * (half // 8) : (at + 1) * (half // 8)] = tiles
 
 
 def partial_hidden(carried, counts, mask, neighbours, peak_weight):
     cells, peaks = counts.shape
     width = peak_weight.shape[1]
-    pieces = 4
+    pieces = 2
     whole = pl.BlockSpec(memory_space=pltpu.VMEM)
     main = pl.BlockSpec(memory_space=pltpu.HBM)
-    rows = cells // 2 + (EXTRA if carried else 0)
+    tiles = tiles_of(cells // 2, width) + (tiles_of(SLOTS, cells) if carried else 0)
     return pl.pallas_call(
         functools.partial(partial_kernel, carried, pieces),
-        out_shape=[pltpu.VMEM((rows, width), F32)] * 2 + [pltpu.VMEM((cells, peaks), BF16)],
+        out_shape=[pltpu.VMEM((tiles, 8, TILE), F32)] * 2 + [pltpu.VMEM((cells, peaks), BF16)],
         in_specs=[main] * 4,
         out_specs=[whole] * 3,
         scratch_shapes=[
@@ -127,7 +131,7 @@
         ),
         cost_estimate=pl.CostEstimate(
             flops=2 * cells * peaks * width,
-            bytes_accessed=4 * cells * peaks + 2 * peaks * width + 8 * rows * width,
+            bytes_accessed=4 * cells * peaks + 2 * peaks * width + 64 * tiles * TILE,
             transcendentals=0,
         ),
     )(*(pltpu.with_memory_space_constraint(x, pltpu.HBM) for x in (counts, mask, neighbours, peak_weight)))
@@ -164,16 +168,18 @@
     in_copy = pltpu.make_async_copy(in_grad_ref, in_grad_hbm, side_sem.at[1])
     out_copy = pltpu.make_async_copy(out_grad_ref, out_grad_hbm, side_sem.at[2])
     mine = own_half()
-    hidden_ref[pl.ds(mine * half, half), :] = own_ref[:half, :] * (1.0 / LIFT)
-    hidden_ref[pl.ds((1 - mine) * half, half), :] = other_ref[:half, :] * (1.0 / LIFT)
-
-    def list_row(slot):
-        if not carried:
-            return lists_ref[slot : slot + 1, :].astype(F32)
-        side, row, column = list_places(length_of, cells, own_ref.shape[1])[slot]
-        at = (pl.ds(half + row, 1), pl.ds(column, cells))
-        return jnp.where(mine == side, own_ref[at], other_ref[at])
-
+    for ref, side in ((own_ref, mine), (other_ref, 1 - mine)):
+        for at in range(hidden_ref.shape[1] // TILE):
+            tiles = ref[at * (half // 8) : (at + 1) * (half // 8)]
+            hidden_ref[pl.ds(side * half, half), at * TILE : (at + 1) * TILE] = tiles.reshape(half, TILE) * (1.0 / LIFT)
+    if carried:
+        first = tiles_of(half, hidden_ref.shape[1])
+        pairs = [(own_ref[at], other_ref[at]) for at in range(first, own_ref.shape[0])]
+        low = [jnp.where(mine == 0, own, other) for own, other in pairs]
+        high = [jnp.where(mine == 0, other, own) for own, other in pairs]
+        lists = jnp.concatenate([jnp.concatenate(low, axis=1), jnp.concatenate(high, axis=1)], axis=0)
+    else:
+        lists = lists_ref[...].astype(F32)
     gain = gain_ref[...]
     w_in, w_out = w_in_ref[...], w_out_ref[...]
 
@@ -201,7 +207,7 @@
     places = targets.astype(F32)
     tallies = jnp.zeros((cells, cells), F32)
     for slot in range(length_of):
-        tallies = tallies + (list_row(slot) == places).astype(F32)
+        tallies = tallies + (lists[slot : slot + 1] == places).astype(F32)
     coupling = (prob - tallies / length_of).astype(BF16)
     dcodes = (dot(coupling, codes, 0, 0) + dot(coupling, codes, 1, 0)) / sharpness_divisor
 
@@ -283,7 +289,7 @@
     peak_bits = [bit for bit in (1, 2, 4, 8, 16, 32, 64) if bit < n_peak]
     order = grp_bits + peak_bits
     if len(order) == 4:
-        order = [order[0], order[2], order[1], order[3]]
+        order = [order[3], order[0], order[2], order[1]]
     swapped = list(order)
     for at in range(0, len(order) - 1, 2):
         swapped[at], swapped[at + 1] = order[at + 1], order[at]
@@ -293,9 +299,7 @@
 def body(n_grp, n_peak, counts, tile_mask, neighbours, peak_weight, gain, w_in, w_out):
     cells = counts.shape[0]
     length_of = neighbours.shape[1]
-    carried = cells <= peak_weight.shape[1] and 1 + max(
-        row for _, row, _ in list_places(length_of, cells, peak_weight.shape[1])
-    ) <= EXTRA
+    carried = cells <= 512 and length_of <= 2 * SLOTS
     devices = n_grp * n_peak
 
     def exchange(values, bits):

time: 28.1 us -> 27.5 us (0.979)
  starting transfers between devices: 10.1 us -> 9.78 us
    ppermute x6, starting transfers between devices: 10.1 us -> 9.78 us  [exchange(): return lax.ppermute(values, ALL, pairs)]
where the time goes in v5:
time: 27.5 us; the launch traced here: 27.3 us
  waiting for transfers between devices  10 us (36%)
  starting transfers between devices  9.78 us (36%)
  Pallas kernels  6.58 us (24%)
  between operations  0.74 us (3%)
    ppermute x6, waiting for transfers between devices, exchange(): return lax.ppermute(values, ALL, pairs)  10 us
    ppermute x6, starting transfers between devices, exchange(): return lax.ppermute(values, ALL, pairs)  9.78 us
    pallas_call x1, Pallas kernels, tower(): pl.pallas_call(functools.partial(tower_kernel, carried, length_of, pieces...  4.02 us
    pallas_call x1, Pallas kernels, partial_hidden(): pl.pallas_call(functools.partial(partial_kernel, carried, pieces), out_sh...  2.37 us
  transfers between devices with their start and end apart: 6, of which 6 were waited for; matrix products, arithmetic and copies ran while one was open for 0% of the time, Pallas kernels for 1%

profile of v5, /device:TPU:0, one launch (start us, length us, event | category | flops | bytes accessed | tf_op | source)
XLA Modules:
  0.0 27.3 jit_solution(3627253841002748948)
XLA Ops:
  0.6 0.0 copy-start
  0.6 0.0 copy-start.2
  0.7 0.0 copy-start.1
  0.7 0.0 copy-start.3
  0.7 2.4 %shard_map.102 = (f32[33,8,128]{2,1,0:T(8,128)S(1)}, f32[33,8,128]{2,1,0:T(8,128)S(1)}, bf16[128,2048]{1,0:T(8,128)(2,1)S(1)}) custom-call(bf16[128,2048]{1,0:T(8,128)(2,1)} %counts_hbm.1, s32[16,128]{1,0:T(8,128)} %bitcast.4, s32[4,15]{1,0:T(4,128)} %lists_ref.1, bf16[2048,512]{1,0:T(8,128)(2,1)} %weight_hbm.1), custom_call_target="tpu_custom_call" | custom-call | flops 268435456 | bytes 3416064 | tf_op jit(solution)/shard_map/pallas_call | solution.py:114
  3.0 0.5 %collective-permute-start = (f32[33,8,128]{2,1,0:T(8,128)S(1)}, f32[33,8,128]{2,1,0:T(8,128)S(1)}, u32[]{:S(2)}, u32[]{:S(2)}) collective-permute-start(f32[33,8,128]{2,1,0:T(8,128)S(1)} %get-tuple-element.14), channel_id=1, source_target_pairs={{0,8},{1,9},{2,10},{3,11},{4,12},{5,13},{6,14},{7,15},{8,0},{9,1},... | collective-permute-start | bytes 405512 | tf_op jit(solution)/shard_map/ppermute | solution.py:307
  3.6 1.0 %collective-permute-done = f32[33,8,128]{2,1,0:T(8,128)S(1)} collective-permute-done((f32[33,8,128]{2,1,0:T(8,128)S(1)}, f32[33,8,128]{2,1,0:T(8,128)S(1)}, u32[]{:S(2)}, u32[]{:S(2)}) %collective-permute-start) | collective-permute-done | bytes 135200 | tf_op jit(solution)/shard_map/ppermute | solution.py:307
  4.6 3.8 %collective-permute-start.1 = (f16[33,8,128]{2,1,0:T(8,128)(2,1)S(1)}, f16[33,8,128]{2,1,0:T(8,128)(2,1)S(1)}, u32[]{:S(2)}, u32[]{:S(2)}) collective-permute-start(f16[33,8,128]{2,1,0:T(8,128)(2,1)S(1)} %add_convert_fusion.4), channel_id=1, source_target_pairs={{0,12},{1,25},{2,26},{3,15},{4,28},{5,9},{6,10},{7,31},{8,16},{9,5... | collective-permute-start | bytes 202760 | tf_op jit(solution)/shard_map/ppermute | solution.py:307
  8.3 2.0 %collective-permute-done.1 = f16[33,8,128]{2,1,0:T(8,128)(2,1)S(1)} collective-permute-done((f16[33,8,128]{2,1,0:T(8,128)(2,1)S(1)}, f16[33,8,128]{2,1,0:T(8,128)(2,1)S(1)}, u32[]{:S(2)}, u32[]{:S(2)}) %collective-permute-start.1) | collective-permute-done | bytes 67616 | tf_op jit(solution)/shard_map/ppermute | solution.py:307
  10.3 1.6 %collective-permute-start.2 = (f16[33,8,128]{2,1,0:T(8,128)(2,1)S(1)}, f16[33,8,128]{2,1,0:T(8,128)(2,1)S(1)}, u32[]{:S(2)}, u32[]{:S(2)}) collective-permute-start(f16[33,8,128]{2,1,0:T(8,128)(2,1)S(1)} %add_convert_fusion.3), channel_id=1, source_target_pairs={{0,24},{1,13},{2,14},{3,27},{4,8},{5,29},{6,30},{7,11},{8,4},{9,17... | collective-permute-start | bytes 202760 | tf_op jit(solution)/shard_map/ppermute | solution.py:307
  12.0 2.2 %collective-permute-done.2 = f16[33,8,128]{2,1,0:T(8,128)(2,1)S(1)} collective-permute-done((f16[33,8,128]{2,1,0:T(8,128)(2,1)S(1)}, f16[33,8,128]{2,1,0:T(8,128)(2,1)S(1)}, u32[]{:S(2)}, u32[]{:S(2)}) %collective-permute-start.2) | collective-permute-done | bytes 67616 | tf_op jit(solution)/shard_map/ppermute | solution.py:307
  14.2 1.7 %collective-permute-start.3 = (f16[33,8,128]{2,1,0:T(8,128)(2,1)S(1)}, f16[33,8,128]{2,1,0:T(8,128)(2,1)S(1)}, u32[]{:S(2)}, u32[]{:S(2)}) collective-permute-start(f16[33,8,128]{2,1,0:T(8,128)(2,1)S(1)} %add_convert_fusion.2), channel_id=1, source_target_pairs={{0,10},{1,8},{2,11},{3,9},{4,13},{5,15},{6,12},{7,14},{8,1},{9,3},... | collective-permute-start | bytes 202760 | tf_op jit(solution)/shard_map/ppermute | solution.py:307
  15.8 0.2 shard_map.103.turned_ref
  16.0 1.9 %collective-permute-done.3 = f16[33,8,128]{2,1,0:T(8,128)(2,1)S(1)} collective-permute-done((f16[33,8,128]{2,1,0:T(8,128)(2,1)S(1)}, f16[33,8,128]{2,1,0:T(8,128)(2,1)S(1)}, u32[]{:S(2)}, u32[]{:S(2)}) %collective-permute-start.3) | collective-permute-done | bytes 67616 | tf_op jit(solution)/shard_map/ppermute | solution.py:307
  18.0 1.6 %collective-permute-start.4 = (f16[33,8,128]{2,1,0:T(8,128)(2,1)S(1)}, f16[33,8,128]{2,1,0:T(8,128)(2,1)S(1)}, u32[]{:S(2)}, u32[]{:S(2)}) collective-permute-start(f16[33,8,128]{2,1,0:T(8,128)(2,1)S(1)} %add_convert_fusion.1), channel_id=1, source_target_pairs={{0,9},{1,11},{2,8},{3,10},{4,14},{5,12},{6,15},{7,13},{8,2},{9,0},... | collective-permute-start | bytes 202760 | tf_op jit(solution)/shard_map/ppermute | solution.py:307
  19.6 2.1 %collective-permute-done.4 = f16[33,8,128]{2,1,0:T(8,128)(2,1)S(1)} collective-permute-done((f16[33,8,128]{2,1,0:T(8,128)(2,1)S(1)}, f16[33,8,128]{2,1,0:T(8,128)(2,1)S(1)}, u32[]{:S(2)}, u32[]{:S(2)}) %collective-permute-start.4) | collective-permute-done | bytes 67616 | tf_op jit(solution)/shard_map/ppermute | solution.py:307
  21.8 0.5 %collective-permute-start.5 = (f16[33,8,128]{2,1,0:T(8,128)(2,1)S(1)}, f16[33,8,128]{2,1,0:T(8,128)(2,1)S(1)}, u32[]{:S(2)}, u32[]{:S(2)}) collective-permute-start(f16[33,8,128]{2,1,0:T(8,128)(2,1)S(1)} %add_convert_fusion), channel_id=1, source_target_pairs={{0,8},{1,9},{2,10},{3,11},{4,12},{5,13},{6,14},{7,15},{8,0},{9,1},... | collective-permute-start | bytes 202760 | tf_op jit(solution)/shard_map/ppermute | solution.py:307
  22.3 0.9 %collective-permute-done.5 = f16[33,8,128]{2,1,0:T(8,128)(2,1)S(1)} collective-permute-done((f16[33,8,128]{2,1,0:T(8,128)(2,1)S(1)}, f16[33,8,128]{2,1,0:T(8,128)(2,1)S(1)}, u32[]{:S(2)}, u32[]{:S(2)}) %collective-permute-start.5) | collective-permute-done | bytes 67616 | tf_op jit(solution)/shard_map/ppermute | solution.py:307
  23.2 0.0 copy-done
  23.2 0.0 copy-done.2
  23.3 0.0 copy-done.1
  23.3 0.0 copy-done.3
  23.3 4.0 %shard_map.104 = (f32[2048,512]{1,0:T(8,128)}, f32[1,512]{1,0:T(1,128)}, f32[512,512]{1,0:T(8,128)}, f32[512,256]{1,0:T(8,128)}) custom-call(f32[33,8,128]{2,1,0:T(8,128)S(1)} %convert_element_type.58.own_ref, f32[33,8,128]{2,1,0:T(8,128)S(1)} %convert_element_type.59.other_ref, s32[4,15]{1,0:T(4,128)S(1)} %copy-done, ...), custom_call_target="tpu_custom_call" | custom-call | flops 570425344 | bytes 7077888 | tf_op jit(solution)/shard_map/pallas_call | solution.py:254
  (7 shorter events, 0.2 us)
Async XLA Ops:
  0.6 22.6 %copy-start = (s32[4,15]{1,0:T(4,128)S(1)}, s32[4,15]{1,0:T(4,128)}, u32[]{:S(2)}) copy-start(s32[4,15]{1,0:T(4,128)} %lists_ref.1) | copy-start | bytes 724
  0.6 22.6 %copy-start.2 = (bf16[512,256]{1,0:T(8,128)(2,1)S(1)}, bf16[512,256]{1,0:T(8,128)(2,1)}, u32[]{:S(2)}) copy-start(bf16[512,256]{1,0:T(8,128)(2,1)} %w_out_ref.1) | copy-start | bytes 786436
  0.7 22.6 %copy-start.1 = (bf16[512,512]{1,0:T(8,128)(2,1)S(1)}, bf16[512,512]{1,0:T(8,128)(2,1)}, u32[]{:S(2)}) copy-start(bf16[512,512]{1,0:T(8,128)(2,1)} %w_in_ref.1) | copy-start | bytes 1572868
  0.7 22.6 %copy-start.3 = (f32[512]{0:T(512)S(1)}, f32[512]{0:T(512)}, u32[]{:S(2)}) copy-start(f32[512]{0:T(512)} %param.11) | copy-start | bytes 6148
  3.0 1.5 %collective-permute-start = (f32[33,8,128]{2,1,0:T(8,128)S(1)}, f32[33,8,128]{2,1,0:T(8,128)S(1)}, u32[]{:S(2)}, u32[]{:S(2)}) collective-permute-start(f32[33,8,128]{2,1,0:T(8,128)S(1)} %get-tuple-element.14), channel_id=1, source_target_pairs={{0,8},{1,9},{2,10},{3,11},{4,12},{5,13},{6,14},{7,15},{8,0},{9,1},... | collective-permute-start | bytes 405512 | tf_op jit(solution)/shard_map/ppermute | solution.py:307
  4.6 5.7 %collective-permute-start.1 = (f16[33,8,128]{2,1,0:T(8,128)(2,1)S(1)}, f16[33,8,128]{2,1,0:T(8,128)(2,1)S(1)}, u32[]{:S(2)}, u32[]{:S(2)}) collective-permute-start(f16[33,8,128]{2,1,0:T(8,128)(2,1)S(1)} %add_convert_fusion.4), channel_id=1, source_target_pairs={{0,12},{1,25},{2,26},{3,15},{4,28},{5,9},{6,10},{7,31},{8,16},{9,5... | collective-permute-start | bytes 202760 | tf_op jit(solution)/shard_map/ppermute | solution.py:307
  10.3 3.8 %collective-permute-start.2 = (f16[33,8,128]{2,1,0:T(8,128)(2,1)S(1)}, f16[33,8,128]{2,1,0:T(8,128)(2,1)S(1)}, u32[]{:S(2)}, u32[]{:S(2)}) collective-permute-start(f16[33,8,128]{2,1,0:T(8,128)(2,1)S(1)} %add_convert_fusion.3), channel_id=1, source_target_pairs={{0,24},{1,13},{2,14},{3,27},{4,8},{5,29},{6,30},{7,11},{8,4},{9,17... | collective-permute-start | bytes 202760 | tf_op jit(solution)/shard_map/ppermute | solution.py:307
  14.2 3.8 %collective-permute-start.3 = (f16[33,8,128]{2,1,0:T(8,128)(2,1)S(1)}, f16[33,8,128]{2,1,0:T(8,128)(2,1)S(1)}, u32[]{:S(2)}, u32[]{:S(2)}) collective-permute-start(f16[33,8,128]{2,1,0:T(8,128)(2,1)S(1)} %add_convert_fusion.2), channel_id=1, source_target_pairs={{0,10},{1,8},{2,11},{3,9},{4,13},{5,15},{6,12},{7,14},{8,1},{9,3},... | collective-permute-start | bytes 202760 | tf_op jit(solution)/shard_map/ppermute | solution.py:307
  18.0 3.8 %collective-permute-start.4 = (f16[33,8,128]{2,1,0:T(8,128)(2,1)S(1)}, f16[33,8,128]{2,1,0:T(8,128)(2,1)S(1)}, u32[]{:S(2)}, u32[]{:S(2)}) collective-permute-start(f16[33,8,128]{2,1,0:T(8,128)(2,1)S(1)} %add_convert_fusion.1), channel_id=1, source_target_pairs={{0,9},{1,11},{2,8},{3,10},{4,14},{5,12},{6,15},{7,13},{8,2},{9,0},... | collective-permute-start | bytes 202760 | tf_op jit(solution)/shard_map/ppermute | solution.py:307
  21.8 1.4 %collective-permute-start.5 = (f16[33,8,128]{2,1,0:T(8,128)(2,1)S(1)}, f16[33,8,128]{2,1,0:T(8,128)(2,1)S(1)}, u32[]{:S(2)}, u32[]{:S(2)}) collective-permute-start(f16[33,8,128]{2,1,0:T(8,128)(2,1)S(1)} %add_convert_fusion), channel_id=1, source_target_pairs={{0,8},{1,9},{2,10},{3,11},{4,12},{5,13},{6,14},{7,15},{8,0},{9,1},... | collective-permute-start | bytes 202760 | tf_op jit(solution)/shard_map/ppermute | solution.py:307

commit v6 on v5

--- a/solution.py
+++ b/solution.py
@@ -158,10 +158,11 @@
 
 
 def tower_kernel(
-    carried, length_of, pieces, own_ref, other_ref, lists_ref, turned_ref, gain_ref, w_in_ref, w_out_ref,
-    peak_grad_hbm, gain_grad_hbm, in_grad_hbm, out_grad_hbm,
-    hidden_ref, peak_grad_ref, gain_grad_ref, in_grad_ref, out_grad_ref, peak_sem, side_sem,
+    carried, length_of, pieces, own_ref, other_ref, turned_ref, gain_ref, w_in_ref, w_out_ref, *refs
 ):
+    lists_refs, refs = ((), refs) if carried else (refs[:1], refs[1:])
+    peak_grad_hbm, gain_grad_hbm, in_grad_hbm, out_grad_hbm, *refs = refs
+    hidden_ref, peak_grad_ref, gain_grad_ref, in_grad_ref, out_grad_ref, peak_sem, side_sem = refs
     cells = hidden_ref.shape[0]
     half = cells // 2
     gain_copy = pltpu.make_async_copy(gain_grad_ref, gain_grad_hbm, side_sem.at[0])
@@ -179,7 +180,7 @@
         high = [jnp.where(mine == 0, other, own) for own, other in pairs]
         lists = jnp.concatenate([jnp.concatenate(low, axis=1), jnp.concatenate(high, axis=1)], axis=0)
     else:
-        lists = lists_ref[...].astype(F32)
+        lists = lists_refs[0][...].astype(F32)
     gain = gain_ref[...]
     w_in, w_out = w_in_ref[...], w_out_ref[...]
 
@@ -244,7 +245,7 @@
     out_copy.wait()
 
 
-def tower(carried, length_of, own, other, lists, turned, gain, w_in, w_out):
+def tower(carried, length_of, own, other, turned, gain, w_in, w_out, *lists):
     peaks, cells = turned.shape
     width, hid = w_in.shape
     codes = w_out.shape[1]
@@ -259,7 +260,7 @@
             jax.ShapeDtypeStruct((width, hid), F32),
             jax.ShapeDtypeStruct((hid, codes), F32),
         ],
-        in_specs=[whole] * 7,
+        in_specs=[whole] * (6 + len(lists)),
         out_specs=[main] * 4,
         scratch_shapes=[
             pltpu.VMEM((cells, width), F32),
@@ -281,7 +282,7 @@
             bytes_accessed=2 * peaks * cells + 4 * peaks * width + 6 * width * hid + 6 * hid * codes,
             transcendentals=cells * (hid + cells),
         ),
-    )(own, other, lists, turned, gain, w_in, w_out)
+    )(own, other, turned, gain, w_in, w_out, *lists)
 
 
 def flips(n_grp, n_peak):
@@ -312,6 +313,8 @@
     mask = tile_mask.T
     send, held, masked = partial_hidden(carried, counts, mask, neighbours, peak_weight)
     held = add(held, exchange(send, (n_peak, n_peak)))
+    held, w_in, w_out, gain = lax.optimization_barrier((held, w_in, w_out, gain))
+    gain = gain.reshape(1, -1)
     turned = turn(masked)
     steps = flips(n_grp, n_peak)
     for at, bits in enumerate(steps):
@@ -320,12 +323,9 @@
             held, turned = lax.optimization_barrier((held, turned))
     other = exchange(held, (n_peak, n_peak)).astype(F32)
     held = held.astype(F32)
-    if carried:
-        lists = neighbours
-    else:
-        lists = lax.all_gather(neighbours, ALL, axis=0, tiled=True).T
+    lists = () if carried else (lax.all_gather(neighbours, ALL, axis=0, tiled=True).T,)
     peak_grad, gain_grad, in_grad, out_grad = tower(
-        carried, length_of, held, other, lists, turned, gain.reshape(1, -1), w_in, w_out
+        carried, length_of, held, other, turned, gain, w_in, w_out, *lists
     )
     return (peak_grad, gain_grad.reshape(-1), in_grad, out_grad)
 

time: 27.5 us -> 27.4 us (level)
  no operation moved by 1% of the time
where the time goes in v6:
time: 27.4 us; the launch traced here: 27.2 us
  waiting for transfers between devices  10 us (36%)
  starting transfers between devices  9.77 us (36%)
  Pallas kernels  6.48 us (24%)
  between operations  0.72 us (3%)
    ppermute x6, waiting for transfers between devices, exchange(): return lax.ppermute(values, ALL, pairs)  10 us
    ppermute x6, starting transfers between devices, exchange(): return lax.ppermute(values, ALL, pairs)  9.77 us
    pallas_call x1, Pallas kernels, tower(): pl.pallas_call(functools.partial(tower_kernel, carried, length_of, pieces...  4.04 us
    pallas_call x1, Pallas kernels, partial_hidden(): pl.pallas_call(functools.partial(partial_kernel, carried, pieces), out_sh...  2.25 us
  transfers between devices with their start and end apart: 6, of which 6 were waited for; matrix products, arithmetic and copies ran while one was open for 0% of the time, Pallas kernels for 1%

profile of v6, /device:TPU:0, one launch (start us, length us, event | category | flops | bytes accessed | tf_op | source)
XLA Modules:
  0.0 27.2 jit_solution(5254490004479961042)
XLA Ops:
  0.6 0.0 copy-start.1
  0.6 0.0 copy-start
  0.7 0.0 copy-start.2
  0.7 2.3 %shard_map.102 = (f32[33,8,128]{2,1,0:T(8,128)S(1)}, f32[33,8,128]{2,1,0:T(8,128)S(1)}, bf16[128,2048]{1,0:T(8,128)(2,1)S(1)}) custom-call(bf16[128,2048]{1,0:T(8,128)(2,1)} %counts_hbm.1, s32[16,128]{1,0:T(8,128)} %bitcast.4, s32[4,15]{1,0:T(4,128)} %lists_hbm.1, bf16[2048,512]{1,0:T(8,128)(2,1)} %weight_hbm.1), custom_call_target="tpu_custom_call" | custom-call | flops 268435456 | bytes 3416064 | tf_op jit(solution)/shard_map/pallas_call | solution.py:114
  2.9 0.5 %collective-permute-start = (f32[33,8,128]{2,1,0:T(8,128)S(1)}, f32[33,8,128]{2,1,0:T(8,128)S(1)}, u32[]{:S(2)}, u32[]{:S(2)}) collective-permute-start(f32[33,8,128]{2,1,0:T(8,128)S(1)} %get-tuple-element.18), channel_id=1, source_target_pairs={{0,8},{1,9},{2,10},{3,11},{4,12},{5,13},{6,14},{7,15},{8,0},{9,1},... | collective-permute-start | bytes 405512 | tf_op jit(solution)/shard_map/ppermute | solution.py:308
  3.4 1.0 %collective-permute-done = f32[33,8,128]{2,1,0:T(8,128)S(1)} collective-permute-done((f32[33,8,128]{2,1,0:T(8,128)S(1)}, f32[33,8,128]{2,1,0:T(8,128)S(1)}, u32[]{:S(2)}, u32[]{:S(2)}) %collective-permute-start) | collective-permute-done | bytes 135200 | tf_op jit(solution)/shard_map/ppermute | solution.py:308
  4.5 3.8 %collective-permute-start.1 = (f16[33,8,128]{2,1,0:T(8,128)(2,1)S(1)}, f16[33,8,128]{2,1,0:T(8,128)(2,1)S(1)}, u32[]{:S(2)}, u32[]{:S(2)}) collective-permute-start(f16[33,8,128]{2,1,0:T(8,128)(2,1)S(1)} %add_convert_fusion.4), channel_id=1, source_target_pairs={{0,12},{1,25},{2,26},{3,15},{4,28},{5,9},{6,10},{7,31},{8,16},{9,5... | collective-permute-start | bytes 202760 | tf_op jit(solution)/shard_map/ppermute | solution.py:308
  8.2 2.0 %collective-permute-done.1 = f16[33,8,128]{2,1,0:T(8,128)(2,1)S(1)} collective-permute-done((f16[33,8,128]{2,1,0:T(8,128)(2,1)S(1)}, f16[33,8,128]{2,1,0:T(8,128)(2,1)S(1)}, u32[]{:S(2)}, u32[]{:S(2)}) %collective-permute-start.1) | collective-permute-done | bytes 67616 | tf_op jit(solution)/shard_map/ppermute | solution.py:308
  10.2 1.6 %collective-permute-start.2 = (f16[33,8,128]{2,1,0:T(8,128)(2,1)S(1)}, f16[33,8,128]{2,1,0:T(8,128)(2,1)S(1)}, u32[]{:S(2)}, u32[]{:S(2)}) collective-permute-start(f16[33,8,128]{2,1,0:T(8,128)(2,1)S(1)} %add_convert_fusion.3), channel_id=1, source_target_pairs={{0,24},{1,13},{2,14},{3,27},{4,8},{5,29},{6,30},{7,11},{8,4},{9,17... | collective-permute-start | bytes 202760 | tf_op jit(solution)/shard_map/ppermute | solution.py:308
  11.8 2.2 %collective-permute-done.2 = f16[33,8,128]{2,1,0:T(8,128)(2,1)S(1)} collective-permute-done((f16[33,8,128]{2,1,0:T(8,128)(2,1)S(1)}, f16[33,8,128]{2,1,0:T(8,128)(2,1)S(1)}, u32[]{:S(2)}, u32[]{:S(2)}) %collective-permute-start.2) | collective-permute-done | bytes 67616 | tf_op jit(solution)/shard_map/ppermute | solution.py:308
  14.0 1.7 %collective-permute-start.3 = (f16[33,8,128]{2,1,0:T(8,128)(2,1)S(1)}, f16[33,8,128]{2,1,0:T(8,128)(2,1)S(1)}, u32[]{:S(2)}, u32[]{:S(2)}) collective-permute-start(f16[33,8,128]{2,1,0:T(8,128)(2,1)S(1)} %add_convert_fusion.2), channel_id=1, source_target_pairs={{0,10},{1,8},{2,11},{3,9},{4,13},{5,15},{6,12},{7,14},{8,1},{9,3},... | collective-permute-start | bytes 202760 | tf_op jit(solution)/shard_map/ppermute | solution.py:308
  15.7 0.2 shard_map.103.turned_ref
  15.9 1.9 %collective-permute-done.3 = f16[33,8,128]{2,1,0:T(8,128)(2,1)S(1)} collective-permute-done((f16[33,8,128]{2,1,0:T(8,128)(2,1)S(1)}, f16[33,8,128]{2,1,0:T(8,128)(2,1)S(1)}, u32[]{:S(2)}, u32[]{:S(2)}) %collective-permute-start.3) | collective-permute-done | bytes 67616 | tf_op jit(solution)/shard_map/ppermute | solution.py:308
  17.8 1.6 %collective-permute-start.4 = (f16[33,8,128]{2,1,0:T(8,128)(2,1)S(1)}, f16[33,8,128]{2,1,0:T(8,128)(2,1)S(1)}, u32[]{:S(2)}, u32[]{:S(2)}) collective-permute-start(f16[33,8,128]{2,1,0:T(8,128)(2,1)S(1)} %add_convert_fusion.1), channel_id=1, source_target_pairs={{0,9},{1,11},{2,8},{3,10},{4,14},{5,12},{6,15},{7,13},{8,2},{9,0},... | collective-permute-start | bytes 202760 | tf_op jit(solution)/shard_map/ppermute | solution.py:308
  19.5 2.1 %collective-permute-done.4 = f16[33,8,128]{2,1,0:T(8,128)(2,1)S(1)} collective-permute-done((f16[33,8,128]{2,1,0:T(8,128)(2,1)S(1)}, f16[33,8,128]{2,1,0:T(8,128)(2,1)S(1)}, u32[]{:S(2)}, u32[]{:S(2)}) %collective-permute-start.4) | collective-permute-done | bytes 67616 | tf_op jit(solution)/shard_map/ppermute | solution.py:308
  21.7 0.5 %collective-permute-start.5 = (f16[33,8,128]{2,1,0:T(8,128)(2,1)S(1)}, f16[33,8,128]{2,1,0:T(8,128)(2,1)S(1)}, u32[]{:S(2)}, u32[]{:S(2)}) collective-permute-start(f16[33,8,128]{2,1,0:T(8,128)(2,1)S(1)} %add_convert_fusion), channel_id=1, source_target_pairs={{0,8},{1,9},{2,10},{3,11},{4,12},{5,13},{6,14},{7,15},{8,0},{9,1},... | collective-permute-start | bytes 202760 | tf_op jit(solution)/shard_map/ppermute | solution.py:308
  22.2 0.9 %collective-permute-done.5 = f16[33,8,128]{2,1,0:T(8,128)(2,1)S(1)} collective-permute-done((f16[33,8,128]{2,1,0:T(8,128)(2,1)S(1)}, f16[33,8,128]{2,1,0:T(8,128)(2,1)S(1)}, u32[]{:S(2)}, u32[]{:S(2)}) %collective-permute-start.5) | collective-permute-done | bytes 67616 | tf_op jit(solution)/shard_map/ppermute | solution.py:308
  23.1 0.0 copy-done.1
  23.1 0.0 copy-done
  23.1 0.0 copy-done.2
  23.1 4.0 %shard_map.104 = (f32[2048,512]{1,0:T(8,128)}, f32[1,512]{1,0:T(1,128)}, f32[512,512]{1,0:T(8,128)}, f32[512,256]{1,0:T(8,128)}) custom-call(f32[33,8,128]{2,1,0:T(8,128)S(1)} %convert_element_type.58.own_ref, f32[33,8,128]{2,1,0:T(8,128)S(1)} %convert_element_type.59.other_ref, bf16[2048,128]{1,0:T(8,128)(2,1)S(1)} %shard_map.103.turned_ref, ...), custom_call_target="tpu_custom_call" | custom-call | flops 570425344 | bytes 7077888 | tf_op jit(solution)/shard_map/pallas_call | solution.py:255
  (7 shorter events, 0.2 us)
Async XLA Ops:
  0.6 22.5 %copy-start.1 = (bf16[512,256]{1,0:T(8,128)(2,1)S(1)}, bf16[512,256]{1,0:T(8,128)(2,1)}, u32[]{:S(2)}) copy-start(bf16[512,256]{1,0:T(8,128)(2,1)} %w_out_ref) | copy-start | bytes 786436
  0.6 22.5 %copy-start = (bf16[512,512]{1,0:T(8,128)(2,1)S(1)}, bf16[512,512]{1,0:T(8,128)(2,1)}, u32[]{:S(2)}) copy-start(bf16[512,512]{1,0:T(8,128)(2,1)} %w_in_ref) | copy-start | bytes 1572868
  0.7 22.5 %copy-start.2 = (f32[512]{0:T(512)S(1)}, f32[512]{0:T(512)}, u32[]{:S(2)}) copy-start(f32[512]{0:T(512)} %param.11) | copy-start | bytes 6148
  2.9 1.5 %collective-permute-start = (f32[33,8,128]{2,1,0:T(8,128)S(1)}, f32[33,8,128]{2,1,0:T(8,128)S(1)}, u32[]{:S(2)}, u32[]{:S(2)}) collective-permute-start(f32[33,8,128]{2,1,0:T(8,128)S(1)} %get-tuple-element.18), channel_id=1, source_target_pairs={{0,8},{1,9},{2,10},{3,11},{4,12},{5,13},{6,14},{7,15},{8,0},{9,1},... | collective-permute-start | bytes 405512 | tf_op jit(solution)/shard_map/ppermute | solution.py:308
  4.5 5.7 %collective-permute-start.1 = (f16[33,8,128]{2,1,0:T(8,128)(2,1)S(1)}, f16[33,8,128]{2,1,0:T(8,128)(2,1)S(1)}, u32[]{:S(2)}, u32[]{:S(2)}) collective-permute-start(f16[33,8,128]{2,1,0:T(8,128)(2,1)S(1)} %add_convert_fusion.4), channel_id=1, source_target_pairs={{0,12},{1,25},{2,26},{3,15},{4,28},{5,9},{6,10},{7,31},{8,16},{9,5... | collective-permute-start | bytes 202760 | tf_op jit(solution)/shard_map/ppermute | solution.py:308
  10.2 3.8 %collective-permute-start.2 = (f16[33,8,128]{2,1,0:T(8,128)(2,1)S(1)}, f16[33,8,128]{2,1,0:T(8,128)(2,1)S(1)}, u32[]{:S(2)}, u32[]{:S(2)}) collective-permute-start(f16[33,8,128]{2,1,0:T(8,128)(2,1)S(1)} %add_convert_fusion.3), channel_id=1, source_target_pairs={{0,24},{1,13},{2,14},{3,27},{4,8},{5,29},{6,30},{7,11},{8,4},{9,17... | collective-permute-start | bytes 202760 | tf_op jit(solution)/shard_map/ppermute | solution.py:308
  14.0 3.8 %collective-permute-start.3 = (f16[33,8,128]{2,1,0:T(8,128)(2,1)S(1)}, f16[33,8,128]{2,1,0:T(8,128)(2,1)S(1)}, u32[]{:S(2)}, u32[]{:S(2)}) collective-permute-start(f16[33,8,128]{2,1,0:T(8,128)(2,1)S(1)} %add_convert_fusion.2), channel_id=1, source_target_pairs={{0,10},{1,8},{2,11},{3,9},{4,13},{5,15},{6,12},{7,14},{8,1},{9,3},... | collective-permute-start | bytes 202760 | tf_op jit(solution)/shard_map/ppermute | solution.py:308
  17.8 3.8 %collective-permute-start.4 = (f16[33,8,128]{2,1,0:T(8,128)(2,1)S(1)}, f16[33,8,128]{2,1,0:T(8,128)(2,1)S(1)}, u32[]{:S(2)}, u32[]{:S(2)}) collective-permute-start(f16[33,8,128]{2,1,0:T(8,128)(2,1)S(1)} %add_convert_fusion.1), channel_id=1, source_target_pairs={{0,9},{1,11},{2,8},{3,10},{4,14},{5,12},{6,15},{7,13},{8,2},{9,0},... | collective-permute-start | bytes 202760 | tf_op jit(solution)/shard_map/ppermute | solution.py:308
  21.7 1.4 %collective-permute-start.5 = (f16[33,8,128]{2,1,0:T(8,128)(2,1)S(1)}, f16[33,8,128]{2,1,0:T(8,128)(2,1)S(1)}, u32[]{:S(2)}, u32[]{:S(2)}) collective-permute-start(f16[33,8,128]{2,1,0:T(8,128)(2,1)S(1)} %add_convert_fusion), channel_id=1, source_target_pairs={{0,8},{1,9},{2,10},{3,11},{4,12},{5,13},{6,14},{7,15},{8,0},{9,1},... | collective-permute-start | bytes 202760 | tf_op jit(solution)/shard_map/ppermute | solution.py:308

commit v7 on v6

--- a/solution.py
+++ b/solution.py
@@ -285,16 +285,13 @@
     )(own, other, turned, gain, w_in, w_out, *lists)
 
 
-def flips(n_grp, n_peak):
+def chip_steps(n_grp, n_peak):
     grp_bits = [bit * n_peak for bit in (2, 4, 8, 16, 32, 64) if bit < n_grp]
     peak_bits = [bit for bit in (1, 2, 4, 8, 16, 32, 64) if bit < n_peak]
     order = grp_bits + peak_bits
-    if len(order) == 4:
-        order = [order[3], order[0], order[2], order[1]]
-    swapped = list(order)
-    for at in range(0, len(order) - 1, 2):
-        swapped[at], swapped[at + 1] = order[at + 1], order[at]
-    return list(zip(order, swapped, strict=True))
+    fours = [(min(pair), max(pair), sum(pair)) for pair in zip(order[::2], order[1::2], strict=False)]
+    steps = [list(zip(*both, strict=True)) for both in zip(reversed(fours), fours, strict=True)]
+    return steps + [[(bit, bit)] for bit in order[2 * len(fours) :]]
 
 
 def body(n_grp, n_peak, counts, tile_mask, neighbours, peak_weight, gain, w_in, w_out):
@@ -304,24 +301,33 @@
     devices = n_grp * n_peak
 
     def exchange(values, bits):
-        pairs = [(i, i ^ bits[i.bit_count() % 2]) for i in range(devices)]
-        return lax.ppermute(values, ALL, pairs)
-
-    def add(left, right):
-        return lax.optimization_barrier((left.astype(F32) + right.astype(F32)).astype(LINK))
+        def partner(i):
+            bit = bits[i.bit_count() % 2]
+            return i ^ bit ^ (n_peak if bit.bit_count() % 2 else 0)
+
+        return lax.ppermute(values, ALL, [(i, partner(i)) for i in range(devices)])
+
+    def between_cores(values):
+        return lax.ppermute(values, ALL, [(i, i ^ n_peak) for i in range(devices)])
+
+    def total(terms):
+        terms = [term.astype(F32) for term in terms]
+        while len(terms) > 1:
+            terms = [left + right for left, right in zip(terms[::2], terms[1::2], strict=True)]
+        return lax.optimization_barrier(terms[0].astype(LINK))
 
     mask = tile_mask.T
     send, held, masked = partial_hidden(carried, counts, mask, neighbours, peak_weight)
-    held = add(held, exchange(send, (n_peak, n_peak)))
+    held = total([held, between_cores(send)])
     held, w_in, w_out, gain = lax.optimization_barrier((held, w_in, w_out, gain))
     gain = gain.reshape(1, -1)
     turned = turn(masked)
-    steps = flips(n_grp, n_peak)
-    for at, bits in enumerate(steps):
-        held = add(held, exchange(held, tuple(bit ^ n_peak for bit in bits)))
-        if at == len(steps) // 2:
+    steps = chip_steps(n_grp, n_peak)
+    for step in steps:
+        held = total([held] + [exchange(held, bits) for bits in step])
+        if step is steps[-1]:
             held, turned = lax.optimization_barrier((held, turned))
-    other = exchange(held, (n_peak, n_peak)).astype(F32)
+    other = between_cores(held).astype(F32)
     held = held.astype(F32)
     lists = () if carried else (lax.all_gather(neighbours, ALL, axis=0, tiled=True).T,)
     peak_grad, gain_grad, in_grad, out_grad = tower(

time: 27.4 us -> 26.1 us (0.953)
  waiting for transfers between devices: 10 us -> 8.89 us
    ppermute x6 -> x8, waiting for transfers between devices: 10 us -> 8.89 us  [the longest x6 7.01 us: exchange(): return lax.ppermute(values, ALL, [(i, partner(i)) for i in range(devices)])]
    ppermute x6 -> x8, starting transfers between devices: 9.77 us -> 9.72 us  [the longest x6 8.66 us: exchange(): return lax.ppermute(values, ALL, [(i, partner(i)) for i in range(devices)])]
  transfers between devices with their start and end apart: 6 -> 8, of which waited for: 6 -> 6; matrix products, arithmetic and copies ran while one was open for 0% -> 0% of each run, Pallas kernels for 1% -> 1%
where the time goes in v7:
time: 26.1 us; the launch traced here: 26 us
  starting transfers between devices  9.72 us (37%)
  waiting for transfers between devices  8.89 us (34%)
  Pallas kernels  6.48 us (25%)
  between operations  0.72 us (3%)
    ppermute x6, starting transfers between devices, exchange(): return lax.ppermute(values, ALL, [(i, partner(i)) for i in range(devices)])  8.66 us
    ppermute x6, waiting for transfers between devices, exchange(): return lax.ppermute(values, ALL, [(i, partner(i)) for i in range(devices)])  7.01 us
    pallas_call x1, Pallas kernels, tower(): pl.pallas_call(functools.partial(tower_kernel, carried, length_of, pieces...  4.04 us
    pallas_call x1, Pallas kernels, partial_hidden(): pl.pallas_call(functools.partial(partial_kernel, carried, pieces), out_sh...  2.25 us
    ppermute x2, waiting for transfers between devices, between_cores(): return lax.ppermute(values, ALL, [(i, i ^ n_peak) for i in range(devices)])  1.88 us
    ppermute x2, starting transfers between devices, between_cores(): return lax.ppermute(values, ALL, [(i, i ^ n_peak) for i in range(devices)])  1.06 us
  transfers between devices with their start and end apart: 8, of which 6 were waited for; matrix products, arithmetic and copies ran while one was open for 0% of the time, Pallas kernels for 1%

profile of v7, /device:TPU:0, one launch (start us, length us, event | category | flops | bytes accessed | tf_op | source)
XLA Modules:
  0.0 26.0 jit_solution(2761924583420462561)
XLA Ops:
  0.6 0.0 copy-start.1
  0.6 0.0 copy-start
  0.7 0.0 copy-start.2
  0.7 2.3 %shard_map.102 = (f32[33,8,128]{2,1,0:T(8,128)S(1)}, f32[33,8,128]{2,1,0:T(8,128)S(1)}, bf16[128,2048]{1,0:T(8,128)(2,1)S(1)}) custom-call(bf16[128,2048]{1,0:T(8,128)(2,1)} %counts_hbm.1, s32[16,128]{1,0:T(8,128)} %bitcast.4, s32[4,15]{1,0:T(4,128)} %lists_hbm.1, bf16[2048,512]{1,0:T(8,128)(2,1)} %weight_hbm.1), custom_call_target="tpu_custom_call" | custom-call | flops 268435456 | bytes 3416064 | tf_op jit(solution)/shard_map/pallas_call | solution.py:114
  2.9 0.5 %collective-permute-start = (f32[33,8,128]{2,1,0:T(8,128)S(1)}, f32[33,8,128]{2,1,0:T(8,128)S(1)}, u32[]{:S(2)}, u32[]{:S(2)}) collective-permute-start(f32[33,8,128]{2,1,0:T(8,128)S(1)} %get-tuple-element.18), channel_id=1, source_target_pairs={{0,8},{1,9},{2,10},{3,11},{4,12},{5,13},{6,14},{7,15},{8,0},{9,1},... | collective-permute-start | bytes 405512 | tf_op jit(solution)/shard_map/ppermute | solution.py:311
  3.4 1.0 %collective-permute-done = f32[33,8,128]{2,1,0:T(8,128)S(1)} collective-permute-done((f32[33,8,128]{2,1,0:T(8,128)S(1)}, f32[33,8,128]{2,1,0:T(8,128)S(1)}, u32[]{:S(2)}, u32[]{:S(2)}) %collective-permute-start) | collective-permute-done | bytes 135200 | tf_op jit(solution)/shard_map/ppermute | solution.py:311
  4.5 5.0 %collective-permute-start.3 = (f16[33,8,128]{2,1,0:T(8,128)(2,1)S(1)}, f16[33,8,128]{2,1,0:T(8,128)(2,1)S(1)}, u32[]{:S(2)}, u32[]{:S(2)}) collective-permute-start(f16[33,8,128]{2,1,0:T(8,128)(2,1)S(1)} %add_convert_fusion.2), channel_id=1, source_target_pairs={{0,6},{1,16},{2,19},{3,5},{4,21},{5,3},{6,0},{7,22},{8,25},{9,15},... | collective-permute-start | bytes 202760 | tf_op jit(solution)/shard_map/ppermute | solution.py:308
  9.5 0.0 collective-permute-start.2
  9.5 0.4 %collective-permute-start.1 = (f16[33,8,128]{2,1,0:T(8,128)(2,1)S(1)}, f16[33,8,128]{2,1,0:T(8,128)(2,1)S(1)}, u32[]{:S(2)}, u32[]{:S(2)}) collective-permute-start(f16[33,8,128]{2,1,0:T(8,128)(2,1)S(1)} %add_convert_fusion.2), channel_id=1, source_target_pairs={{0,10},{1,8},{2,11},{3,9},{4,13},{5,15},{6,12},{7,14},{8,1},{9,3},... | collective-permute-start | bytes 202760 | tf_op jit(solution)/shard_map/ppermute | solution.py:308
  9.8 1.9 %collective-permute-done.3 = f16[33,8,128]{2,1,0:T(8,128)(2,1)S(1)} collective-permute-done((f16[33,8,128]{2,1,0:T(8,128)(2,1)S(1)}, f16[33,8,128]{2,1,0:T(8,128)(2,1)S(1)}, u32[]{:S(2)}, u32[]{:S(2)}) %collective-permute-start.3) | collective-permute-done | bytes 67616 | tf_op jit(solution)/shard_map/ppermute | solution.py:308
  11.8 2.3 %collective-permute-done.2 = f16[33,8,128]{2,1,0:T(8,128)(2,1)S(1)} collective-permute-done((f16[33,8,128]{2,1,0:T(8,128)(2,1)S(1)}, f16[33,8,128]{2,1,0:T(8,128)(2,1)S(1)}, u32[]{:S(2)}, u32[]{:S(2)}) %collective-permute-start.2) | collective-permute-done | bytes 67616 | tf_op jit(solution)/shard_map/ppermute | solution.py:308
  14.1 0.0 collective-permute-done.1
  14.1 2.5 %collective-permute-start.6 = (f16[33,8,128]{2,1,0:T(8,128)(2,1)S(1)}, f16[33,8,128]{2,1,0:T(8,128)(2,1)S(1)}, u32[]{:S(2)}, u32[]{:S(2)}) collective-permute-start(f16[33,8,128]{2,1,0:T(8,128)(2,1)S(1)} %add_convert_fusion.1), channel_id=1, source_target_pairs={{0,17},{1,7},{2,4},{3,18},{4,2},{5,20},{6,23},{7,1},{8,14},{9,24},... | collective-permute-start | bytes 202760 | tf_op jit(solution)/shard_map/ppermute | solution.py:308
  16.7 0.0 collective-permute-start.5
  16.7 0.8 %collective-permute-start.4 = (f16[33,8,128]{2,1,0:T(8,128)(2,1)S(1)}, f16[33,8,128]{2,1,0:T(8,128)(2,1)S(1)}, u32[]{:S(2)}, u32[]{:S(2)}) collective-permute-start(f16[33,8,128]{2,1,0:T(8,128)(2,1)S(1)} %add_convert_fusion.1), channel_id=1, source_target_pairs={{0,9},{1,11},{2,8},{3,10},{4,14},{5,12},{6,15},{7,13},{8,2},{9,0},... | collective-permute-start | bytes 202760 | tf_op jit(solution)/shard_map/ppermute | solution.py:308
  17.4 0.2 shard_map.103.turned_ref
  17.6 1.8 %collective-permute-done.6 = f16[33,8,128]{2,1,0:T(8,128)(2,1)S(1)} collective-permute-done((f16[33,8,128]{2,1,0:T(8,128)(2,1)S(1)}, f16[33,8,128]{2,1,0:T(8,128)(2,1)S(1)}, u32[]{:S(2)}, u32[]{:S(2)}) %collective-permute-start.6) | collective-permute-done | bytes 67616 | tf_op jit(solution)/shard_map/ppermute | solution.py:308
  19.4 1.0 %collective-permute-done.5 = f16[33,8,128]{2,1,0:T(8,128)(2,1)S(1)} collective-permute-done((f16[33,8,128]{2,1,0:T(8,128)(2,1)S(1)}, f16[33,8,128]{2,1,0:T(8,128)(2,1)S(1)}, u32[]{:S(2)}, u32[]{:S(2)}) %collective-permute-start.5) | collective-permute-done | bytes 67616 | tf_op jit(solution)/shard_map/ppermute | solution.py:308
  20.4 0.0 collective-permute-done.4
  20.4 0.5 %collective-permute-start.7 = (f16[33,8,128]{2,1,0:T(8,128)(2,1)S(1)}, f16[33,8,128]{2,1,0:T(8,128)(2,1)S(1)}, u32[]{:S(2)}, u32[]{:S(2)}) collective-permute-start(f16[33,8,128]{2,1,0:T(8,128)(2,1)S(1)} %add_convert_fusion), channel_id=1, source_target_pairs={{0,8},{1,9},{2,10},{3,11},{4,12},{5,13},{6,14},{7,15},{8,0},{9,1},... | collective-permute-start | bytes 202760 | tf_op jit(solution)/shard_map/ppermute | solution.py:311
  21.0 0.9 %collective-permute-done.7 = f16[33,8,128]{2,1,0:T(8,128)(2,1)S(1)} collective-permute-done((f16[33,8,128]{2,1,0:T(8,128)(2,1)S(1)}, f16[33,8,128]{2,1,0:T(8,128)(2,1)S(1)}, u32[]{:S(2)}, u32[]{:S(2)}) %collective-permute-start.7) | collective-permute-done | bytes 67616 | tf_op jit(solution)/shard_map/ppermute | solution.py:311
  21.9 0.0 copy-done.1
  21.9 0.0 copy-done
  21.9 0.0 copy-done.2
  21.9 4.0 %shard_map.104 = (f32[2048,512]{1,0:T(8,128)}, f32[1,512]{1,0:T(1,128)}, f32[512,512]{1,0:T(8,128)}, f32[512,256]{1,0:T(8,128)}) custom-call(f32[33,8,128]{2,1,0:T(8,128)S(1)} %convert_element_type.50.own_ref, f32[33,8,128]{2,1,0:T(8,128)S(1)} %convert_element_type.51.other_ref, bf16[2048,128]{1,0:T(8,128)(2,1)S(1)} %shard_map.103.turned_ref, ...), custom_call_target="tpu_custom_call" | custom-call | flops 570425344 | bytes 7077888 | tf_op jit(solution)/shard_map/pallas_call | solution.py:255
  (5 shorter events, 0.1 us)
Async XLA Ops:
  0.6 21.3 %copy-start.1 = (bf16[512,256]{1,0:T(8,128)(2,1)S(1)}, bf16[512,256]{1,0:T(8,128)(2,1)}, u32[]{:S(2)}) copy-start(bf16[512,256]{1,0:T(8,128)(2,1)} %w_out_ref) | copy-start | bytes 786436
  0.6 21.3 %copy-start = (bf16[512,512]{1,0:T(8,128)(2,1)S(1)}, bf16[512,512]{1,0:T(8,128)(2,1)}, u32[]{:S(2)}) copy-start(bf16[512,512]{1,0:T(8,128)(2,1)} %w_in_ref) | copy-start | bytes 1572868
  0.7 21.3 %copy-start.2 = (f32[512]{0:T(512)S(1)}, f32[512]{0:T(512)}, u32[]{:S(2)}) copy-start(f32[512]{0:T(512)} %param.11) | copy-start | bytes 6148
  2.9 1.5 %collective-permute-start = (f32[33,8,128]{2,1,0:T(8,128)S(1)}, f32[33,8,128]{2,1,0:T(8,128)S(1)}, u32[]{:S(2)}, u32[]{:S(2)}) collective-permute-start(f32[33,8,128]{2,1,0:T(8,128)S(1)} %get-tuple-element.18), channel_id=1, source_target_pairs={{0,8},{1,9},{2,10},{3,11},{4,12},{5,13},{6,14},{7,15},{8,0},{9,1},... | collective-permute-start | bytes 405512 | tf_op jit(solution)/shard_map/ppermute | solution.py:311
  4.5 7.3 %collective-permute-start.3 = (f16[33,8,128]{2,1,0:T(8,128)(2,1)S(1)}, f16[33,8,128]{2,1,0:T(8,128)(2,1)S(1)}, u32[]{:S(2)}, u32[]{:S(2)}) collective-permute-start(f16[33,8,128]{2,1,0:T(8,128)(2,1)S(1)} %add_convert_fusion.2), channel_id=1, source_target_pairs={{0,6},{1,16},{2,19},{3,5},{4,21},{5,3},{6,0},{7,22},{8,25},{9,15},... | collective-permute-start | bytes 202760 | tf_op jit(solution)/shard_map/ppermute | solution.py:308
  9.5 4.6 %collective-permute-start.2 = (f16[33,8,128]{2,1,0:T(8,128)(2,1)S(1)}, f16[33,8,128]{2,1,0:T(8,128)(2,1)S(1)}, u32[]{:S(2)}, u32[]{:S(2)}) collective-permute-start(f16[33,8,128]{2,1,0:T(8,128)(2,1)S(1)} %add_convert_fusion.2), channel_id=1, source_target_pairs={{0,12},{1,25},{2,26},{3,15},{4,28},{5,9},{6,10},{7,31},{8,16},{9,5... | collective-permute-start | bytes 202760 | tf_op jit(solution)/shard_map/ppermute | solution.py:308
  9.5 4.6 %collective-permute-start.1 = (f16[33,8,128]{2,1,0:T(8,128)(2,1)S(1)}, f16[33,8,128]{2,1,0:T(8,128)(2,1)S(1)}, u32[]{:S(2)}, u32[]{:S(2)}) collective-permute-start(f16[33,8,128]{2,1,0:T(8,128)(2,1)S(1)} %add_convert_fusion.2), channel_id=1, source_target_pairs={{0,10},{1,8},{2,11},{3,9},{4,13},{5,15},{6,12},{7,14},{8,1},{9,3},... | collective-permute-start | bytes 202760 | tf_op jit(solution)/shard_map/ppermute | solution.py:308
  14.1 5.3 %collective-permute-start.6 = (f16[33,8,128]{2,1,0:T(8,128)(2,1)S(1)}, f16[33,8,128]{2,1,0:T(8,128)(2,1)S(1)}, u32[]{:S(2)}, u32[]{:S(2)}) collective-permute-start(f16[33,8,128]{2,1,0:T(8,128)(2,1)S(1)} %add_convert_fusion.1), channel_id=1, source_target_pairs={{0,17},{1,7},{2,4},{3,18},{4,2},{5,20},{6,23},{7,1},{8,14},{9,24},... | collective-permute-start | bytes 202760 | tf_op jit(solution)/shard_map/ppermute | solution.py:308
  16.7 3.7 %collective-permute-start.5 = (f16[33,8,128]{2,1,0:T(8,128)(2,1)S(1)}, f16[33,8,128]{2,1,0:T(8,128)(2,1)S(1)}, u32[]{:S(2)}, u32[]{:S(2)}) collective-permute-start(f16[33,8,128]{2,1,0:T(8,128)(2,1)S(1)} %add_convert_fusion.1), channel_id=1, source_target_pairs={{0,24},{1,13},{2,14},{3,27},{4,8},{5,29},{6,30},{7,11},{8,4},{9,17... | collective-permute-start | bytes 202760 | tf_op jit(solution)/shard_map/ppermute | solution.py:308
  16.7 3.7 %collective-permute-start.4 = (f16[33,8,128]{2,1,0:T(8,128)(2,1)S(1)}, f16[33,8,128]{2,1,0:T(8,128)(2,1)S(1)}, u32[]{:S(2)}, u32[]{:S(2)}) collective-permute-start(f16[33,8,128]{2,1,0:T(8,128)(2,1)S(1)} %add_convert_fusion.1), channel_id=1, source_target_pairs={{0,9},{1,11},{2,8},{3,10},{4,14},{5,12},{6,15},{7,13},{8,2},{9,0},... | collective-permute-start | bytes 202760 | tf_op jit(solution)/shard_map/ppermute | solution.py:308
  20.4 1.4 %collective-permute-start.7 = (f16[33,8,128]{2,1,0:T(8,128)(2,1)S(1)}, f16[33,8,128]{2,1,0:T(8,128)(2,1)S(1)}, u32[]{:S(2)}, u32[]{:S(2)}) collective-permute-start(f16[33,8,128]{2,1,0:T(8,128)(2,1)S(1)} %add_convert_fusion), channel_id=1, source_target_pairs={{0,8},{1,9},{2,10},{3,11},{4,12},{5,13},{6,14},{7,15},{8,0},{9,1},... | collective-permute-start | bytes 202760 | tf_op jit(solution)/shard_map/ppermute | solution.py:311

commit v8 on v7

--- a/solution.py
+++ b/solution.py
@@ -318,7 +318,7 @@
 
     mask = tile_mask.T
     send, held, masked = partial_hidden(carried, counts, mask, neighbours, peak_weight)
-    held = total([held, between_cores(send)])
+    held = total([held, between_cores(lax.optimization_barrier(send.astype(LINK)))])
     held, w_in, w_out, gain = lax.optimization_barrier((held, w_in, w_out, gain))
     gain = gain.reshape(1, -1)
     turned = turn(masked)

time: 26.1 us -> 26 us (level)
  no operation moved by 1% of the time
where the time goes in v8:
time: 26 us; the launch traced here: 25.9 us
  starting transfers between devices  9.71 us (37%)
  waiting for transfers between devices  8.81 us (34%)
  Pallas kernels  6.47 us (25%)
  between operations  0.73 us (3%)
    ppermute x6, starting transfers between devices, exchange(): return lax.ppermute(values, ALL, [(i, partner(i)) for i in range(devices)])  8.65 us
    ppermute x6, waiting for transfers between devices, exchange(): return lax.ppermute(values, ALL, [(i, partner(i)) for i in range(devices)])  7.01 us
    pallas_call x1, Pallas kernels, tower(): pl.pallas_call(functools.partial(tower_kernel, carried, length_of, pieces...  4.03 us
    pallas_call x1, Pallas kernels, partial_hidden(): pl.pallas_call(functools.partial(partial_kernel, carried, pieces), out_sh...  2.25 us
    ppermute x2, waiting for transfers between devices, between_cores(): return lax.ppermute(values, ALL, [(i, i ^ n_peak) for i in range(devices)])  1.8 us
    ppermute x2, starting transfers between devices, between_cores(): return lax.ppermute(values, ALL, [(i, i ^ n_peak) for i in range(devices)])  1.06 us
  transfers between devices with their start and end apart: 8, of which 6 were waited for; matrix products, arithmetic and copies ran while one was open for 0% of the time, Pallas kernels for 1%

profile of v8, /device:TPU:0, one launch (start us, length us, event | category | flops | bytes accessed | tf_op | source)
XLA Modules:
  0.0 25.9 jit_solution(7694041923787539437)
XLA Ops:
  0.6 0.0 copy-start.1
  0.6 0.0 copy-start
  0.7 0.0 copy-start.2
  0.7 2.3 %shard_map.102 = (f32[33,8,128]{2,1,0:T(8,128)S(1)}, f32[33,8,128]{2,1,0:T(8,128)S(1)}, bf16[128,2048]{1,0:T(8,128)(2,1)S(1)}) custom-call(bf16[128,2048]{1,0:T(8,128)(2,1)} %counts_hbm.1, s32[16,128]{1,0:T(8,128)} %bitcast.4, s32[4,15]{1,0:T(4,128)} %lists_hbm.1, bf16[2048,512]{1,0:T(8,128)(2,1)} %weight_hbm.1), custom_call_target="tpu_custom_call" | custom-call | flops 268435456 | bytes 3416064 | tf_op jit(solution)/shard_map/pallas_call | solution.py:114
  2.9 0.5 %collective-permute-start = (f16[33,8,128]{2,1,0:T(8,128)(2,1)S(1)}, f16[33,8,128]{2,1,0:T(8,128)(2,1)S(1)}, u32[]{:S(2)}, u32[]{:S(2)}) collective-permute-start(f16[33,8,128]{2,1,0:T(8,128)(2,1)S(1)} %convert_element_type.45), channel_id=1, source_target_pairs={{0,8},{1,9},{2,10},{3,11},{4,12},{5,13},{6,14},{7,15},{8,0},{9,1},... | collective-permute-start | bytes 202760 | tf_op jit(solution)/shard_map/ppermute | solution.py:311
  3.5 0.9 %collective-permute-done = f16[33,8,128]{2,1,0:T(8,128)(2,1)S(1)} collective-permute-done((f16[33,8,128]{2,1,0:T(8,128)(2,1)S(1)}, f16[33,8,128]{2,1,0:T(8,128)(2,1)S(1)}, u32[]{:S(2)}, u32[]{:S(2)}) %collective-permute-start) | collective-permute-done | bytes 67616 | tf_op jit(solution)/shard_map/ppermute | solution.py:311
  4.4 5.0 %collective-permute-start.3 = (f16[33,8,128]{2,1,0:T(8,128)(2,1)S(1)}, f16[33,8,128]{2,1,0:T(8,128)(2,1)S(1)}, u32[]{:S(2)}, u32[]{:S(2)}) collective-permute-start(f16[33,8,128]{2,1,0:T(8,128)(2,1)S(1)} %add_convert_fusion.2), channel_id=1, source_target_pairs={{0,6},{1,16},{2,19},{3,5},{4,21},{5,3},{6,0},{7,22},{8,25},{9,15},... | collective-permute-start | bytes 202760 | tf_op jit(solution)/shard_map/ppermute | solution.py:308
  9.4 0.0 collective-permute-start.2
  9.4 0.4 %collective-permute-start.1 = (f16[33,8,128]{2,1,0:T(8,128)(2,1)S(1)}, f16[33,8,128]{2,1,0:T(8,128)(2,1)S(1)}, u32[]{:S(2)}, u32[]{:S(2)}) collective-permute-start(f16[33,8,128]{2,1,0:T(8,128)(2,1)S(1)} %add_convert_fusion.2), channel_id=1, source_target_pairs={{0,10},{1,8},{2,11},{3,9},{4,13},{5,15},{6,12},{7,14},{8,1},{9,3},... | collective-permute-start | bytes 202760 | tf_op jit(solution)/shard_map/ppermute | solution.py:308
  9.8 1.9 %collective-permute-done.3 = f16[33,8,128]{2,1,0:T(8,128)(2,1)S(1)} collective-permute-done((f16[33,8,128]{2,1,0:T(8,128)(2,1)S(1)}, f16[33,8,128]{2,1,0:T(8,128)(2,1)S(1)}, u32[]{:S(2)}, u32[]{:S(2)}) %collective-permute-start.3) | collective-permute-done | bytes 67616 | tf_op jit(solution)/shard_map/ppermute | solution.py:308
  11.7 2.3 %collective-permute-done.2 = f16[33,8,128]{2,1,0:T(8,128)(2,1)S(1)} collective-permute-done((f16[33,8,128]{2,1,0:T(8,128)(2,1)S(1)}, f16[33,8,128]{2,1,0:T(8,128)(2,1)S(1)}, u32[]{:S(2)}, u32[]{:S(2)}) %collective-permute-start.2) | collective-permute-done | bytes 67616 | tf_op jit(solution)/shard_map/ppermute | solution.py:308
  14.0 0.0 collective-permute-done.1
  14.1 2.5 %collective-permute-start.6 = (f16[33,8,128]{2,1,0:T(8,128)(2,1)S(1)}, f16[33,8,128]{2,1,0:T(8,128)(2,1)S(1)}, u32[]{:S(2)}, u32[]{:S(2)}) collective-permute-start(f16[33,8,128]{2,1,0:T(8,128)(2,1)S(1)} %add_convert_fusion.1), channel_id=1, source_target_pairs={{0,17},{1,7},{2,4},{3,18},{4,2},{5,20},{6,23},{7,1},{8,14},{9,24},... | collective-permute-start | bytes 202760 | tf_op jit(solution)/shard_map/ppermute | solution.py:308
  16.6 0.0 collective-permute-start.5
  16.6 0.8 %collective-permute-start.4 = (f16[33,8,128]{2,1,0:T(8,128)(2,1)S(1)}, f16[33,8,128]{2,1,0:T(8,128)(2,1)S(1)}, u32[]{:S(2)}, u32[]{:S(2)}) collective-permute-start(f16[33,8,128]{2,1,0:T(8,128)(2,1)S(1)} %add_convert_fusion.1), channel_id=1, source_target_pairs={{0,9},{1,11},{2,8},{3,10},{4,14},{5,12},{6,15},{7,13},{8,2},{9,0},... | collective-permute-start | bytes 202760 | tf_op jit(solution)/shard_map/ppermute | solution.py:308
  17.4 0.2 shard_map.103.turned_ref
  17.5 1.8 %collective-permute-done.6 = f16[33,8,128]{2,1,0:T(8,128)(2,1)S(1)} collective-permute-done((f16[33,8,128]{2,1,0:T(8,128)(2,1)S(1)}, f16[33,8,128]{2,1,0:T(8,128)(2,1)S(1)}, u32[]{:S(2)}, u32[]{:S(2)}) %collective-permute-start.6) | collective-permute-done | bytes 67616 | tf_op jit(solution)/shard_map/ppermute | solution.py:308
  19.3 1.0 %collective-permute-done.5 = f16[33,8,128]{2,1,0:T(8,128)(2,1)S(1)} collective-permute-done((f16[33,8,128]{2,1,0:T(8,128)(2,1)S(1)}, f16[33,8,128]{2,1,0:T(8,128)(2,1)S(1)}, u32[]{:S(2)}, u32[]{:S(2)}) %collective-permute-start.5) | collective-permute-done | bytes 67616 | tf_op jit(solution)/shard_map/ppermute | solution.py:308
  20.3 0.0 collective-permute-done.4
  20.4 0.5 %collective-permute-start.7 = (f16[33,8,128]{2,1,0:T(8,128)(2,1)S(1)}, f16[33,8,128]{2,1,0:T(8,128)(2,1)S(1)}, u32[]{:S(2)}, u32[]{:S(2)}) collective-permute-start(f16[33,8,128]{2,1,0:T(8,128)(2,1)S(1)} %add_convert_fusion), channel_id=1, source_target_pairs={{0,8},{1,9},{2,10},{3,11},{4,12},{5,13},{6,14},{7,15},{8,0},{9,1},... | collective-permute-start | bytes 202760 | tf_op jit(solution)/shard_map/ppermute | solution.py:311
  20.9 0.9 %collective-permute-done.7 = f16[33,8,128]{2,1,0:T(8,128)(2,1)S(1)} collective-permute-done((f16[33,8,128]{2,1,0:T(8,128)(2,1)S(1)}, f16[33,8,128]{2,1,0:T(8,128)(2,1)S(1)}, u32[]{:S(2)}, u32[]{:S(2)}) %collective-permute-start.7) | collective-permute-done | bytes 67616 | tf_op jit(solution)/shard_map/ppermute | solution.py:311
  21.8 0.0 copy-done.1
  21.8 0.0 copy-done
  21.8 0.0 copy-done.2
  21.8 4.0 %shard_map.104 = (f32[2048,512]{1,0:T(8,128)}, f32[1,512]{1,0:T(1,128)}, f32[512,512]{1,0:T(8,128)}, f32[512,256]{1,0:T(8,128)}) custom-call(f32[33,8,128]{2,1,0:T(8,128)S(1)} %convert_element_type.58.own_ref, f32[33,8,128]{2,1,0:T(8,128)S(1)} %convert_element_type.59.other_ref, bf16[2048,128]{1,0:T(8,128)(2,1)S(1)} %shard_map.103.turned_ref, ...), custom_call_target="tpu_custom_call" | custom-call | flops 570425344 | bytes 7077888 | tf_op jit(solution)/shard_map/pallas_call | solution.py:255
  (6 shorter events, 0.2 us)
Async XLA Ops:
  0.6 21.2 %copy-start.1 = (bf16[512,256]{1,0:T(8,128)(2,1)S(1)}, bf16[512,256]{1,0:T(8,128)(2,1)}, u32[]{:S(2)}) copy-start(bf16[512,256]{1,0:T(8,128)(2,1)} %w_out_ref) | copy-start | bytes 786436
  0.6 21.2 %copy-start = (bf16[512,512]{1,0:T(8,128)(2,1)S(1)}, bf16[512,512]{1,0:T(8,128)(2,1)}, u32[]{:S(2)}) copy-start(bf16[512,512]{1,0:T(8,128)(2,1)} %w_in_ref) | copy-start | bytes 1572868
  0.7 21.2 %copy-start.2 = (f32[512]{0:T(512)S(1)}, f32[512]{0:T(512)}, u32[]{:S(2)}) copy-start(f32[512]{0:T(512)} %param.11) | copy-start | bytes 6148
  2.9 1.4 %collective-permute-start = (f16[33,8,128]{2,1,0:T(8,128)(2,1)S(1)}, f16[33,8,128]{2,1,0:T(8,128)(2,1)S(1)}, u32[]{:S(2)}, u32[]{:S(2)}) collective-permute-start(f16[33,8,128]{2,1,0:T(8,128)(2,1)S(1)} %convert_element_type.45), channel_id=1, source_target_pairs={{0,8},{1,9},{2,10},{3,11},{4,12},{5,13},{6,14},{7,15},{8,0},{9,1},... | collective-permute-start | bytes 202760 | tf_op jit(solution)/shard_map/ppermute | solution.py:311
  4.4 7.3 %collective-permute-start.3 = (f16[33,8,128]{2,1,0:T(8,128)(2,1)S(1)}, f16[33,8,128]{2,1,0:T(8,128)(2,1)S(1)}, u32[]{:S(2)}, u32[]{:S(2)}) collective-permute-start(f16[33,8,128]{2,1,0:T(8,128)(2,1)S(1)} %add_convert_fusion.2), channel_id=1, source_target_pairs={{0,6},{1,16},{2,19},{3,5},{4,21},{5,3},{6,0},{7,22},{8,25},{9,15},... | collective-permute-start | bytes 202760 | tf_op jit(solution)/shard_map/ppermute | solution.py:308
  9.4 4.6 %collective-permute-start.2 = (f16[33,8,128]{2,1,0:T(8,128)(2,1)S(1)}, f16[33,8,128]{2,1,0:T(8,128)(2,1)S(1)}, u32[]{:S(2)}, u32[]{:S(2)}) collective-permute-start(f16[33,8,128]{2,1,0:T(8,128)(2,1)S(1)} %add_convert_fusion.2), channel_id=1, source_target_pairs={{0,12},{1,25},{2,26},{3,15},{4,28},{5,9},{6,10},{7,31},{8,16},{9,5... | collective-permute-start | bytes 202760 | tf_op jit(solution)/shard_map/ppermute | solution.py:308
  9.4 4.6 %collective-permute-start.1 = (f16[33,8,128]{2,1,0:T(8,128)(2,1)S(1)}, f16[33,8,128]{2,1,0:T(8,128)(2,1)S(1)}, u32[]{:S(2)}, u32[]{:S(2)}) collective-permute-start(f16[33,8,128]{2,1,0:T(8,128)(2,1)S(1)} %add_convert_fusion.2), channel_id=1, source_target_pairs={{0,10},{1,8},{2,11},{3,9},{4,13},{5,15},{6,12},{7,14},{8,1},{9,3},... | collective-permute-start | bytes 202760 | tf_op jit(solution)/shard_map/ppermute | solution.py:308
  14.1 5.3 %collective-permute-start.6 = (f16[33,8,128]{2,1,0:T(8,128)(2,1)S(1)}, f16[33,8,128]{2,1,0:T(8,128)(2,1)S(1)}, u32[]{:S(2)}, u32[]{:S(2)}) collective-permute-start(f16[33,8,128]{2,1,0:T(8,128)(2,1)S(1)} %add_convert_fusion.1), channel_id=1, source_target_pairs={{0,17},{1,7},{2,4},{3,18},{4,2},{5,20},{6,23},{7,1},{8,14},{9,24},... | collective-permute-start | bytes 202760 | tf_op jit(solution)/shard_map/ppermute | solution.py:308
  16.6 3.7 %collective-permute-start.5 = (f16[33,8,128]{2,1,0:T(8,128)(2,1)S(1)}, f16[33,8,128]{2,1,0:T(8,128)(2,1)S(1)}, u32[]{:S(2)}, u32[]{:S(2)}) collective-permute-start(f16[33,8,128]{2,1,0:T(8,128)(2,1)S(1)} %add_convert_fusion.1), channel_id=1, source_target_pairs={{0,24},{1,13},{2,14},{3,27},{4,8},{5,29},{6,30},{7,11},{8,4},{9,17... | collective-permute-start | bytes 202760 | tf_op jit(solution)/shard_map/ppermute | solution.py:308
  16.6 3.7 %collective-permute-start.4 = (f16[33,8,128]{2,1,0:T(8,128)(2,1)S(1)}, f16[33,8,128]{2,1,0:T(8,128)(2,1)S(1)}, u32[]{:S(2)}, u32[]{:S(2)}) collective-permute-start(f16[33,8,128]{2,1,0:T(8,128)(2,1)S(1)} %add_convert_fusion.1), channel_id=1, source_target_pairs={{0,9},{1,11},{2,8},{3,10},{4,14},{5,12},{6,15},{7,13},{8,2},{9,0},... | collective-permute-start | bytes 202760 | tf_op jit(solution)/shard_map/ppermute | solution.py:308
  20.4 1.4 %collective-permute-start.7 = (f16[33,8,128]{2,1,0:T(8,128)(2,1)S(1)}, f16[33,8,128]{2,1,0:T(8,128)(2,1)S(1)}, u32[]{:S(2)}, u32[]{:S(2)}) collective-permute-start(f16[33,8,128]{2,1,0:T(8,128)(2,1)S(1)} %add_convert_fusion), channel_id=1, source_target_pairs={{0,8},{1,9},{2,10},{3,11},{4,12},{5,13},{6,14},{7,15},{8,0},{9,1},... | collective-permute-start | bytes 202760 | tf_op jit(solution)/shard_map/ppermute | solution.py:311

commit v9 on v8

--- a/solution.py
+++ b/solution.py
@@ -200,7 +200,7 @@
     unit = project * length
     codes = unit.astype(BF16)
 
-    scores = dot(codes, codes, 1, 1) / sharpness_divisor
+    scores = dot(codes, codes, 1, 1) * (1.0 / sharpness_divisor)
     targets = lax.broadcasted_iota(jnp.int32, (cells, cells), 0)
     sources = lax.broadcasted_iota(jnp.int32, (cells, cells), 1)
     expo = jnp.where(targets == sources, 0.0, jnp.exp(scores))
@@ -209,8 +209,8 @@
     tallies = jnp.zeros((cells, cells), F32)
     for slot in range(length_of):
         tallies = tallies + (lists[slot : slot + 1] == places).astype(F32)
-    coupling = (prob - tallies / length_of).astype(BF16)
-    dcodes = (dot(coupling, codes, 0, 0) + dot(coupling, codes, 1, 0)) / sharpness_divisor
+    coupling = (prob - tallies * (1.0 / length_of)).astype(BF16)
+    dcodes = (dot(coupling, codes, 0, 0) + dot(coupling, codes, 1, 0)) * (1.0 / sharpness_divisor)
 
     dproj = (length * (dcodes - unit * jnp.sum(unit * dcodes, axis=1, keepdims=True))).astype(BF16)
     dpre = (dot(dproj, w_out, 1, 1) * slope).astype(BF16)

time: 26 us -> 26 us (level)
  no operation moved by 1% of the time
where the time goes in v9:
time: 26 us; the launch traced here: 25.9 us
  starting transfers between devices  9.71 us (37%)
  waiting for transfers between devices  8.81 us (34%)
  Pallas kernels  6.47 us (25%)
  between operations  0.73 us (3%)
    ppermute x6, starting transfers between devices, exchange(): return lax.ppermute(values, ALL, [(i, partner(i)) for i in range(devices)])  8.65 us
    ppermute x6, waiting for transfers between devices, exchange(): return lax.ppermute(values, ALL, [(i, partner(i)) for i in range(devices)])  7.01 us
    pallas_call x1, Pallas kernels, tower(): pl.pallas_call(functools.partial(tower_kernel, carried, length_of, pieces...  4.03 us
    pallas_call x1, Pallas kernels, partial_hidden(): pl.pallas_call(functools.partial(partial_kernel, carried, pieces), out_sh...  2.25 us
    ppermute x2, waiting for transfers between devices, between_cores(): return lax.ppermute(values, ALL, [(i, i ^ n_peak) for i in range(devices)])  1.8 us
    ppermute x2, starting transfers between devices, between_cores(): return lax.ppermute(values, ALL, [(i, i ^ n_peak) for i in range(devices)])  1.06 us
  transfers between devices with their start and end apart: 8, of which 6 were waited for; matrix products, arithmetic and copies ran while one was open for 0% of the time, Pallas kernels for 1%

profile of v9, /device:TPU:0, one launch (start us, length us, event | category | flops | bytes accessed | tf_op | source)
XLA Modules:
  0.0 25.9 jit_solution(7694041923787539437)
XLA Ops:
  0.6 0.0 copy-start.1
  0.6 0.0 copy-start
  0.7 0.0 copy-start.2
  0.7 2.3 %shard_map.102 = (f32[33,8,128]{2,1,0:T(8,128)S(1)}, f32[33,8,128]{2,1,0:T(8,128)S(1)}, bf16[128,2048]{1,0:T(8,128)(2,1)S(1)}) custom-call(bf16[128,2048]{1,0:T(8,128)(2,1)} %counts_hbm.1, s32[16,128]{1,0:T(8,128)} %bitcast.4, s32[4,15]{1,0:T(4,128)} %lists_hbm.1, bf16[2048,512]{1,0:T(8,128)(2,1)} %weight_hbm.1), custom_call_target="tpu_custom_call" | custom-call | flops 268435456 | bytes 3416064 | tf_op jit(solution)/shard_map/pallas_call | solution.py:114
  2.9 0.5 %collective-permute-start = (f16[33,8,128]{2,1,0:T(8,128)(2,1)S(1)}, f16[33,8,128]{2,1,0:T(8,128)(2,1)S(1)}, u32[]{:S(2)}, u32[]{:S(2)}) collective-permute-start(f16[33,8,128]{2,1,0:T(8,128)(2,1)S(1)} %convert_element_type.45), channel_id=1, source_target_pairs={{0,8},{1,9},{2,10},{3,11},{4,12},{5,13},{6,14},{7,15},{8,0},{9,1},... | collective-permute-start | bytes 202760 | tf_op jit(solution)/shard_map/ppermute | solution.py:311
  3.5 0.9 %collective-permute-done = f16[33,8,128]{2,1,0:T(8,128)(2,1)S(1)} collective-permute-done((f16[33,8,128]{2,1,0:T(8,128)(2,1)S(1)}, f16[33,8,128]{2,1,0:T(8,128)(2,1)S(1)}, u32[]{:S(2)}, u32[]{:S(2)}) %collective-permute-start) | collective-permute-done | bytes 67616 | tf_op jit(solution)/shard_map/ppermute | solution.py:311
  4.4 5.0 %collective-permute-start.3 = (f16[33,8,128]{2,1,0:T(8,128)(2,1)S(1)}, f16[33,8,128]{2,1,0:T(8,128)(2,1)S(1)}, u32[]{:S(2)}, u32[]{:S(2)}) collective-permute-start(f16[33,8,128]{2,1,0:T(8,128)(2,1)S(1)} %add_convert_fusion.2), channel_id=1, source_target_pairs={{0,6},{1,16},{2,19},{3,5},{4,21},{5,3},{6,0},{7,22},{8,25},{9,15},... | collective-permute-start | bytes 202760 | tf_op jit(solution)/shard_map/ppermute | solution.py:308
  9.4 0.0 collective-permute-start.2
  9.4 0.4 %collective-permute-start.1 = (f16[33,8,128]{2,1,0:T(8,128)(2,1)S(1)}, f16[33,8,128]{2,1,0:T(8,128)(2,1)S(1)}, u32[]{:S(2)}, u32[]{:S(2)}) collective-permute-start(f16[33,8,128]{2,1,0:T(8,128)(2,1)S(1)} %add_convert_fusion.2), channel_id=1, source_target_pairs={{0,10},{1,8},{2,11},{3,9},{4,13},{5,15},{6,12},{7,14},{8,1},{9,3},... | collective-permute-start | bytes 202760 | tf_op jit(solution)/shard_map/ppermute | solution.py:308
  9.8 1.9 %collective-permute-done.3 = f16[33,8,128]{2,1,0:T(8,128)(2,1)S(1)} collective-permute-done((f16[33,8,128]{2,1,0:T(8,128)(2,1)S(1)}, f16[33,8,128]{2,1,0:T(8,128)(2,1)S(1)}, u32[]{:S(2)}, u32[]{:S(2)}) %collective-permute-start.3) | collective-permute-done | bytes 67616 | tf_op jit(solution)/shard_map/ppermute | solution.py:308
  11.7 2.3 %collective-permute-done.2 = f16[33,8,128]{2,1,0:T(8,128)(2,1)S(1)} collective-permute-done((f16[33,8,128]{2,1,0:T(8,128)(2,1)S(1)}, f16[33,8,128]{2,1,0:T(8,128)(2,1)S(1)}, u32[]{:S(2)}, u32[]{:S(2)}) %collective-permute-start.2) | collective-permute-done | bytes 67616 | tf_op jit(solution)/shard_map/ppermute | solution.py:308
  14.0 0.0 collective-permute-done.1
  14.1 2.5 %collective-permute-start.6 = (f16[33,8,128]{2,1,0:T(8,128)(2,1)S(1)}, f16[33,8,128]{2,1,0:T(8,128)(2,1)S(1)}, u32[]{:S(2)}, u32[]{:S(2)}) collective-permute-start(f16[33,8,128]{2,1,0:T(8,128)(2,1)S(1)} %add_convert_fusion.1), channel_id=1, source_target_pairs={{0,17},{1,7},{2,4},{3,18},{4,2},{5,20},{6,23},{7,1},{8,14},{9,24},... | collective-permute-start | bytes 202760 | tf_op jit(solution)/shard_map/ppermute | solution.py:308
  16.6 0.0 collective-permute-start.5
  16.6 0.8 %collective-permute-start.4 = (f16[33,8,128]{2,1,0:T(8,128)(2,1)S(1)}, f16[33,8,128]{2,1,0:T(8,128)(2,1)S(1)}, u32[]{:S(2)}, u32[]{:S(2)}) collective-permute-start(f16[33,8,128]{2,1,0:T(8,128)(2,1)S(1)} %add_convert_fusion.1), channel_id=1, source_target_pairs={{0,9},{1,11},{2,8},{3,10},{4,14},{5,12},{6,15},{7,13},{8,2},{9,0},... | collective-permute-start | bytes 202760 | tf_op jit(solution)/shard_map/ppermute | solution.py:308
  17.4 0.2 shard_map.103.turned_ref
  17.5 1.8 %collective-permute-done.6 = f16[33,8,128]{2,1,0:T(8,128)(2,1)S(1)} collective-permute-done((f16[33,8,128]{2,1,0:T(8,128)(2,1)S(1)}, f16[33,8,128]{2,1,0:T(8,128)(2,1)S(1)}, u32[]{:S(2)}, u32[]{:S(2)}) %collective-permute-start.6) | collective-permute-done | bytes 67616 | tf_op jit(solution)/shard_map/ppermute | solution.py:308
  19.3 1.0 %collective-permute-done.5 = f16[33,8,128]{2,1,0:T(8,128)(2,1)S(1)} collective-permute-done((f16[33,8,128]{2,1,0:T(8,128)(2,1)S(1)}, f16[33,8,128]{2,1,0:T(8,128)(2,1)S(1)}, u32[]{:S(2)}, u32[]{:S(2)}) %collective-permute-start.5) | collective-permute-done | bytes 67616 | tf_op jit(solution)/shard_map/ppermute | solution.py:308
  20.3 0.0 collective-permute-done.4
  20.4 0.5 %collective-permute-start.7 = (f16[33,8,128]{2,1,0:T(8,128)(2,1)S(1)}, f16[33,8,128]{2,1,0:T(8,128)(2,1)S(1)}, u32[]{:S(2)}, u32[]{:S(2)}) collective-permute-start(f16[33,8,128]{2,1,0:T(8,128)(2,1)S(1)} %add_convert_fusion), channel_id=1, source_target_pairs={{0,8},{1,9},{2,10},{3,11},{4,12},{5,13},{6,14},{7,15},{8,0},{9,1},... | collective-permute-start | bytes 202760 | tf_op jit(solution)/shard_map/ppermute | solution.py:311
  20.9 0.9 %collective-permute-done.7 = f16[33,8,128]{2,1,0:T(8,128)(2,1)S(1)} collective-permute-done((f16[33,8,128]{2,1,0:T(8,128)(2,1)S(1)}, f16[33,8,128]{2,1,0:T(8,128)(2,1)S(1)}, u32[]{:S(2)}, u32[]{:S(2)}) %collective-permute-start.7) | collective-permute-done | bytes 67616 | tf_op jit(solution)/shard_map/ppermute | solution.py:311
  21.8 0.0 copy-done.1
  21.8 0.0 copy-done
  21.8 0.0 copy-done.2
  21.8 4.0 %shard_map.104 = (f32[2048,512]{1,0:T(8,128)}, f32[1,512]{1,0:T(1,128)}, f32[512,512]{1,0:T(8,128)}, f32[512,256]{1,0:T(8,128)}) custom-call(f32[33,8,128]{2,1,0:T(8,128)S(1)} %convert_element_type.58.own_ref, f32[33,8,128]{2,1,0:T(8,128)S(1)} %convert_element_type.59.other_ref, bf16[2048,128]{1,0:T(8,128)(2,1)S(1)} %shard_map.103.turned_ref, ...), custom_call_target="tpu_custom_call" | custom-call | flops 570425344 | bytes 7077888 | tf_op jit(solution)/shard_map/pallas_call | solution.py:255
  (6 shorter events, 0.2 us)
Async XLA Ops:
  0.6 21.2 %copy-start.1 = (bf16[512,256]{1,0:T(8,128)(2,1)S(1)}, bf16[512,256]{1,0:T(8,128)(2,1)}, u32[]{:S(2)}) copy-start(bf16[512,256]{1,0:T(8,128)(2,1)} %w_out_ref) | copy-start | bytes 786436
  0.6 21.2 %copy-start = (bf16[512,512]{1,0:T(8,128)(2,1)S(1)}, bf16[512,512]{1,0:T(8,128)(2,1)}, u32[]{:S(2)}) copy-start(bf16[512,512]{1,0:T(8,128)(2,1)} %w_in_ref) | copy-start | bytes 1572868
  0.7 21.2 %copy-start.2 = (f32[512]{0:T(512)S(1)}, f32[512]{0:T(512)}, u32[]{:S(2)}) copy-start(f32[512]{0:T(512)} %param.11) | copy-start | bytes 6148
  2.9 1.4 %collective-permute-start = (f16[33,8,128]{2,1,0:T(8,128)(2,1)S(1)}, f16[33,8,128]{2,1,0:T(8,128)(2,1)S(1)}, u32[]{:S(2)}, u32[]{:S(2)}) collective-permute-start(f16[33,8,128]{2,1,0:T(8,128)(2,1)S(1)} %convert_element_type.45), channel_id=1, source_target_pairs={{0,8},{1,9},{2,10},{3,11},{4,12},{5,13},{6,14},{7,15},{8,0},{9,1},... | collective-permute-start | bytes 202760 | tf_op jit(solution)/shard_map/ppermute | solution.py:311
  4.4 7.3 %collective-permute-start.3 = (f16[33,8,128]{2,1,0:T(8,128)(2,1)S(1)}, f16[33,8,128]{2,1,0:T(8,128)(2,1)S(1)}, u32[]{:S(2)}, u32[]{:S(2)}) collective-permute-start(f16[33,8,128]{2,1,0:T(8,128)(2,1)S(1)} %add_convert_fusion.2), channel_id=1, source_target_pairs={{0,6},{1,16},{2,19},{3,5},{4,21},{5,3},{6,0},{7,22},{8,25},{9,15},... | collective-permute-start | bytes 202760 | tf_op jit(solution)/shard_map/ppermute | solution.py:308
  9.4 4.6 %collective-permute-start.2 = (f16[33,8,128]{2,1,0:T(8,128)(2,1)S(1)}, f16[33,8,128]{2,1,0:T(8,128)(2,1)S(1)}, u32[]{:S(2)}, u32[]{:S(2)}) collective-permute-start(f16[33,8,128]{2,1,0:T(8,128)(2,1)S(1)} %add_convert_fusion.2), channel_id=1, source_target_pairs={{0,12},{1,25},{2,26},{3,15},{4,28},{5,9},{6,10},{7,31},{8,16},{9,5... | collective-permute-start | bytes 202760 | tf_op jit(solution)/shard_map/ppermute | solution.py:308
  9.4 4.6 %collective-permute-start.1 = (f16[33,8,128]{2,1,0:T(8,128)(2,1)S(1)}, f16[33,8,128]{2,1,0:T(8,128)(2,1)S(1)}, u32[]{:S(2)}, u32[]{:S(2)}) collective-permute-start(f16[33,8,128]{2,1,0:T(8,128)(2,1)S(1)} %add_convert_fusion.2), channel_id=1, source_target_pairs={{0,10},{1,8},{2,11},{3,9},{4,13},{5,15},{6,12},{7,14},{8,1},{9,3},... | collective-permute-start | bytes 202760 | tf_op jit(solution)/shard_map/ppermute | solution.py:308
  14.1 5.3 %collective-permute-start.6 = (f16[33,8,128]{2,1,0:T(8,128)(2,1)S(1)}, f16[33,8,128]{2,1,0:T(8,128)(2,1)S(1)}, u32[]{:S(2)}, u32[]{:S(2)}) collective-permute-start(f16[33,8,128]{2,1,0:T(8,128)(2,1)S(1)} %add_convert_fusion.1), channel_id=1, source_target_pairs={{0,17},{1,7},{2,4},{3,18},{4,2},{5,20},{6,23},{7,1},{8,14},{9,24},... | collective-permute-start | bytes 202760 | tf_op jit(solution)/shard_map/ppermute | solution.py:308
  16.6 3.7 %collective-permute-start.5 = (f16[33,8,128]{2,1,0:T(8,128)(2,1)S(1)}, f16[33,8,128]{2,1,0:T(8,128)(2,1)S(1)}, u32[]{:S(2)}, u32[]{:S(2)}) collective-permute-start(f16[33,8,128]{2,1,0:T(8,128)(2,1)S(1)} %add_convert_fusion.1), channel_id=1, source_target_pairs={{0,24},{1,13},{2,14},{3,27},{4,8},{5,29},{6,30},{7,11},{8,4},{9,17... | collective-permute-start | bytes 202760 | tf_op jit(solution)/shard_map/ppermute | solution.py:308
  16.6 3.7 %collective-permute-start.4 = (f16[33,8,128]{2,1,0:T(8,128)(2,1)S(1)}, f16[33,8,128]{2,1,0:T(8,128)(2,1)S(1)}, u32[]{:S(2)}, u32[]{:S(2)}) collective-permute-start(f16[33,8,128]{2,1,0:T(8,128)(2,1)S(1)} %add_convert_fusion.1), channel_id=1, source_target_pairs={{0,9},{1,11},{2,8},{3,10},{4,14},{5,12},{6,15},{7,13},{8,2},{9,0},... | collective-permute-start | bytes 202760 | tf_op jit(solution)/shard_map/ppermute | solution.py:308
  20.4 1.4 %collective-permute-start.7 = (f16[33,8,128]{2,1,0:T(8,128)(2,1)S(1)}, f16[33,8,128]{2,1,0:T(8,128)(2,1)S(1)}, u32[]{:S(2)}, u32[]{:S(2)}) collective-permute-start(f16[33,8,128]{2,1,0:T(8,128)(2,1)S(1)} %add_convert_fusion), channel_id=1, source_target_pairs={{0,8},{1,9},{2,10},{3,11},{4,12},{5,13},{6,14},{7,15},{8,0},{9,1},... | collective-permute-start | bytes 202760 | tf_op jit(solution)/shard_map/ppermute | solution.py:311
